TPU v7x, 32 devices: a whole 2x2x4 slice. The times are simulated.
32 devices in a mesh: dp: 2 (over x), zero: 4 (over z), seq: 4 (over y, core).
Axes of the slice: x: 2, y: 2, z: 4, core: 2. Of those that a mesh axis runs over, the one named last changes fastest.
Arguments:
- inputs: bfloat16 [8, 1024, 2048], P(('dp', 'zero'), 'seq'), may hold values from -8 to 8
- out_grad: bfloat16 [8, 1024, 2048], P(('dp', 'zero'), 'seq'), may hold values from -6 to 6
- vectors: float32 [26624], P(('zero', 'seq')), may hold values from -1 to 1.5
- qkv_weight: float32 [2048, 6144], P(('zero', 'seq')), may hold values from -1 to 1
- dense_weight: float32 [2048, 2048], P(('zero', 'seq')), may hold values from -1.5 to 1.5
- up_weight: float32 [2048, 8192], P(('zero', 'seq')), may hold values from -0.125 to 0.125
- down_weight: float32 [8192, 2048], P(None, ('zero', 'seq')), may hold values from -1 to 1
- vectors_first: float32 [26624], P(('zero', 'seq')), may hold values from -28 to 28
- qkv_first: float32 [2048, 6144], P(('zero', 'seq')), may hold values from -40 to 40
- dense_first: float32 [2048, 2048], P(('zero', 'seq')), may hold values from -6 to 6
- up_first: float32 [2048, 8192], P(('zero', 'seq')), may hold values from -28 to 28
- down_first: float32 [8192, 2048], P(None, ('zero', 'seq')), may hold values from -28 to 28
- vectors_second: float32 [26624], P(('zero', 'seq')), may hold values from 163.84 to 983.04
- qkv_second: float32 [2048, 6144], P(('zero', 'seq')), may hold values from 409.6 to 1638.4
- dense_second: float32 [2048, 2048], P(('zero', 'seq')), may hold values from 3.2 to 16
- up_second: float32 [2048, 8192], P(('zero', 'seq')), may hold values from 163.84 to 819.2
- down_second: float32 [8192, 2048], P(None, ('zero', 'seq')), may hold values from 163.84 to 655.36
Outputs:
- outputs: bfloat16 [8, 1024, 2048], P(('dp', 'zero'), 'seq')
- input_grad: bfloat16 [8, 1024, 2048], P(('dp', 'zero'), 'seq')
- vectors_grad: float32 [26624], P(('zero', 'seq'))
- qkv_grad: float32 [2048, 6144], P(('zero', 'seq'))
- dense_grad: float32 [2048, 2048], P(('zero', 'seq'))
- up_grad: float32 [2048, 8192], P(('zero', 'seq'))
- down_grad: float32 [8192, 2048], P(None, ('zero', 'seq'))
- vectors_new: float32 [26624], P(('zero', 'seq'))
- qkv_new: float32 [2048, 6144], P(('zero', 'seq'))
- dense_new: float32 [2048, 2048], P(('zero', 'seq'))
- up_new: float32 [2048, 8192], P(('zero', 'seq'))
- down_new: float32 [8192, 2048], P(None, ('zero', 'seq'))
- vectors_first_new: float32 [26624], P(('zero', 'seq'))
- qkv_first_new: float32 [2048, 6144], P(('zero', 'seq'))
- dense_first_new: float32 [2048, 2048], P(('zero', 'seq'))
- up_first_new: float32 [2048, 8192], P(('zero', 'seq'))
- down_first_new: float32 [8192, 2048], P(None, ('zero', 'seq'))
- vectors_second_new: float32 [26624], P(('zero', 'seq'))
- qkv_second_new: float32 [2048, 6144], P(('zero', 'seq'))
- dense_second_new: float32 [2048, 2048], P(('zero', 'seq'))
- up_second_new: float32 [2048, 8192], P(('zero', 'seq'))
- down_second_new: float32 [8192, 2048], P(None, ('zero', 'seq'))
All inputs are finite; a program needn't handle non-finite values.
Results may differ from a plain program's by a relative error of at most 0.012.
Values may be sent and summed in bfloat16 or wider, within the bound.
A program may use at most 896 MiB of HBM per device.

v0:
```python
import math

import jax
import jax.numpy as jnp
from jax import lax
from jax.sharding import PartitionSpec as P

D = 2048
HEADS = 8
HEAD_DIM = 256
FF = 8192
ROT = 64
ADAM_STEP = 4


BETA_ONE = 0.9
BETA_TWO = 0.95
LEARN_RATE = 0.5
EPSILON = 1e-08
WEIGHT_DECAY = 0.1
NORM_EPSILON = 1e-05
MASKED = -1e30
CONTRACT_LAST = (((1,), (1,)), ((), ()))
CONTRACT_ROWS = (((0,), (0,)), ((), ()))


def layer_norm(values, gain_vec, bias_vec):
    average = jnp.mean(values, axis=-1, keepdims=True)
    centred = values - average
    spread = jnp.mean(centred * centred, axis=-1, keepdims=True)
    return centred * lax.rsqrt(spread + NORM_EPSILON) * gain_vec + bias_vec


def gelu_exact(values):
    return 0.5 * values * (1.0 + lax.erf(values * (1.0 / math.sqrt(2.0))))


def split_vectors(wide_vec):
    return (
        wide_vec[0:D],
        wide_vec[D : 2 * D],
        wide_vec[2 * D : 5 * D],
        wide_vec[5 * D : 6 * D],
        wide_vec[6 * D : 7 * D],
        wide_vec[7 * D : 8 * D],
        wide_vec[8 * D : 8 * D + FF],
        wide_vec[8 * D + FF : 9 * D + FF],
    )


def rotary_tables(positions):
    half_rot = ROT // 2
    exponent = jnp.arange(half_rot, dtype=jnp.float32) * (2.0 / ROT)
    inverse = jnp.power(10000.0, -exponent)
    angles = positions[:, None] * inverse[None, :]
    angles = jnp.concatenate([angles, angles], axis=1)
    return (jnp.cos(angles), jnp.sin(angles))


def apply_rotary(head_values, cosine, sine_table):
    half_rot = ROT // 2
    rot_part = head_values[..., :ROT]
    turned = jnp.concatenate([-rot_part[..., half_rot:], rot_part[..., :half_rot]], axis=-1)
    mixed_part = rot_part * cosine[:, None, :] + turned * sine_table[:, None, :]
    return jnp.concatenate([mixed_part, head_values[..., ROT:]], axis=-1)


def rotary_back(grad_heads, cosine, sine_table):
    half_rot = ROT // 2
    rot_part = grad_heads[..., :ROT]
    scaled = rot_part * sine_table[:, None, :]
    turned = jnp.concatenate([scaled[..., half_rot:], -scaled[..., :half_rot]], axis=-1)
    mixed_part = rot_part * cosine[:, None, :] + turned
    return jnp.concatenate([mixed_part, grad_heads[..., ROT:]], axis=-1)


def adam_step(parameter, gradient, first_moment, second, decay_rate):
    first_new = BETA_ONE * first_moment + (1.0 - BETA_ONE) * gradient
    second_new = BETA_TWO * second + (1.0 - BETA_TWO) * gradient * gradient
    first_hat = first_new / (1.0 - BETA_ONE**ADAM_STEP)
    second_hat = second_new / (1.0 - BETA_TWO**ADAM_STEP)
    param_new = parameter - LEARN_RATE * (
        first_hat / (jnp.sqrt(second_hat) + EPSILON) + decay_rate * parameter
    )
    return (param_new, first_new, second_new)


def body(
    inputs,
    out_grad,
    vectors,
    qkv_weight,
    dense_weight,
    up_weight,
    down_weight,
    vectors_first,
    qkv_first,
    dense_first,
    up_first,
    down_first,
    vectors_second,
    qkv_second,
    dense_second,
    up_second,
    down_second,
):
    full_vec, full_qkv, full_dense, full_up, full_down_t = (
        lax.all_gather(vectors.astype(jnp.bfloat16), ("zero", "seq"), axis=0, tiled=True),
        lax.all_gather(qkv_weight.astype(jnp.bfloat16), ("zero", "seq"), axis=0, tiled=True),
        lax.all_gather(dense_weight.astype(jnp.bfloat16), ("zero", "seq"), axis=0, tiled=True),
        lax.all_gather(up_weight.astype(jnp.bfloat16), ("zero", "seq"), axis=0, tiled=True),
        lax.all_gather(down_weight.T.astype(jnp.bfloat16), ("zero", "seq"), axis=0, tiled=True),
    )
    ln1_gain, ln1_bias, qkv_bias, dense_bias, ln2_gain, ln2_bias, up_bias, down_bias = (
        split_vectors(full_vec.astype(jnp.float32))
    )
    seqs_here = inputs.shape[0]
    local_len = inputs.shape[1]
    token_rows = seqs_here * local_len
    tokens = inputs.reshape(token_rows, D).astype(jnp.float32)
    normed_one = layer_norm(tokens, ln1_gain, ln1_bias).astype(jnp.bfloat16)
    projected = jnp.dot(normed_one, full_qkv, preferred_element_type=jnp.float32) + qkv_bias
    positions = lax.axis_index("seq") * local_len + jnp.arange(local_len)
    cosine, sine_table = rotary_tables(positions.astype(jnp.float32))
    four_shape = (seqs_here, local_len, HEADS, HEAD_DIM)
    queries = apply_rotary(projected[:, :D].reshape(four_shape), cosine, sine_table).astype(
        jnp.bfloat16
    )
    keys_local = apply_rotary(
        projected[:, D : 2 * D].reshape(four_shape), cosine, sine_table
    ).astype(jnp.bfloat16)
    values_local = projected[:, 2 * D :].reshape(seqs_here, local_len, D).astype(jnp.bfloat16)
    keys_all, values_all = (
        lax.all_gather(keys_local.reshape(seqs_here, local_len, D), "seq", axis=1, tiled=True),
        lax.all_gather(values_local, "seq", axis=1, tiled=True),
    )
    total_len = keys_all.shape[1]
    keys_heads = keys_all.reshape(seqs_here, total_len, HEADS, HEAD_DIM)
    values_heads = values_all.reshape(seqs_here, total_len, HEADS, HEAD_DIM)
    scale_factor = 1.0 / math.sqrt(HEAD_DIM)
    allowed = positions[:, None] >= jnp.arange(total_len)[None, :]

    def score_block():
        raw_scores = (
            jnp.einsum("sqhd,skhd->shqk", queries, keys_heads, preferred_element_type=jnp.float32)
            * scale_factor
        )
        return jnp.where(allowed[None, None], raw_scores, MASKED)

    scores = score_block()
    top_score = jnp.max(scores, axis=-1, keepdims=True)
    log_total = top_score + jnp.log(jnp.sum(jnp.exp(scores - top_score), axis=-1, keepdims=True))
    prob_low = jnp.exp(scores - log_total).astype(jnp.bfloat16)
    attended = (
        jnp.einsum("shqk,skhd->sqhd", prob_low, values_heads, preferred_element_type=jnp.float32)
        .reshape(token_rows, D)
        .astype(jnp.bfloat16)
    )
    dense_out = jnp.dot(attended, full_dense, preferred_element_type=jnp.float32) + dense_bias
    normed_two = layer_norm(tokens, ln2_gain, ln2_bias).astype(jnp.bfloat16)
    pre_act = jnp.dot(normed_two, full_up, preferred_element_type=jnp.float32) + up_bias
    hidden = gelu_exact(pre_act).astype(jnp.bfloat16)
    mlp_out = (
        lax.dot_general(hidden, full_down_t, CONTRACT_LAST, preferred_element_type=jnp.float32)
        + down_bias
    )
    outputs = (tokens + dense_out + mlp_out).astype(jnp.bfloat16).reshape(inputs.shape)
    back_qkv, back_dense, back_up, back_down_t = (full_qkv, full_dense, full_up, full_down_t)
    grad_low = out_grad.reshape(token_rows, D)
    grad_wide = grad_low.astype(jnp.float32)
    d_hidden = jnp.dot(grad_low, back_down_t, preferred_element_type=jnp.float32)
    gelu_value, gelu_pull = jax.vjp(gelu_exact, pre_act)
    d_pre = gelu_pull(d_hidden)[0].astype(jnp.bfloat16)
    d_normed_two = lax.dot_general(
        d_pre, back_up, CONTRACT_LAST, preferred_element_type=jnp.float32
    )
    norm_two_value, norm_two_pull = jax.vjp(layer_norm, tokens, ln2_gain, ln2_bias)
    d_tokens_two, d_gain_two, d_bias_two = norm_two_pull(d_normed_two)
    d_up_bias = jnp.sum(d_pre.astype(jnp.float32), axis=0)
    d_out_bias = jnp.sum(grad_wide, axis=0)
    d_attended = lax.dot_general(
        grad_low, back_dense, CONTRACT_LAST, preferred_element_type=jnp.float32
    ).astype(jnp.bfloat16)
    d_att_heads = d_attended.reshape(four_shape)
    scores_again = score_block()
    prob_full = jnp.exp(scores_again - log_total)
    prob_again = prob_full.astype(jnp.bfloat16)
    d_probs = jnp.einsum(
        "sqhd,skhd->shqk", d_att_heads, values_heads, preferred_element_type=jnp.float32
    )
    d_scores = (
        prob_full * (d_probs - jnp.sum(d_probs * prob_full, axis=-1, keepdims=True))
    ).astype(jnp.bfloat16)
    d_queries = (
        jnp.einsum("shqk,skhd->sqhd", d_scores, keys_heads, preferred_element_type=jnp.float32)
        * scale_factor
    )
    d_keys_part = (
        jnp.einsum("shqk,sqhd->skhd", d_scores, queries, preferred_element_type=jnp.float32)
        * scale_factor
    )
    d_values_part = jnp.einsum(
        "shqk,sqhd->skhd", prob_again, d_att_heads, preferred_element_type=jnp.float32
    )
    d_keys_own, d_values_own = (
        lax.psum_scatter(
            d_keys_part.reshape(seqs_here, total_len, D), "seq", scatter_dimension=1, tiled=True
        ),
        lax.psum_scatter(
            d_values_part.reshape(seqs_here, total_len, D), "seq", scatter_dimension=1, tiled=True
        ),
    )
    d_query_flat = rotary_back(d_queries, cosine, sine_table).reshape(token_rows, D)
    d_key_flat = rotary_back(d_keys_own.reshape(four_shape), cosine, sine_table).reshape(
        token_rows, D
    )
    d_projected = jnp.concatenate(
        [d_query_flat, d_key_flat, d_values_own.reshape(token_rows, D)], axis=1
    ).astype(jnp.bfloat16)
    d_qkv_bias = jnp.sum(d_projected.astype(jnp.float32), axis=0)
    d_normed_one = lax.dot_general(
        d_projected, back_qkv, CONTRACT_LAST, preferred_element_type=jnp.float32
    )
    norm_one_value, norm_one_pull = jax.vjp(layer_norm, tokens, ln1_gain, ln1_bias)
    d_tokens_one, d_gain_one, d_bias_one = norm_one_pull(d_normed_one)
    input_grad = (
        (grad_wide + d_tokens_one + d_tokens_two).astype(jnp.bfloat16).reshape(inputs.shape)
    )
    up_part = lax.dot_general(normed_two, d_pre, CONTRACT_ROWS, preferred_element_type=jnp.float32)
    down_part = lax.dot_general(grad_low, hidden, CONTRACT_ROWS, preferred_element_type=jnp.float32)
    qkv_part = lax.dot_general(
        normed_one, d_projected, CONTRACT_ROWS, preferred_element_type=jnp.float32
    )
    dense_part = lax.dot_general(
        attended, grad_low, CONTRACT_ROWS, preferred_element_type=jnp.float32
    )
    whole_shard = lax.psum_scatter(
        jnp.concatenate(
            [
                jnp.concatenate([qkv_part, dense_part], axis=1),
                jnp.concatenate([up_part, down_part], axis=1),
            ],
            axis=1,
        ),
        ("zero", "seq"),
        scatter_dimension=0,
        tiled=True,
    )
    attention_shard = whole_shard[:, : 4 * D]
    mlp_shard = whole_shard[:, 4 * D :]
    vector_local = jnp.concatenate(
        [
            d_gain_one,
            d_bias_one,
            d_qkv_bias,
            d_out_bias,
            d_gain_two,
            d_bias_two,
            d_up_bias,
            d_out_bias,
        ],
        axis=0,
    )
    vector_shard = lax.psum_scatter(vector_local, ("zero", "seq"), scatter_dimension=0, tiled=True)
    vectors_grad, qkv_grad, dense_grad, up_grad, down_grad = lax.psum(
        (
            vector_shard,
            attention_shard[:, : 3 * D],
            attention_shard[:, 3 * D :],
            mlp_shard[:, :FF],
            mlp_shard[:, FF:].T,
        ),
        "dp",
    )
    vec_upd = adam_step(vectors, vectors_grad, vectors_first, vectors_second, 0.0)
    qkv_upd = adam_step(qkv_weight, qkv_grad, qkv_first, qkv_second, WEIGHT_DECAY)
    dense_upd = adam_step(dense_weight, dense_grad, dense_first, dense_second, WEIGHT_DECAY)
    up_upd = adam_step(up_weight, up_grad, up_first, up_second, WEIGHT_DECAY)
    down_upd = adam_step(down_weight, down_grad, down_first, down_second, WEIGHT_DECAY)
    return (
        outputs,
        input_grad,
        vectors_grad,
        qkv_grad,
        dense_grad,
        up_grad,
        down_grad,
        vec_upd[0],
        qkv_upd[0],
        dense_upd[0],
        up_upd[0],
        down_upd[0],
        vec_upd[1],
        qkv_upd[1],
        dense_upd[1],
        up_upd[1],
        down_upd[1],
        vec_upd[2],
        qkv_upd[2],
        dense_upd[2],
        up_upd[2],
        down_upd[2],
    )


def solution(mesh):
    placed = (
        P(("dp", "zero"), "seq", None),
        P(("dp", "zero"), "seq", None),
        P(("zero", "seq")),
        P(("zero", "seq"), None),
        P(("zero", "seq"), None),
        P(("zero", "seq"), None),
        P(None, ("zero", "seq")),
        P(("zero", "seq")),
        P(("zero", "seq"), None),
        P(("zero", "seq"), None),
        P(("zero", "seq"), None),
        P(None, ("zero", "seq")),
        P(("zero", "seq")),
        P(("zero", "seq"), None),
        P(("zero", "seq"), None),
        P(("zero", "seq"), None),
        P(None, ("zero", "seq")),
    )
    return jax.shard_map(
        body,
        mesh=mesh,
        in_specs=placed,
        out_specs=(
            P(("dp", "zero"), "seq", None),
            P(("dp", "zero"), "seq", None),
            P(("zero", "seq")),
            P(("zero", "seq"), None),
            P(("zero", "seq"), None),
            P(("zero", "seq"), None),
            P(None, ("zero", "seq")),
            P(("zero", "seq")),
            P(("zero", "seq"), None),
            P(("zero", "seq"), None),
            P(("zero", "seq"), None),
            P(None, ("zero", "seq")),
            P(("zero", "seq")),
            P(("zero", "seq"), None),
            P(("zero", "seq"), None),
            P(("zero", "seq"), None),
            P(None, ("zero", "seq")),
            P(("zero", "seq")),
            P(("zero", "seq"), None),
            P(("zero", "seq"), None),
            P(("zero", "seq"), None),
            P(None, ("zero", "seq")),
        ),
        check_vma=False,
    )
```

profile of v0, /device:TPU:0, one launch (start us, length us, event | category | flops | bytes accessed | tf_op | source)
XLA Modules:
  0.0 4664.3 jit_solution(11611791577902142899)
XLA Ops:
  11.7 23.7 all-gather.1
  38.1 104.4 %all-gather.9.cloned.1.call-done = bf16[2048,6144]{1,0:T(8,128)(2,1)} async-done(((bf16[128,6144]{1,0:T(8,128)(2,1)}), bf16[2048,6144]{1,0:T(8,128)(2,1)}) %all-gather.9.cloned.1.call-update) | async-done | bytes 25165840 | tf_op jit(solution)/shard_map/all_gather | solution.py:109
  142.5 11.8 convolution_add_fusion.1
  177.9 42.4 all-gather.13.cloned.1.call-done
  230.3 25.5 all-gather.11.cloned.1.call-done
  263.8 28.4 all-gather.19.cloned.1.call-done
  307.9 9.6 fusion.66
  341.6 120.8 %all-gather.15.cloned.1.call-done = bf16[2048,8192]{1,0:T(8,128)(2,1)} async-done(((bf16[128,8192]{1,0:T(8,128)(2,1)}), bf16[2048,8192]{1,0:T(8,128)(2,1)}) %all-gather.15.cloned.1.call-update) | async-done | bytes 33554448 | tf_op jit(solution)/shard_map/all_gather | solution.py:111
  462.3 18.2 convolution_add_fusion
  480.6 160.7 %all-gather.17.cloned.1.call-done = bf16[2048,8192]{0,1:T(8,128)(2,1)} async-done(((bf16[128,8192]{0,1:T(8,128)(2,1)}), bf16[2048,8192]{0,1:T(8,128)(2,1)}) %all-gather.17.cloned.1.call-update) | async-done | bytes 33554448 | tf_op jit(solution)/shard_map/all_gather | solution.py:112
  641.3 23.8 convert_reduce_fusion
  665.1 28.6 convolution_bitcast_fusion
  693.8 26.0 fusion.69
  736.0 53.0 %reduce-scatter.5.cloned.1.call-done = f32[1,256,2048]{1,2,0:T(8,128)} async-done(((f32[1,1024,2048]{1,2,0:T(8,128)}), f32[1,256,2048]{1,2,0:T(8,128)}) %reduce-scatter.5.cloned.1.call-update) | async-done | bytes 2097168 | tf_op jit(solution)/shard_map/reduce_scatter | solution.py:209
  791.7 19.8 fusion.72
  811.5 130.5 %pad_maximum_fusion = f32[2048,24576]{1,0:T(8,128)} fusion(f32[2048,8192]{1,0:T(8,128)} %convolution_bitcast_fusion, f32[2048,8192]{1,0:T(8,128)} %fusion.69, f32[2048,2048]{1,0:T(8,128)} %fusion.50, f32[2048,6144]{1,0:T(8,128)} %fusion.72), kind=kLoop, calls=%fused_computation | loop fusion | flops 150994944 | bytes 402653184 | tf_op jit(solution)/shard_map/concatenate | solution.py:238
  943.9 19.3 fusion.91
  963.3 13.8 fusion.79
  985.7 3226.9 %all-reduce.9.cloned.1.call-done = f32[2048,24576]{1,0:T(8,128)} async-done(((f32[2048,24576]{1,0:T(8,128)}), f32[2048,24576]{1,0:T(8,128)}) %all-reduce.9.cloned.1.call-update) | async-done | bytes 201326608
  4212.6 9.1 dynamic-slice_bitcast_fusion
  4253.1 23.5 fusion.25
  4276.6 25.0 all-reduce.7.cloned.1.call-done
  4308.0 289.9 %all-reduce.11.cloned.1.call-done = (f32[128,6144]{1,0:T(8,128)}, f32[128,2048]{1,0:T(8,128)}, f32[128,8192]{1,0:T(8,128)}, f32[8192,128]{0,1:T(8,128)}) async-done(((f32[128,6144]{1,0:T(8,128)}, f32[128,2048]{1,0:T(8,128)}, f32[128,8192]{1,0:T(8,128)}, f32[8192,128]{0,1:T(8,128)}), (f32[128,6144]{1,0:T(8,128)}, f32[128,2048]{1,0:T(8,128)}, f32[128,8192]{1,0:T(8,128)}, ...) | async-done | bytes 12582928 | tf_op jit(solution)/shard_map/psum | solution.py:265
  4603.7 11.4 multiply_subtract_fusion
  (261 shorter events, 201.7 us)
Async XLA Ops:
  7.2 135.2 %all-gather.9.cloned.1.call-start = ((), (), s32[]{:S(2)}) async-start(), calls=%async_computation.2 | async-start | bytes 26738688 | tf_op jit(solution)/shard_map/all_gather | solution.py:109
  10.7 209.6 %all-gather.13.cloned.1.call-start = ((), (), s32[]{:S(2)}) async-start(), calls=%async_computation.4 | async-start | bytes 8912896 | tf_op jit(solution)/shard_map/all_gather | solution.py:110
  11.6 244.1 %all-gather.11.cloned.1.call-start = ((), (), s32[]{:S(2)}) async-start(), calls=%async_computation.3 | async-start | bytes 5242880 | tf_op jit(solution)/shard_map/all_gather | solution.py:134
  35.5 118.7 %copy-start.44 = (f32[16,1,1664]{2,1,0:T(1,128)}, f32[16,1,1664]{2,1,0:T(1,128)S(1)}, u32[]{:S(2)}) copy-start(f32[16,1,1664]{2,1,0:T(1,128)S(1)} %convert_element_type.139) | copy-start | bytes 319492
  36.2 124.5 %copy-start.33 = (f32[256,64]{1,0:T(8,128)}, f32[256,64]{1,0:T(8,128)S(1)}, u32[]{:S(2)}) copy-start(f32[256,64]{1,0:T(8,128)S(1)} %get-tuple-element.141) | copy-start | bytes 196612
  36.5 117.8 %copy-start.45 = (f32[256]{0:T(256)}, f32[256]{0:T(256)S(1)}, u32[]{:S(2)}) copy-start(f32[256]{0:T(256)S(1)} %broadcast_multiply_fusion.3) | copy-start | bytes 3076
  37.5 116.8 %copy-start.49 = (f32[256]{0:T(256)}, f32[256]{0:T(256)S(1)}, u32[]{:S(2)}) copy-start(f32[256]{0:T(256)S(1)} %fusion.62) | copy-start | bytes 3076
  38.1 116.2 %copy-start.37 = (f32[2048]{0:T(1024)}, f32[2048]{0:T(1024)S(1)}, u32[]{:S(2)}) copy-start(f32[2048]{0:T(1024)S(1)} %get-tuple-element.148) | copy-start | bytes 24580
  38.1 116.2 %copy-start.42 = (f32[2048]{0:T(1024)}, f32[2048]{0:T(1024)S(1)}, u32[]{:S(2)}) copy-start(f32[2048]{0:T(1024)S(1)} %get-tuple-element.147) | copy-start | bytes 24580
  38.1 655.7 %copy-start.40 = (f32[2048]{0:T(1024)}, f32[2048]{0:T(1024)S(1)}, u32[]{:S(2)}) copy-start(f32[2048]{0:T(1024)S(1)} %get-tuple-element.143) | copy-start | bytes 24580
  166.7 125.5 %all-gather.19.cloned.1.call-start = ((), (), s32[]{:S(2)}) async-start(), calls=%async_computation.9 | async-start | bytes 5242880 | tf_op jit(solution)/shard_map/all_gather | solution.py:135
  169.5 292.8 %all-gather.15.cloned.1.call-start = ((), (), s32[]{:S(2)}) async-start(), calls=%async_computation.5 | async-start | bytes 35651584 | tf_op jit(solution)/shard_map/all_gather | solution.py:111
  173.4 467.9 %all-gather.17.cloned.1.call-start = ((), (), s32[]{:S(2)}) async-start(), calls=%async_computation.6 | async-start | bytes 35651584 | tf_op jit(solution)/shard_map/all_gather | solution.py:112
  177.6 542.2 %reduce-scatter.3.cloned.1.call-start = ((), (), s32[]{:S(2)}) async-start(), calls=%async_computation.7 | async-start | bytes 10485760 | tf_op jit(solution)/shard_map/reduce_scatter | solution.py:206
  307.7 481.3 %reduce-scatter.5.cloned.1.call-start = ((), (), s32[]{:S(2)}) async-start(), calls=%async_computation.8 | async-start | bytes 10485760 | tf_op jit(solution)/shard_map/reduce_scatter | solution.py:209
  317.5 3895.2 %all-reduce.9.cloned.1.call-start = ((), (), s32[]{:S(2)}) async-start(), calls=%async_computation.11 | async-start | bytes 402653184
  333.3 129.0 %copy-start.46 = (f32[256]{0:T(256)S(1)}, f32[256]{0:T(256)}, u32[]{:S(2)}) copy-start(f32[256]{0:T(256)} %copy-done.45) | copy-start | bytes 3076
  333.3 129.0 %copy-start.50 = (f32[256]{0:T(256)S(1)}, f32[256]{0:T(256)}, u32[]{:S(2)}) copy-start(f32[256]{0:T(256)} %copy-done.49) | copy-start | bytes 3076
  333.3 129.0 %copy-start.61 = (f32[8192]{0:T(1024)S(1)}, f32[8192]{0:T(1024)}, u32[]{:S(2)}) copy-start(f32[8192]{0:T(1024)} %slice.156) | copy-start | bytes 98308
  734.4 77.1 %copy-start.11 = (bf16[1,256,8,256]{1,3,2,0:T(8,128)(2,1)}, bf16[1,256,8,256]{1,3,2,0:T(8,128)(2,1)S(1)}, u32[]{:S(2)}) copy-start(bf16[1,256,8,256]{1,3,2,0:T(8,128)(2,1)S(1)} %copy.107) | copy-start | bytes 3145732
  736.0 75.5 %copy-start.13 = (bf16[1,256,8,256]{1,3,2,0:T(8,128)(2,1)}, bf16[1,256,8,256]{1,3,2,0:T(8,128)(2,1)S(1)}, u32[]{:S(2)}) copy-start(bf16[1,256,8,256]{1,3,2,0:T(8,128)(2,1)S(1)} %pad_maximum_fusion.5) | copy-start | bytes 3145732
  942.0 3359.6 %all-reduce.7.cloned.1.call-start = ((), (), s32[]{:S(2)}) async-start(), calls=%async_computation.10 | async-start | bytes 212992
  985.7 3612.2 %all-reduce.11.cloned.1.call-start = ((), (), s32[]{:S(2)}) async-start(), calls=%async_computation.12 | async-start | bytes 25165824 | tf_op jit(solution)/shard_map/psum | solution.py:265
  4307.4 296.3 %copy-start.59 = (f32[1664]{0:T(1024)}, f32[1664]{0:T(1024)S(1)}, u32[]{:S(2)}) copy-start(f32[1664]{0:T(1024)S(1)} %psum.35) | copy-start | bytes 19972
  (57 other events, 901.7 us)
Sparse Core Ops, SparseCore 0:
  10.8 131.6 all-gather.8
  145.2 75.0 all-gather.12
  222.4 33.2 all-gather.10
  257.7 34.4 all-gather.18
  294.2 168.0 all-gather.14
  464.3 176.9 all-gather.16
  643.9 70.5 reduce-scatter.2
  717.3 71.6 reduce-scatter.4
  942.1 3270.4 all-reduce.8
  4216.9 84.6 all-reduce.6
  4305.6 292.2 all-reduce.10
where the time goes:
time: 4670 us; the launch traced here: 4660 us
  waiting for transfers between devices  4080 us (87%)
  matrix products  246 us (5%)
  other arithmetic  198 us (4%)
  local copies, waits for them, and re-layouts  97.1 us (2%)
    unnamed x13, waiting for transfers between devices  3250 us
    psum x1, waiting for transfers between devices, body(): lax.psum((vector_shard, attention_shard[:, :3 * D], attention_shard[:, 3...  290 us
    all_gather x1, waiting for transfers between devices, body(): lax.all_gather(down_weight.T.astype(jnp.bfloat16), ('zero', 'seq'), axis=...  161 us
    concatenate x1, other arithmetic, body(): jnp.concatenate([jnp.concatenate([qkv_part, dense_part], axis=1), jnp.con...  130 us
    all_gather x1, waiting for transfers between devices, body(): lax.all_gather(up_weight.astype(jnp.bfloat16), ('zero', 'seq'), axis=0, t...  121 us
    all_gather x1, waiting for transfers between devices, body(): lax.all_gather(qkv_weight.astype(jnp.bfloat16), ('zero', 'seq'), axis=0,...  104 us
  transfers between devices with their start and end apart: 11, of which 10 were waited for; matrix products, arithmetic and copies ran while one was open for 7% of the time, Pallas kernels for 0%

commit v1 on v0

v1 whole, which is shorter than its diff:
```python
import functools
import math

import jax
import jax.numpy as jnp
from jax import lax
from jax.experimental import pallas as pl
from jax.experimental.pallas import tpu as pltpu
from jax.sharding import PartitionSpec as P

D = 2048
HEADS = 8
HEAD_DIM = 256
FF = 8192
ROT = 64
ADAM_STEP = 4

BETA_ONE = 0.9
BETA_TWO = 0.95
LEARN_RATE = 0.5
EPSILON = 1e-08
WEIGHT_DECAY = 0.1
NORM_EPSILON = 1e-05
MASKED = -1e30
BF = jnp.bfloat16
F32 = jnp.float32
NT = (((1,), (1,)), ((), ()))
TN = (((0,), (0,)), ((), ()))


def rotary_tables(positions):
    half_rot = ROT // 2
    exponent = jnp.arange(half_rot, dtype=F32) * (2.0 / ROT)
    inverse = jnp.power(10000.0, -exponent)
    angles = positions[:, None] * inverse[None, :]
    angles = jnp.concatenate([angles, angles], axis=1)
    return (jnp.cos(angles), jnp.sin(angles))


def adam_step(parameter, gradient, first_moment, second, decay_rate):
    first_new = BETA_ONE * first_moment + (1.0 - BETA_ONE) * gradient
    second_new = BETA_TWO * second + (1.0 - BETA_TWO) * gradient * gradient
    first_hat = first_new / (1.0 - BETA_ONE**ADAM_STEP)
    second_hat = second_new / (1.0 - BETA_TWO**ADAM_STEP)
    param_new = parameter - LEARN_RATE * (
        first_hat / (jnp.sqrt(second_hat) + EPSILON) + decay_rate * parameter
    )
    return (param_new, first_new, second_new)


def swap(value, axis, size, bit):
    return lax.ppermute(value, axis, [(i, i ^ bit) for i in range(size)])


def take(value, index, axis):
    return lax.dynamic_index_in_dim(value, index, axis, keepdims=False)


def pair(mine, other, my_bit, axis):
    low = jnp.where(my_bit == 0, mine, other)
    high = jnp.where(my_bit == 0, other, mine)
    return jnp.stack([low, high], axis=axis)


def bits_of(size):
    return [1 << k for k in reversed(range(size.bit_length() - 1))]


def exchange(value, axis, size):
    place = lax.axis_index(axis)
    rest = value.shape[1:]
    for bit in bits_of(size):
        outer = size // (2 * bit)
        split = value.reshape((outer, 2, bit) + rest)
        my_bit = (place // bit) % 2
        mine = take(split, my_bit, 1)
        theirs = take(split, 1 - my_bit, 1)
        got = swap(theirs, axis, size, bit)
        value = pair(mine, got, my_bit, 1).reshape((size,) + rest)
    return value


def line_gather(block, size):
    place = lax.axis_index("zero")
    whole = jnp.zeros((size,) + block.shape, block.dtype)
    whole = lax.dynamic_update_index_in_dim(whole, block, place, 0)
    above, below = block, block
    ups, downs = {}, {}
    for step in range(1, size):
        above = lax.ppermute(above, "zero", [(i, i + 1) for i in range(step - 1, size - 1)])
        below = lax.ppermute(below, "zero", [(i, i - 1) for i in range(1, size - step + 1)])
        ups[step], downs[size - step] = above, below
    for step in range(1, size):
        got = jnp.where(place >= step, ups[step], downs[step])
        whole = lax.dynamic_update_index_in_dim(whole, got, lax.rem(place - step + size, size), 0)
    return whole


def line_scatter(parts, size):
    place = lax.axis_index("zero")
    up_sum, down_sum = None, None
    for step in range(1, size):
        up_at = jnp.clip(size + place - step, 0, size - 1)
        down_at = jnp.clip(place + step - size, 0, size - 1)
        up_own = take(parts, up_at, 0)
        down_own = take(parts, down_at, 0)
        if up_sum is None:
            up_send, down_send = up_own, down_own
        else:
            up_send = (up_own.astype(F32) + up_sum.astype(F32)).astype(BF)
            down_send = (down_own.astype(F32) + down_sum.astype(F32)).astype(BF)
        up_sum = lax.ppermute(up_send, "zero", [(i, i + 1) for i in range(0, step)])
        down_sum = lax.ppermute(down_send, "zero", [(i, i - 1) for i in range(size - step, size)])
    own = take(parts, place, 0)
    return (own.astype(F32) + up_sum.astype(F32) + down_sum.astype(F32)).astype(BF)


def attention_body(scale, projected, cos_ref, sin_ref, d_att_ref, att_ref, d_proj_ref, keys_acc, values_acc):
    length = projected.shape[1]
    tile = min(256, length)
    half = ROT // 2
    cosine = cos_ref[...]
    sine = sin_ref[...]

    def turn(block):
        first = block[:, :128]
        rolled = jnp.concatenate([first[:, half:ROT], first[:, :half], first[:, ROT:]], axis=1)
        return jnp.concatenate([first * cosine + rolled * sine, block[:, 128:]], axis=1)

    def turn_back(block):
        first = block[:, :128]
        scaled = first * sine
        rolled = jnp.concatenate([scaled[:, half:ROT], scaled[:, :half], scaled[:, ROT:]], axis=1)
        return jnp.concatenate([first * cosine + rolled, block[:, 128:]], axis=1)

    queries = turn(projected[0, :, 0:HEAD_DIM]).astype(BF)
    keys = turn(projected[0, :, HEAD_DIM : 2 * HEAD_DIM]).astype(BF)
    values = projected[0, :, 2 * HEAD_DIM :].astype(BF)
    d_att_all = d_att_ref[0]
    keys_acc[...] = jnp.zeros_like(keys_acc)
    values_acc[...] = jnp.zeros_like(values_acc)
    d_queries = []
    for at in range(length // tile):
        rows = slice(at * tile, (at + 1) * tile)
        seen = (at + 1) * tile
        q = queries[rows]
        d_att = d_att_all[rows]
        k, v = keys[:seen], values[:seen]
        scores = lax.dot_general(q, k, NT, preferred_element_type=F32) * scale
        row = lax.broadcasted_iota(jnp.int32, scores.shape, 0) + at * tile
        column = lax.broadcasted_iota(jnp.int32, scores.shape, 1)
        scores = jnp.where(row >= column, scores, MASKED)
        top = jnp.max(scores, axis=1, keepdims=True)
        grown = jnp.exp(scores - top)
        prob = grown * (1.0 / jnp.sum(grown, axis=1, keepdims=True))
        prob_low = prob.astype(BF)
        att_ref[0, rows, :] = jnp.dot(prob_low, v, preferred_element_type=F32).astype(BF)
        d_prob = lax.dot_general(d_att, v, NT, preferred_element_type=F32)
        inner = jnp.sum(d_prob * prob, axis=1, keepdims=True)
        d_scores = (prob * (d_prob - inner)).astype(BF)
        d_queries.append(jnp.dot(d_scores, k, preferred_element_type=F32) * scale)
        keys_acc[:seen, :] += lax.dot_general(d_scores, q, TN, preferred_element_type=F32)
        values_acc[:seen, :] += lax.dot_general(prob_low, d_att, TN, preferred_element_type=F32)
    d_proj_ref[0, :, 0:HEAD_DIM] = turn_back(jnp.concatenate(d_queries, axis=0)).astype(BF)
    d_proj_ref[0, :, HEAD_DIM : 2 * HEAD_DIM] = turn_back(keys_acc[...] * scale).astype(BF)
    d_proj_ref[0, :, 2 * HEAD_DIM :] = values_acc[...].astype(BF)


def attention(projected, d_att):
    seqs, length, _ = projected.shape
    cosine, sine = rotary_tables(jnp.arange(length).astype(F32))
    half = ROT // 2
    sine_turn = jnp.concatenate([-sine[:, :half], sine[:, half:]], axis=1)
    cosine = jnp.concatenate([cosine, jnp.ones((length, 128 - ROT), F32)], axis=1)
    sine_turn = jnp.concatenate([sine_turn, jnp.zeros((length, 128 - ROT), F32)], axis=1)
    whole = pl.BlockSpec((length, 128), lambda s: (0, 0))
    one = lambda width: pl.BlockSpec((1, length, width), lambda s: (s, 0, 0))
    return pl.pallas_call(
        functools.partial(attention_body, 1.0 / math.sqrt(HEAD_DIM)),
        grid=(seqs,),
        in_specs=[one(3 * HEAD_DIM), whole, whole, one(HEAD_DIM)],
        out_specs=[one(HEAD_DIM), one(3 * HEAD_DIM)],
        out_shape=[
            jax.ShapeDtypeStruct((seqs, length, HEAD_DIM), BF),
            jax.ShapeDtypeStruct((seqs, length, 3 * HEAD_DIM), BF),
        ],
        scratch_shapes=[pltpu.VMEM((length, HEAD_DIM), F32), pltpu.VMEM((length, HEAD_DIM), F32)],
        compiler_params=pltpu.CompilerParams(vmem_limit_bytes=48 * 1024 * 1024),
        cost_estimate=pl.CostEstimate(
            flops=seqs * length * length * HEAD_DIM * 9,
            bytes_accessed=seqs * length * HEAD_DIM * 22,
            transcendentals=seqs * length * length,
        ),
        name="attention",
    )(projected, cosine, sine_turn, d_att)


def gelu_parts(values):
    phi_wide = 0.5 * (1.0 + lax.erf(values * (1.0 / math.sqrt(2.0))))
    density = jnp.exp(-0.5 * values * values) * (1.0 / math.sqrt(2.0 * math.pi))
    return values * phi_wide, phi_wide + values * density


def make_body(sizes):
    n_dp, n_zero, n_seq = sizes["dp"], sizes["zero"], sizes["seq"]
    parts = n_dp * n_seq
    head_w = D // parts
    hid_w = FF // parts
    plane = ("dp", "seq")
    dp_bits = [("dp", n_dp, bit) for bit in bits_of(n_dp)]
    seq_bits = [("seq", n_seq, bit) for bit in bits_of(n_seq)]
    far_bits, core_bits = seq_bits[:-1], seq_bits[-1:]

    def plane_gather(value, steps):
        shape = value.shape
        for axis, size, bit in steps:
            got = swap(value, axis, size, bit)
            value = pair(value, got, (lax.axis_index(axis) // bit) % 2, 0)
        order = [parts_index for parts_index in reversed(steps)]
        value = value.reshape((2,) * len(steps) + shape)
        wanted = dp_bits + seq_bits
        perm = [order.index(step) for step in wanted]
        value = jnp.transpose(value, perm + [len(steps) + k for k in range(len(shape))])
        return value.reshape((n_dp, n_seq) + shape)

    def plane_exchange(value):
        rest = value.shape[1:]
        value = value.reshape((n_dp, n_seq) + rest)
        value = jnp.swapaxes(value, 0, 1)
        value = exchange(value, "seq", n_seq)
        value = jnp.swapaxes(value, 0, 1)
        value = exchange(value, "dp", n_dp)
        return value.reshape((parts,) + rest)

    def body(
        inputs,
        out_grad,
        vectors,
        qkv_weight,
        dense_weight,
        up_weight,
        down_weight,
        vectors_first,
        qkv_first,
        dense_first,
        up_first,
        down_first,
        vectors_second,
        qkv_second,
        dense_second,
        up_second,
        down_second,
    ):
        dp_i, zero_i, seq_i = lax.axis_index("dp"), lax.axis_index("zero"), lax.axis_index("seq")
        part_i = dp_i * n_seq + seq_i
        seqs_here, local_len = inputs.shape[0], inputs.shape[1]
        token_rows = seqs_here * local_len
        rows_d = qkv_weight.shape[0]
        block_d = rows_d * n_seq

        vec_all = lax.all_gather(vectors.astype(BF), ("zero", "seq"), axis=0, tiled=True).astype(F32)
        ln1_gain, ln1_bias = vec_all[:D], vec_all[D : 2 * D]
        qkv_bias = vec_all[2 * D : 5 * D].reshape(3, parts, head_w)
        dense_bias = vec_all[5 * D : 6 * D]
        ln2_gain, ln2_bias = vec_all[6 * D : 7 * D], vec_all[7 * D : 8 * D]
        up_bias = vec_all[8 * D : 8 * D + FF].reshape(parts, hid_w)
        down_bias = vec_all[8 * D + FF :]

        half = lambda value, axis: take(
            value.reshape(value.shape[:axis] + (n_dp, n_seq, -1) + value.shape[axis + 1 :]), dp_i, axis
        )
        qkv_low = qkv_weight.astype(BF).reshape(rows_d, 3, n_dp, n_seq, head_w)
        qkv_low = take(qkv_low, dp_i, 2).transpose(2, 0, 1, 3).reshape(n_seq, rows_d, 3 * head_w)
        dense_low = half(dense_weight.astype(BF), 1).transpose(1, 0, 2)
        up_low = half(up_weight.astype(BF), 1).transpose(1, 0, 2)
        down_low = half(down_weight.astype(BF), 0)

        attn_block = exchange(jnp.concatenate([dense_low, qkv_low], axis=2), "seq", n_seq)
        attn_block = attn_block.reshape(block_d, 4 * head_w)
        dense_cols = line_gather(attn_block[:, :head_w], n_zero).reshape(D, head_w)
        qkv_own = line_gather(attn_block[:, head_w:], n_zero).reshape(D, 3 * head_w)
        dense_own = plane_exchange(dense_cols.reshape(parts, head_w, head_w))
        dense_own = dense_own.transpose(1, 0, 2).reshape(head_w, D)
        up_block = exchange(up_low, "seq", n_seq).reshape(block_d, hid_w)
        up_own = line_gather(up_block, n_zero).reshape(D, hid_w)
        down_block = exchange(down_low, "seq", n_seq).transpose(1, 0, 2).reshape(hid_w, block_d)
        down_own = line_gather(down_block, n_zero).transpose(1, 0, 2).reshape(hid_w, D)

        tokens_low = inputs.reshape(token_rows, D)
        grad_low = out_grad.reshape(token_rows, D)
        tokens_all = plane_gather(tokens_low, far_bits + dp_bits + core_bits)
        grad_all = plane_gather(grad_low, dp_bits + far_bits + core_bits)
        order = lambda value: value.reshape(n_dp, n_seq, seqs_here, local_len, D).transpose(
            0, 2, 1, 3, 4
        ).reshape(n_dp * seqs_here * n_seq * local_len, D)
        unorder = lambda value: value.reshape(n_dp, seqs_here, n_seq, local_len, D).transpose(
            0, 2, 1, 3, 4
        ).reshape(n_dp, n_seq, token_rows, D)
        tokens = order(tokens_all)
        grads = order(grad_all)
        seqs = n_dp * seqs_here
        length = n_seq * local_len

        def statistics(values):
            average = jnp.mean(values, axis=-1, keepdims=True)
            centred = values - average
            spread = jnp.mean(centred * centred, axis=-1, keepdims=True)
            return centred, lax.rsqrt(spread + NORM_EPSILON)

        centred, rate = statistics(tokens.astype(F32))
        xhat = centred * rate
        normed_one = (xhat * ln1_gain + ln1_bias).astype(BF)
        normed_two = (xhat * ln2_gain + ln2_bias).astype(BF)

        projected = jnp.dot(normed_one, qkv_own, preferred_element_type=F32)
        projected = projected + take(qkv_bias, part_i, 1).reshape(3 * head_w)
        d_att = lax.dot_general(grads, dense_own, NT, preferred_element_type=F32).astype(BF)
        attended, d_proj = attention(
            projected.reshape(seqs, length, 3 * head_w), d_att.reshape(seqs, length, head_w)
        )
        attended = attended.reshape(seqs * length, head_w)
        d_proj = d_proj.reshape(seqs * length, 3 * head_w)
        d_qkv_bias = jnp.sum(d_proj.astype(F32), axis=0)
        d_normed_one = lax.dot_general(d_proj, qkv_own, NT, preferred_element_type=F32)
        qkv_part = lax.dot_general(normed_one, d_proj, TN, preferred_element_type=F32).astype(BF)
        dense_part = lax.dot_general(attended, grads, TN, preferred_element_type=F32).astype(BF)
        dense_part = plane_exchange(dense_part.reshape(head_w, parts, head_w).transpose(1, 0, 2))
        dense_part = dense_part.reshape(D, head_w)
        attn_parts = jnp.concatenate([dense_part, qkv_part], axis=1).reshape(n_zero, block_d, 4 * head_w)
        attn_sum = line_scatter(attn_parts, n_zero)

        pre_act = jnp.dot(normed_two, up_own, preferred_element_type=F32) + take(up_bias, part_i, 0)
        hidden_wide, slope = gelu_parts(pre_act)
        hidden = hidden_wide.astype(BF)
        down_part = lax.dot_general(hidden, grads, TN, preferred_element_type=F32).astype(BF)
        down_parts = down_part.reshape(hid_w, n_zero, block_d).transpose(1, 0, 2)
        down_sum = line_scatter(down_parts, n_zero)
        d_hidden = lax.dot_general(grads, down_own, NT, preferred_element_type=F32)
        d_pre_wide = (d_hidden * slope).astype(BF)
        d_pre = d_pre_wide
        d_up_bias = jnp.sum(d_pre.astype(F32), axis=0)
        up_part = lax.dot_general(normed_two, d_pre, TN, preferred_element_type=F32).astype(BF)
        up_sum = line_scatter(up_part.reshape(n_zero, block_d, hid_w), n_zero)
        d_normed_two = lax.dot_general(d_pre, up_own, NT, preferred_element_type=F32)

        out_part = jnp.dot(attended, dense_own, preferred_element_type=F32) + jnp.dot(
            hidden, down_own, preferred_element_type=F32
        )
        out_sum = lax.psum_scatter(
            unorder(out_part.astype(BF)).reshape(parts, token_rows, D), plane, scatter_dimension=0
        )
        tokens_wide = tokens_low.astype(F32)
        grad_wide = grad_low.astype(F32)
        outputs = (tokens_wide + out_sum.astype(F32) + dense_bias + down_bias).astype(BF)
        outputs = outputs.reshape(inputs.shape)

        d_gain_one = jnp.sum(d_normed_one * xhat, axis=0)
        d_bias_one = jnp.sum(d_normed_one, axis=0)
        d_gain_two = jnp.sum(d_normed_two * xhat, axis=0)
        d_bias_two = jnp.sum(d_normed_two, axis=0)
        d_xhat = (d_normed_one * ln1_gain + d_normed_two * ln2_gain).astype(BF)
        d_xhat = lax.psum_scatter(
            unorder(d_xhat).reshape(parts, token_rows, D), plane, scatter_dimension=0
        ).astype(F32)
        centred_own, rate_own = statistics(tokens_wide)
        xhat_own = centred_own * rate_own
        d_tokens = rate_own * (
            d_xhat
            - jnp.mean(d_xhat, axis=-1, keepdims=True)
            - xhat_own * jnp.mean(d_xhat * xhat_own, axis=-1, keepdims=True)
        )
        input_grad = (grad_wide + d_tokens).astype(BF).reshape(inputs.shape)

        d_out_bias = jnp.sum(grad_wide, axis=0)
        place_in = lambda value, count: lax.dynamic_update_index_in_dim(
            jnp.zeros((value.shape[0], count, value.shape[1]), F32), value, part_i, 1
        ).reshape(-1)
        vector_local = jnp.concatenate(
            [
                d_gain_one,
                d_bias_one,
                place_in(d_qkv_bias.reshape(3, head_w), parts),
                d_out_bias,
                d_gain_two,
                d_bias_two,
                place_in(d_up_bias.reshape(1, hid_w), parts),
                d_out_bias,
            ]
        )
        vector_sum = lax.psum(vector_local, ("dp", "zero", "seq"))
        vectors_grad = lax.dynamic_slice_in_dim(
            vector_sum, (zero_i * n_seq + seq_i) * vectors.shape[0], vectors.shape[0], 0
        )

        def home(value):
            value = exchange(value, "seq", n_seq)
            return exchange_all(value)

        def exchange_all(value):
            for step in dp_bits:
                got = swap(value, *step)
                value = pair(value, got, (dp_i // step[2]) % 2, 0)
            return value.reshape((n_dp, n_seq) + value.shape[-2:])

        attn_home = home(attn_sum.reshape(n_seq, rows_d, 4 * head_w))
        dense_grad = attn_home[..., :head_w].transpose(2, 0, 1, 3).reshape(rows_d, D).astype(F32)
        qkv_grad = attn_home[..., head_w:].reshape(n_dp, n_seq, rows_d, 3, head_w)
        qkv_grad = qkv_grad.transpose(2, 3, 0, 1, 4).reshape(rows_d, 3 * D).astype(F32)
        down_home = home(down_sum.reshape(hid_w, n_seq, rows_d).transpose(1, 0, 2))
        down_grad = down_home.reshape(FF, rows_d).astype(F32)
        up_home = home(up_sum.reshape(n_seq, rows_d, hid_w))
        up_grad = up_home.transpose(2, 0, 1, 3).reshape(rows_d, FF).astype(F32)

        vec_upd = adam_step(vectors, vectors_grad, vectors_first, vectors_second, 0.0)
        qkv_upd = adam_step(qkv_weight, qkv_grad, qkv_first, qkv_second, WEIGHT_DECAY)
        dense_upd = adam_step(dense_weight, dense_grad, dense_first, dense_second, WEIGHT_DECAY)
        up_upd = adam_step(up_weight, up_grad, up_first, up_second, WEIGHT_DECAY)
        down_upd = adam_step(down_weight, down_grad, down_first, down_second, WEIGHT_DECAY)
        updates = (vec_upd, qkv_upd, dense_upd, up_upd, down_upd)
        return (
            (outputs, input_grad, vectors_grad, qkv_grad, dense_grad, up_grad, down_grad)
            + tuple(update[0] for update in updates)
            + tuple(update[1] for update in updates)
            + tuple(update[2] for update in updates)
        )

    return body


def solution(mesh):
    wide = P(("dp", "zero"), "seq", None)
    vector = P(("zero", "seq"))
    rows = P(("zero", "seq"), None)
    columns = P(None, ("zero", "seq"))
    state = (vector, rows, rows, rows, columns)
    return jax.shard_map(
        make_body(dict(mesh.shape)),
        mesh=mesh,
        in_specs=(wide, wide) + state * 3,
        out_specs=(wide, wide) + state * 4,
        check_vma=False,
    )
```

time: 4670 us -> 981 us (0.21)
  waiting for transfers between devices: 4080 us -> 295 us
  starting transfers between devices: 1.09 us -> 127 us
  matrix products: 246 us -> 142 us
  local copies, waits for them, and re-layouts: 97.1 us -> 195 us
    unnamed x13 -> x3, waiting for transfers between devices: 3250 us -> 0.55 us
    all_gather x6 -> x0, waiting for transfers between devices: 482 us -> none  [the longest x1 161 us: body(): lax.all_gather(down_weight.T.astype(jnp.bfloat16), ('zero', 'seq'), axis=...]
    ppermute x0 -> x69, waiting for transfers between devices: none -> 295 us  [the longest x27 126 us: swap(): return lax.ppermute(value, axis, [(i, i ^ bit) for i in range(size)])]
    psum x1, waiting for transfers between devices: 290 us -> 0.01 us  [body(): vector_sum = lax.psum(vector_local, ('dp', 'zero', 'seq'))]
    concatenate x5 -> x1, other arithmetic: 138 us -> 1.41 us  [attention(): jnp.concatenate([sine_turn, jnp.zeros((length, 128 - ROT), F32)], axis=1)]
    ppermute x0 -> x69, starting transfers between devices: none -> 127 us  [the longest x12 43.1 us: line_gather(): lax.ppermute(above, 'zero', [(i, i + 1) for i in range(step - 1, size - 1)])]
    dot_general x18 -> x12, matrix products: 246 us -> 142 us  [the longest x1 21.5 us: body(): lax.dot_general(d_pre, up_own, NT, preferred_element_type=F32)]
    reduce_scatter x2, waiting for transfers between devices: 53 us -> 0.03 us  [the longest x1 0.03 us: body(): lax.psum_scatter(unorder(out_part.astype(BF)).reshape(parts, token_rows,...]
  transfers between devices with their start and end apart: 11 -> 72, of which waited for: 10 -> 31; matrix products, arithmetic and copies ran while one was open for 7% -> 38% of each run, Pallas kernels for 0% -> 1%
where the time goes in v1:
time: 981 us; the launch traced here: 971 us
  waiting for transfers between devices  295 us (30%)
  local copies, waits for them, and re-layouts  195 us (20%)
  other arithmetic  162 us (17%)
  matrix products  142 us (14%)
  starting transfers between devices  127 us (13%)
  blocking collectives  19.4 us (2%)
  between operations  17.8 us (2%)
  Pallas kernels  12.2 us (1%)
    ppermute x27, waiting for transfers between devices, swap(): return lax.ppermute(value, axis, [(i, i ^ bit) for i in range(size)])  126 us
    unnamed x206, local copies, waits for them, and re-layouts  93.2 us
    ppermute x9, waiting for transfers between devices, line_scatter(): up_sum = lax.ppermute(up_send, 'zero', [(i, i + 1) for i in range(0, step)])  86.9 us
    ppermute x12, waiting for transfers between devices, line_gather(): lax.ppermute(below, 'zero', [(i, i - 1) for i in range(1, size - step + 1)])  49.3 us
    ppermute x12, starting transfers between devices, line_gather(): lax.ppermute(above, 'zero', [(i, i + 1) for i in range(step - 1, size - 1)])  43.1 us
    another operation x46, other arithmetic, pair(): return jnp.stack([low, high], axis=axis)  39.9 us
    ppermute x9, starting transfers between devices, line_scatter(): up_sum = lax.ppermute(up_send, 'zero', [(i, i + 1) for i in range(0, step)])  37 us
    sub x5, other arithmetic, adam_step(): parameter - LEARN_RATE * (first_hat / (jnp.sqrt(second_hat) + EPSILON) +...  30.5 us
  transfers between devices with their start and end apart: 72, of which 31 were waited for; matrix products, arithmetic and copies ran while one was open for 38% of the time, Pallas kernels for 1%

profile of v1, /device:TPU:0, one launch (start us, length us, event | category | flops | bytes accessed | tf_op | source)
XLA Modules:
  0.0 970.6 jit_solution(697198243628921441)
XLA Ops:
  60.7 31.5 %collective-permute-done.12 = bf16[2,256,2048]{2,1,0:T(8,128)(2,1)} collective-permute-done((bf16[2,256,2048]{2,1,0:T(8,128)(2,1)}, bf16[2,256,2048]{2,1,0:T(8,128)(2,1)}, u32[]{:S(2)}, u32[]{:S(2)}) %collective-permute-start.12) | collective-permute-done | bytes 2097184 | tf_op jit(solution)/shard_map/ppermute | solution.py:52
  110.3 13.4 %collective-permute-done.25 = bf16[512,1024]{1,0:T(8,128)(2,1)} collective-permute-done((bf16[512,1024]{1,0:T(8,128)(2,1)S(1)}, bf16[512,1024]{1,0:T(8,128)(2,1)}, u32[]{:S(2)}, u32[]{:S(2)}) %collective-permute-start.25) | collective-permute-done | bytes 1048608 | tf_op jit(solution)/shard_map/ppermute | solution.py:90
  148.2 19.4 %all-gather = bf16[16,1,1664]{2,1,0:T(2,128)(2,1)S(1)} all-gather(bf16[1,1,1664]{2,1,0:T(2,128)(2,1)S(1)} %reshape.523), channel_id=1, replica_groups=mesh['dp'=2,'zero'=4,'seq'=4] {'zero','seq'}, dimensions={0}, use_global_device_ids=true | all-gather | bytes 56576 | tf_op jit(solution)/shard_map/all_gather | solution.py:261
  217.1 14.1 %multiply_convert_fusion = (bf16[2048,1024]{1,0:T(8,128)(2,1)S(1)}, f32[2048,1024]{1,0:T(8,128)}) fusion(f32[1024]{0:T(1024)S(1)} %bitcast.661, bf16[2048,2048]{1,0:T(8,128)(2,1)S(1)} %bitcast.606, bf16[2048,1024]{1,0:T(8,128)(2,1)} %bitcast.88), kind=kOutput, calls=%fused_computation.39 | convolution fusion | flops 8602517504 | bytes 25169920 | tf_op jit(solution)/shard_map/dot_general | solution.py:332
  233.2 11.1 %convolution_convert_fusion = bf16[1024,2048]{1,0:T(8,128)(2,1)} fusion(bf16[2048,1024]{1,0:T(8,128)(2,1)S(1)} %get-tuple-element.239, bf16[2048,2048]{1,0:T(8,128)(2,1)S(1)} %bitcast.573), kind=kOutput, calls=%fused_computation.65 | convolution fusion | flops 8592031744 | bytes 16777216 | tf_op jit(solution)/shard_map/dot_general | solution.py:335
  252.1 26.0 %constant_dynamic-slice_fusion.6 = (bf16[1024,1,512]{2,1,0:T(2,128)(2,1)S(1)}, bf16[1024,1,512]{2,1,0:T(2,128)(2,1)}, bf16[1024,1,512]{2,1,0:T(2,128)(2,1)}, bf1...) fusion(bf16[1024,4,512]{2,1,0:T(4,128)(2,1)} %reshape.498, ...), kind=kLoop, calls=%fused_computation.349 | loop fusion | bytes 14680092 | tf_op jit(solution)/shard_map/dynamic-slice.20
  285.2 10.7 %collective-permute-done.3 = bf16[1,2,128,1024]{2,3,1,0:T(8,128)(2,1)S(1)} collective-permute-done((bf16[1,2,128,1024]{2,3,1,0:T(8,128)(2,1)S(1)}, bf16[1,2,128,1024]{2,3,1,0:T(8,128)(2,1)S(1)}, u32[]{:S(2)}, u32[]{:S(2)}) %collective-permute-start.3) | collective-permute-done | bytes 524320 | tf_op jit(solution)/shard_map/ppermute | solution.py:52
  320.2 14.1 %collective-permute-done.61 = bf16[1024,512]{1,0:T(8,128)(2,1)} collective-permute-done((bf16[1024,512]{1,0:T(8,128)(2,1)}, bf16[1024,512]{1,0:T(8,128)(2,1)}, u32[]{:S(2)}, u32[]{:S(2)}) %collective-permute-start.61) | collective-permute-done | bytes 1048608 | tf_op jit(solution)/shard_map/ppermute | solution.py:112
  345.9 12.7 %collective-permute-start.14 = (bf16[512,256]{1,0:T(8,128)(2,1)S(1)}, bf16[512,256]{1,0:T(8,128)(2,1)S(1)}, u32[]{:S(2)}, u32[]{:S(2)}) collective-permute-start(bf16[512,256]{1,0:T(8,128)(2,1)S(1)} %slice.84), channel_id=1, source_target_pairs={{0,4},{4,8},{8,12},{1,5},{5,9},{9,13},{2,6},{6,10},{10,14},{3,7},{... | collective-permute-start | bytes 786440 | tf_op jit(solution)/shard_map/ppermute | solution.py:90
  427.9 11.7 %collective-permute-done.7 = bf16[512,768]{1,0:T(8,128)(2,1)} collective-permute-done((bf16[512,768]{1,0:T(8,128)(2,1)}, bf16[512,768]{1,0:T(8,128)(2,1)}, u32[]{:S(2)}, u32[]{:S(2)}) %collective-permute-start.7) | collective-permute-done | bytes 786464 | tf_op jit(solution)/shard_map/ppermute | solution.py:91
  490.8 11.7 %broadcast_add_fusion = f32[2048,768]{1,0:T(8,128)} fusion(f32[768]{0:T(1024)S(1)} %add.504, bf16[2048,2048]{1,0:T(8,128)(2,1)} %bitcast.600, bf16[2048,768]{1,0:T(8,128)(2,1)} %bitcast.646), kind=kOutput, calls=%fused_computation.74 | convolution fusion | flops 6444023808 | bytes 17828864 | tf_op jit(solution)/shard_map/dot_general | solution.py:315
  521.2 12.2 %attention.1 = (bf16[2,1024,256]{2,1,0:T(8,128)(2,1)S(1)}, bf16[2,1024,768]{2,1,0:T(8,128)(2,1)}) custom-call(f32[2,1024,768]{2,1,0:T(8,128)} %bitcast.664, f32[1024,128]{1,0:T(8,128)S(1)} %concatenate.32.cos_ref, f32[1024,128]{1,0:T(8,128)S(1)} %maximum_maximum_fusion.sin_ref, bf16[2,1024,256]{2,1,0:T(8,128)(2,1)S(1)} %bitcast.568), custom_call_target="tpu_custom_call" | custom-call | flops 4831838208 | bytes 11534336 | tf_op jit(solution)/shard_map/attention/pallas_call | solution.py:178
  542.8 12.3 %fusion.142 = f32[2048,2048]{1,0:T(8,128)} fusion(bf16[2048,768]{1,0:T(8,128)(2,1)} %bitcast.644, bf16[2048,768]{1,0:T(8,128)(2,1)S(1)} %bitcast.647), kind=kOutput, calls=%fused_computation.388 | convolution fusion | flops 6442450944 | bytes 23068672 | tf_op jit(solution)/shard_map/dot_general | solution.py:324
  569.5 16.6 %convert_reduce_fusion = (f32[1024]{0:T(1024)S(1)}, bf16[2048,1024]{1,0:T(8,128)(2,1)}) fusion(f32[2048,1024]{1,0:T(8,128)} %get-tuple-element.240, f32[1024]{0:T(1024)S(1)} %bitcast.662, bf16[2048,2048]{1,0:T(8,128)(2,1)S(1)} %bitcast.576, bf16[1024,2048]{0,1:T(8,128)(2,1)S(1)} %bitcast.624), kind=kOutput, calls=%fused_computation.38 | convolution fusion | flops 8617196544 | bytes 25174016 | tf_op jit(solution)/shard_map/dot_general | solution.py:338
  586.1 21.5 %fusion.133 = (f32[2048]{0:T(1024)S(1)}, f32[2048]{0:T(1024)S(1)}, bf16[2048,2048]{1,0:T(8,128)(2,1)}, f32[2048]{0:T(1024)S(1)}, f32[2048]{0:T(1024)S(1)}, /*index=5*/bf16[2048,2048]{1,0:T(8,128)(2,1)}) fusion(f32[2048]{0:T(1024)S(1)} %bitcast.659, f32[2048]{0:T(1024)S(1)} %bitcast.660, bf16[1,2,2,256,2048]{4,3,0,2,1:T(8,128)(2,1)S(1)} %copy-done.3, ...), kind=kOutput, calls=%fused_computation.384 | convolution fusion | flops 8661229568 | bytes 50405376 | tf_op jit(solution)/shard_map/dot_general | solution.py:344
  619.6 10.5 %collective-permute-done.39 = bf16[1,2,2,256,256]{4,3,2,1,0:T(8,128)(2,1)S(1)} collective-permute-done((bf16[1,2,2,256,256]{4,3,2,1,0:T(8,128)(2,1)S(1)}, bf16[1,2,2,256,256]{4,3,2,1,0:T(8,128)(2,1)S(1)}, u32[]{:S(2)}, u32[]{:S(2)}) %collective-permute-start.39) | collective-permute-done | bytes 524320 | tf_op jit(solution)/shard_map/ppermute | solution.py:52
  633.2 12.0 %convolution_convert_fusion.1 = bf16[2048,1024]{1,0:T(8,128)(2,1)S(1)} fusion(bf16[2048,2048]{1,0:T(8,128)(2,1)} %get-tuple-element.138, bf16[2048,1024]{1,0:T(8,128)(2,1)S(1)} %copy-done.78), kind=kOutput, calls=%fused_computation.66 | convolution fusion | flops 8592031744 | bytes 16777216 | tf_op jit(solution)/shard_map/dot_general | solution.py:342
  659.9 11.0 %collective-permute-done.51 = bf16[512,1024]{1,0:T(8,128)(2,1)S(1)} collective-permute-done((bf16[512,1024]{1,0:T(8,128)(2,1)S(1)}, bf16[512,1024]{1,0:T(8,128)(2,1)S(1)}, u32[]{:S(2)}, u32[]{:S(2)}) %collective-permute-start.51) | collective-permute-done | bytes 1048608 | tf_op jit(solution)/shard_map/ppermute | solution.py:112
  703.3 13.7 %collective-permute-done.52 = bf16[512,1024]{1,0:T(8,128)(2,1)S(1)} collective-permute-done((bf16[512,1024]{1,0:T(8,128)(2,1)S(1)}, bf16[512,1024]{1,0:T(8,128)(2,1)S(1)}, u32[]{:S(2)}, u32[]{:S(2)}) %collective-permute-start.52) | collective-permute-done | bytes 1048608 | tf_op jit(solution)/shard_map/ppermute | solution.py:112
  720.9 15.9 %add_convert_fusion.1 = bf16[2048,2048]{1,0:T(8,128)(2,1)} fusion(f32[2048,2048]{1,0:T(8,128)} %fusion.141, bf16[2048,1024]{1,0:T(8,128)(2,1)} %copy-done.77, bf16[1024,2048]{0,1:T(8,128)(2,1)S(1)} %bitcast.625), kind=kOutput, calls=%fused_computation.21 | convolution fusion | flops 8598323200 | bytes 33554432 | tf_op jit(solution)/shard_map/dot_general | solution.py:346
  755.8 13.8 %collective-permute-done.44 = bf16[512,1024]{1,0:T(8,128)(2,1)S(1)} collective-permute-done((bf16[512,1024]{1,0:T(8,128)(2,1)S(1)}, bf16[512,1024]{1,0:T(8,128)(2,1)S(1)}, u32[]{:S(2)}, u32[]{:S(2)}) %collective-permute-start.44) | collective-permute-done | bytes 1048608 | tf_op jit(solution)/shard_map/ppermute | solution.py:112
  774.5 15.4 %collective-permute-done.53 = bf16[512,1024]{1,0:T(8,128)(2,1)S(1)} collective-permute-done((bf16[512,1024]{1,0:T(8,128)(2,1)S(1)}, bf16[512,1024]{1,0:T(8,128)(2,1)S(1)}, u32[]{:S(2)}, u32[]{:S(2)}) %collective-permute-start.53) | collective-permute-done | bytes 1048608 | tf_op jit(solution)/shard_map/ppermute | solution.py:112
  802.4 18.6 %collective-permute-done.57 = bf16[1,2,128,1024]{2,3,1,0:T(8,128)(2,1)} collective-permute-done((bf16[1,2,128,1024]{2,3,1,0:T(8,128)(2,1)}, bf16[1,2,128,1024]{2,3,1,0:T(8,128)(2,1)}, u32[]{:S(2)}, u32[]{:S(2)}) %collective-permute-start.57) | collective-permute-done | bytes 524320 | tf_op jit(solution)/shard_map/ppermute | solution.py:52
  874.7 11.4 %multiply_subtract_fusion.1 = (f32[128,8192]{0,1:T(8,128)}, f32[128,8192]{0,1:T(8,128)}, f32[128,8192]{0,1:T(8,128)}) fusion(f32[128,8192]{0,1:T(8,128)} %copy.241, f32[128,2,4,1024]{0,3,2,1:T(8,128)} %copy.267, f32[128,8192]{0,1:T(8,128)} %copy.285, f32[128,8192]{0,1:T(8,128)} %copy.286), kind=kLoop, calls=%fused_computation.59 | loop fusion | flops 15728640 | bytes 29360128 | tf_op jit(solution)/shard_map/sub | solution.py:45
  (535 shorter events, 591.6 us)
Async XLA Ops:
  8.0 854.1 %all-reduce.3.cloned.1.call-start = ((), (), s32[]{:S(2)}) async-start(), calls=%async_computation.4 | async-start | bytes 212992 | tf_op jit(solution)/shard_map/psum | solution.py:390
  11.1 41.9 %collective-permute-start = (bf16[256,2048]{1,0:T(8,128)(2,1)}, bf16[256,2048]{1,0:T(8,128)(2,1)}, u32[]{:S(2)}, u32[]{:S(2)}) collective-permute-start(bf16[256,2048]{1,0:T(8,128)(2,1)} %bitcast.583), channel_id=1, source_target_pairs={{0,2},{1,3},{2,0},{3,1},{4,6},{5,7},{6,4},{7,5},{8,10},{9,11},{10,... | collective-permute-start | bytes 3145736 | tf_op jit(solution)/shard_map/ppermute | solution.py:52
  37.4 54.7 %collective-permute-start.12 = (bf16[2,256,2048]{2,1,0:T(8,128)(2,1)}, bf16[2,256,2048]{2,1,0:T(8,128)(2,1)}, u32[]{:S(2)}, u32[]{:S(2)}) collective-permute-start(bf16[2,256,2048]{2,1,0:T(8,128)(2,1)} %pad_maximum_fusion.4), channel_id=1, source_target_pairs={{0,2},{1,3},{2,0},{3,1},{4,6},{5,7},{6,4},{7,5},{8,10},{9,11},{10,... | collective-permute-start | bytes 6291464 | tf_op jit(solution)/shard_map/ppermute | solution.py:52
  56.8 48.4 %collective-permute-start.1 = (bf16[2,256,2048]{2,1,0:T(8,128)(2,1)}, bf16[2,256,2048]{2,1,0:T(8,128)(2,1)}, u32[]{:S(2)}, u32[]{:S(2)}) collective-permute-start(bf16[2,256,2048]{2,1,0:T(8,128)(2,1)} %pad_maximum_fusion.3), channel_id=1, source_target_pairs={{0,16},{16,0},{1,17},{17,1},{2,18},{18,2},{3,19},{19,3},{4,20},{20... | collective-permute-start | bytes 6291464 | tf_op jit(solution)/shard_map/ppermute | solution.py:52
  59.4 42.2 %collective-permute-start.26 = (bf16[512,1024]{1,0:T(8,128)(2,1)S(1)}, bf16[512,1024]{1,0:T(8,128)(2,1)S(1)}, u32[]{:S(2)}, u32[]{:S(2)}) collective-permute-start(bf16[512,1024]{1,0:T(8,128)(2,1)S(1)} %bitcast.616), channel_id=1, source_target_pairs={{4,0},{8,4},{12,8},{5,1},{9,5},{13,9},{6,2},{10,6},{14,10},{7,3},{... | collective-permute-start | bytes 3145736 | tf_op jit(solution)/shard_map/ppermute | solution.py:91
  97.2 84.5 %collective-permute-start.13 = (bf16[2,2,256,2048]{3,2,1,0:T(8,128)(2,1)}, bf16[2,2,256,2048]{3,2,1,0:T(8,128)(2,1)}, u32[]{:S(2)}, u32[]{:S(2)}) collective-permute-start(bf16[2,2,256,2048]{3,2,1,0:T(8,128)(2,1)} %pad_maximum_fusion.2), channel_id=1, source_target_pairs={{0,1},{1,0},{2,3},{3,2},{4,5},{5,4},{6,7},{7,6},{8,9},{9,8},{10,11... | collective-permute-start | bytes 12582920 | tf_op jit(solution)/shard_map/ppermute | solution.py:52
  110.3 92.8 %collective-permute-start.2 = (bf16[2,2,256,2048]{3,2,1,0:T(8,128)(2,1)}, bf16[2,2,256,2048]{3,2,1,0:T(8,128)(2,1)}, u32[]{:S(2)}, u32[]{:S(2)}) collective-permute-start(bf16[2,2,256,2048]{3,2,1,0:T(8,128)(2,1)} %pad_maximum_fusion.1), channel_id=1, source_target_pairs={{0,1},{1,0},{2,3},{3,2},{4,5},{5,4},{6,7},{7,6},{8,9},{9,8},{10,11... | collective-permute-start | bytes 12582920 | tf_op jit(solution)/shard_map/ppermute | solution.py:52
  123.7 44.7 %collective-permute-start.29 = (bf16[512,1024]{1,0:T(8,128)(2,1)}, bf16[512,1024]{1,0:T(8,128)(2,1)}, u32[]{:S(2)}, u32[]{:S(2)}) collective-permute-start(bf16[512,1024]{1,0:T(8,128)(2,1)} %collective-permute-done.25), channel_id=1, source_target_pairs={{4,8},{8,12},{5,9},{9,13},{6,10},{10,14},{7,11},{11,15},{20,24},{2... | collective-permute-start | bytes 3145736 | tf_op jit(solution)/shard_map/ppermute | solution.py:90
  128.9 46.0 %collective-permute-start.28 = (bf16[512,1024]{1,0:T(8,128)(2,1)}, bf16[512,1024]{1,0:T(8,128)(2,1)}, u32[]{:S(2)}, u32[]{:S(2)}) collective-permute-start(bf16[512,1024]{1,0:T(8,128)(2,1)} %collective-permute-done.27), channel_id=1, source_target_pairs={{4,0},{5,1},{6,2},{7,3},{20,16},{21,17},{22,18},{23,19}} | collective-permute-start | bytes 3145736 | tf_op jit(solution)/shard_map/ppermute | solution.py:91
  318.7 39.9 %collective-permute-start.15 = (bf16[512,256]{1,0:T(8,128)(2,1)S(1)}, bf16[512,256]{1,0:T(8,128)(2,1)S(1)}, u32[]{:S(2)}, u32[]{:S(2)}) collective-permute-start(bf16[512,256]{1,0:T(8,128)(2,1)S(1)} %slice.84), channel_id=1, source_target_pairs={{4,0},{8,4},{12,8},{5,1},{9,5},{13,9},{6,2},{10,6},{14,10},{7,3},{... | collective-permute-start | bytes 786440 | tf_op jit(solution)/shard_map/ppermute | solution.py:91
  336.0 62.1 %collective-permute-start.62 = (bf16[1024,512]{1,0:T(8,128)(2,1)S(1)}, bf16[1024,512]{1,0:T(8,128)(2,1)S(1)}, u32[]{:S(2)}, u32[]{:S(2)}) collective-permute-start(bf16[1024,512]{1,0:T(8,128)(2,1)S(1)} %fusion.43), channel_id=1, source_target_pairs={{0,4},{4,8},{8,12},{1,5},{5,9},{9,13},{2,6},{6,10},{10,14},{3,7},{... | collective-permute-start | bytes 3145736 | tf_op jit(solution)/shard_map/ppermute | solution.py:112
  344.5 53.5 %collective-permute-start.65 = (bf16[1024,512]{1,0:T(8,128)(2,1)S(1)}, bf16[1024,512]{1,0:T(8,128)(2,1)S(1)}, u32[]{:S(2)}, u32[]{:S(2)}) collective-permute-start(bf16[1024,512]{1,0:T(8,128)(2,1)S(1)} %fusion.41), channel_id=1, source_target_pairs={{4,0},{8,4},{12,8},{5,1},{9,5},{13,9},{6,2},{10,6},{14,10},{7,3},{... | collective-permute-start | bytes 3145736 | tf_op jit(solution)/shard_map/ppermute | solution.py:113
  440.9 36.9 %collective-permute-start.10 = (bf16[512,768]{1,0:T(8,128)(2,1)}, bf16[512,768]{1,0:T(8,128)(2,1)}, u32[]{:S(2)}, u32[]{:S(2)}) collective-permute-start(bf16[512,768]{1,0:T(8,128)(2,1)} %collective-permute-done.9), channel_id=1, source_target_pairs={{8,12},{9,13},{10,14},{11,15},{24,28},{25,29},{26,30},{27,31}} | collective-permute-start | bytes 2359304 | tf_op jit(solution)/shard_map/ppermute | solution.py:90
  608.5 346.0 %reduce-scatter.5.cloned.1.call-start = ((), (), s32[]{:S(2)}) async-start(), calls=%async_computation.3 | async-start | bytes 9437184 | tf_op jit(solution)/shard_map/reduce_scatter | solution.py:362
  609.1 349.0 %reduce-scatter.3.cloned.1.call-start = ((), (), s32[]{:S(2)}) async-start(), calls=%async_computation.2 | async-start | bytes 9437184 | tf_op jit(solution)/shard_map/reduce_scatter | solution.py:349
  656.6 37.4 %collective-permute-start.42 = (bf16[512,1024]{1,0:T(8,128)(2,1)S(1)}, bf16[512,1024]{1,0:T(8,128)(2,1)S(1)}, u32[]{:S(2)}, u32[]{:S(2)}) collective-permute-start(bf16[512,1024]{1,0:T(8,128)(2,1)S(1)} %get-tuple-element.161), channel_id=1, source_target_pairs={{0,4},{1,5},{2,6},{3,7},{16,20},{17,21},{18,22},{19,23}} | collective-permute-start | bytes 3145736 | tf_op jit(solution)/shard_map/ppermute | solution.py:112
  658.0 36.0 %collective-permute-start.45 = (bf16[512,1024]{1,0:T(8,128)(2,1)S(1)}, bf16[512,1024]{1,0:T(8,128)(2,1)S(1)}, u32[]{:S(2)}, u32[]{:S(2)}) collective-permute-start(bf16[512,1024]{1,0:T(8,128)(2,1)S(1)} %get-tuple-element.162), channel_id=1, source_target_pairs={{12,8},{13,9},{14,10},{15,11},{28,24},{29,25},{30,26},{31,27}} | collective-permute-start | bytes 3145736 | tf_op jit(solution)/shard_map/ppermute | solution.py:113
  658.7 44.6 %collective-permute-start.54 = (bf16[512,1024]{1,0:T(8,128)(2,1)S(1)}, bf16[512,1024]{1,0:T(8,128)(2,1)S(1)}, u32[]{:S(2)}, u32[]{:S(2)}) collective-permute-start(bf16[512,1024]{1,0:T(8,128)(2,1)S(1)} %get-tuple-element.156), channel_id=1, source_target_pairs={{12,8},{13,9},{14,10},{15,11},{28,24},{29,25},{30,26},{31,27}} | collective-permute-start | bytes 3145736 | tf_op jit(solution)/shard_map/ppermute | solution.py:113
  671.3 45.7 %collective-permute-start.52 = (bf16[512,1024]{1,0:T(8,128)(2,1)S(1)}, bf16[512,1024]{1,0:T(8,128)(2,1)S(1)}, u32[]{:S(2)}, u32[]{:S(2)}) collective-permute-start(bf16[512,1024]{1,0:T(8,128)(2,1)S(1)} %fusion.48), channel_id=1, source_target_pairs={{0,4},{4,8},{1,5},{5,9},{2,6},{6,10},{3,7},{7,11},{16,20},{20,24},... | collective-permute-start | bytes 3145736 | tf_op jit(solution)/shard_map/ppermute | solution.py:112
  696.0 43.0 %collective-permute-start.43 = (bf16[512,1024]{1,0:T(8,128)(2,1)}, bf16[512,1024]{1,0:T(8,128)(2,1)}, u32[]{:S(2)}, u32[]{:S(2)}) collective-permute-start(bf16[512,1024]{1,0:T(8,128)(2,1)} %get-tuple-element.159), channel_id=1, source_target_pairs={{0,4},{4,8},{1,5},{5,9},{2,6},{6,10},{3,7},{7,11},{16,20},{20,24},... | collective-permute-start | bytes 3145736 | tf_op jit(solution)/shard_map/ppermute | solution.py:112
  701.6 37.3 %collective-permute-start.46 = (bf16[512,1024]{1,0:T(8,128)(2,1)}, bf16[512,1024]{1,0:T(8,128)(2,1)}, u32[]{:S(2)}, u32[]{:S(2)}) collective-permute-start(bf16[512,1024]{1,0:T(8,128)(2,1)} %get-tuple-element.160), channel_id=1, source_target_pairs={{8,4},{12,8},{9,5},{13,9},{10,6},{14,10},{11,7},{15,11},{24,20},{2... | collective-permute-start | bytes 3145736 | tf_op jit(solution)/shard_map/ppermute | solution.py:113
  747.3 42.6 %collective-permute-start.53 = (bf16[512,1024]{1,0:T(8,128)(2,1)S(1)}, bf16[512,1024]{1,0:T(8,128)(2,1)S(1)}, u32[]{:S(2)}, u32[]{:S(2)}) collective-permute-start(bf16[512,1024]{1,0:T(8,128)(2,1)S(1)} %copy-done.58), channel_id=1, source_target_pairs={{0,4},{4,8},{8,12},{1,5},{5,9},{9,13},{2,6},{6,10},{10,14},{3,7},{... | collective-permute-start | bytes 3145736 | tf_op jit(solution)/shard_map/ppermute | solution.py:112
  754.3 39.8 %collective-permute-start.56 = (bf16[512,1024]{1,0:T(8,128)(2,1)S(1)}, bf16[512,1024]{1,0:T(8,128)(2,1)S(1)}, u32[]{:S(2)}, u32[]{:S(2)}) collective-permute-start(bf16[512,1024]{1,0:T(8,128)(2,1)S(1)} %fusion.47), channel_id=1, source_target_pairs={{4,0},{8,4},{12,8},{5,1},{9,5},{13,9},{6,2},{10,6},{14,10},{7,3},{... | collective-permute-start | bytes 3145736 | tf_op jit(solution)/shard_map/ppermute | solution.py:113
  865.1 43.4 %collective-permute-start.50 = (bf16[4,128,1024]{2,1,0:T(8,128)(2,1)S(1)}, bf16[4,128,1024]{2,1,0:T(8,128)(2,1)S(1)}, u32[]{:S(2)}, u32[]{:S(2)}) collective-permute-start(bf16[4,128,1024]{2,1,0:T(8,128)(2,1)S(1)} %bitcast.614), channel_id=1, source_target_pairs={{0,16},{16,0},{1,17},{17,1},{2,18},{18,2},{3,19},{19,3},{4,20},{20... | collective-permute-start | bytes 3145736 | tf_op jit(solution)/shard_map/ppermute | solution.py:52
  (133 other events, 2216.0 us)
Sparse Core Ops, SparseCore 0:
  608.6 136.7 all-reduce.2
Sparse Core Ops, SparseCore 1:
  612.5 78.8 reduce-scatter.4
  736.9 82.7 reduce-scatter.2

commit v2 on v1

v2 whole, which is shorter than its diff:
```python
import functools
import math

import jax
import jax.numpy as jnp
from jax import lax
from jax.experimental import pallas as pl
from jax.experimental.pallas import tpu as pltpu
from jax.sharding import PartitionSpec as P

D = 2048
HEADS = 8
HEAD_DIM = 256
FF = 8192
ROT = 64
ADAM_STEP = 4

BETA_ONE = 0.9
BETA_TWO = 0.95
LEARN_RATE = 0.5
EPSILON = 1e-08
WEIGHT_DECAY = 0.1
NORM_EPSILON = 1e-05
MASKED = -1e30
N_DP = 2
N_SEQ = 4
PARTS = N_DP * N_SEQ
HEAD_W = D // PARTS
HID_W = FF // PARTS
BF = jnp.bfloat16
F32 = jnp.float32
NT = (((1,), (1,)), ((), ()))
TN = (((0,), (0,)), ((), ()))


def rotary_tables(positions):
    half_rot = ROT // 2
    exponent = jnp.arange(half_rot, dtype=F32) * (2.0 / ROT)
    inverse = jnp.power(10000.0, -exponent)
    angles = positions[:, None] * inverse[None, :]
    angles = jnp.concatenate([angles, angles], axis=1)
    return (jnp.cos(angles), jnp.sin(angles))


def adam_step(parameter, gradient, first_moment, second, decay_rate):
    first_new = BETA_ONE * first_moment + (1.0 - BETA_ONE) * gradient
    second_new = BETA_TWO * second + (1.0 - BETA_TWO) * gradient * gradient
    first_hat = first_new / (1.0 - BETA_ONE**ADAM_STEP)
    second_hat = second_new / (1.0 - BETA_TWO**ADAM_STEP)
    param_new = parameter - LEARN_RATE * (
        first_hat / (jnp.sqrt(second_hat) + EPSILON) + decay_rate * parameter
    )
    return (param_new, first_new, second_new)


class Wire:
    def __init__(self, send_sems, recv_sems):
        self.send_sems, self.recv_sems, self.used = send_sems, recv_sems, 0
        self.sent = []

    def slot(self):
        self.used += 1
        return self.used - 1

    def copy(self, slot, source, target, device):
        return pltpu.make_async_remote_copy(
            src_ref=source,
            dst_ref=target,
            send_sem=self.send_sems.at[slot],
            recv_sem=self.recv_sems.at[slot],
            device_id=device,
            device_id_type=pl.DeviceIdType.MESH,
        )

    def send(self, slot, source, target, device, when=None):
        copy = self.copy(slot, source, target, device)
        guarded(when, copy.start)
        self.sent.append((copy, when))

    def receive(self, slot, target, device, when=None):
        copy = self.copy(slot, target, target, device)
        guarded(when, copy.wait_recv)

    def finish(self):
        for copy, when in self.sent:
            guarded(when, copy.wait_send)
        self.sent = []


def guarded(when, action):
    if when is None:
        action()
    else:
        pl.when(when)(action)


class Place:
    def __init__(self, n_zero):
        self.n = n_zero
        self.dp, self.z, self.s = (lax.axis_index(a) for a in ("dp", "zero", "seq"))
        flip = lambda value, bit: jnp.bitwise_xor(value, bit)
        self.dp_far, self.s_far, self.s_core = 1 - self.dp, flip(self.s, 2), flip(self.s, 1)
        self.s_both = flip(self.s, 3)
        self.across = {"dp": self.dp_far}
        self.far = {"seq": self.s_far}
        self.core = {"seq": self.s_core}
        self.above, self.below = {"zero": self.z + 1}, {"zero": self.z - 1}
        self.part = self.dp * N_SEQ + self.s

    def others(self):
        for step in range(1, N_DP * N_SEQ):
            at = lax.rem(self.part + step, N_DP * N_SEQ)
            dp, s = lax.div(at, N_SEQ), lax.rem(at, N_SEQ)
            yield step, dp, s, {"dp": dp, "seq": s}

    def barrier(self):
        gate = pltpu.get_barrier_semaphore()
        signal = lambda device: pl.semaphore_signal(
            gate, inc=1, device_id=device, device_id_type=pl.DeviceIdType.MESH
        )
        for _, _, _, device in self.others():
            signal(device)
        pl.when(self.z < self.n - 1)(lambda: signal(self.above))
        pl.when(self.z > 0)(lambda: signal(self.below))
        ends = (self.z < self.n - 1).astype(jnp.int32) + (self.z > 0).astype(jnp.int32)
        pl.semaphore_wait(gate, N_DP * N_SEQ - 1 + ends)


class LineGather:
    def __init__(self, wire, place, whole, rows):
        self.wire, self.place, self.whole, self.rows = wire, place, whole, rows
        self.ups = [wire.slot() for _ in range(place.n - 1)]
        self.downs = [wire.slot() for _ in range(place.n - 1)]

    def block(self, index):
        return self.whole.at[pl.ds(pl.multiple_of(index * self.rows, self.rows), self.rows)]

    def take(self, step):
        p = self.place
        self.wire.receive(self.ups[step - 1], self.block(jnp.maximum(p.z - step, 0)), p.below, p.z >= step)
        self.wire.receive(
            self.downs[step - 1], self.block(jnp.minimum(p.z + step, p.n - 1)), p.above, p.z + step < p.n
        )

    def pass_on(self, step):
        p = self.place
        up, down = jnp.maximum(p.z - step + 1, 0), jnp.minimum(p.z + step - 1, p.n - 1)
        self.wire.send(
            self.ups[step - 1], self.block(up), self.block(up), p.above, (p.z < p.n - 1) & (p.z >= step - 1)
        )
        self.wire.send(
            self.downs[step - 1], self.block(down), self.block(down), p.below, (p.z > 0) & (p.z + step <= p.n)
        )


class SeqExchange:
    def __init__(self, wire, place, send, whole, rows):
        self.wire, self.place, self.out, self.whole, self.rows = wire, place, send, whole, rows
        self.slots = [wire.slot() for _ in range(1, N_SEQ)]

    def target(self, s):
        row = (self.place.z * N_SEQ + s) * self.rows
        return self.whole.at[pl.ds(pl.multiple_of(row, self.rows), self.rows)]

    def start(self, local_sem):
        p = self.place
        for step in range(1, N_SEQ):
            to = lax.rem(p.s + step, N_SEQ)
            self.wire.send(self.slots[step - 1], self.out.at[to], self.target(p.s), {"seq": to})
        own = pltpu.make_async_copy(self.out.at[p.s], self.target(p.s), local_sem)
        own.start()
        self.own = own

    def wait(self):
        p = self.place
        for step in range(1, N_SEQ):
            source = lax.rem(p.s - step + N_SEQ, N_SEQ)
            self.wire.receive(self.slots[step - 1], self.target(source), {"seq": source})
        self.own.wait()


class PlaneGather:
    def __init__(self, wire, place, block, whole):
        self.wire, self.place, self.own, self.whole = wire, place, block, whole
        self.slots = {name: wire.slot() for name in ("far", "across", "both0", "both1", "c0", "c1", "c2", "c3")}
        self.half = block.shape[0] // 2

    def start(self, local_sem):
        p, w, slots = self.place, self.wire, self.slots
        mine = self.whole.at[p.dp, p.s]
        w.send(slots["far"], self.own, mine, p.far)
        w.send(slots["across"], self.own, mine, p.across)
        w.send(slots["c0"], self.own, mine, p.core)
        self.copied = pltpu.make_async_copy(self.own, mine, local_sem)
        self.copied.start()

    def turn(self):
        p, w, slots, h = self.place, self.wire, self.slots, self.half
        far, across = self.whole.at[p.dp, p.s_far], self.whole.at[p.dp_far, p.s]
        w.receive(slots["far"], far, p.far)
        w.send(slots["both0"], far.at[pl.ds(0, h)], far.at[pl.ds(0, h)], p.across)
        w.send(slots["c1"], far, far, p.core)
        w.receive(slots["across"], across, p.across)
        w.send(slots["both1"], across.at[pl.ds(h, h)], across.at[pl.ds(h, h)], p.far)
        w.send(slots["c2"], across, across, p.core)

    def turn_again(self):
        p, w, slots, h = self.place, self.wire, self.slots, self.half
        both = self.whole.at[p.dp_far, p.s_far]
        w.receive(slots["both0"], both.at[pl.ds(0, h)], p.across)
        w.receive(slots["both1"], both.at[pl.ds(h, h)], p.far)
        w.send(slots["c3"], both, both, p.core)

    def wait(self):
        p, w, slots = self.place, self.wire, self.slots
        w.receive(slots["c0"], self.whole.at[p.dp, p.s_core], p.core)
        w.receive(slots["c1"], self.whole.at[p.dp, p.s_both], p.core)
        w.receive(slots["c2"], self.whole.at[p.dp_far, p.s_core], p.core)
        w.receive(slots["c3"], self.whole.at[p.dp_far, p.s_both], p.core)
        self.copied.wait()


def add_rows(target, *sources):
    rows = target.shape[0]
    tile = 32 if rows % 32 == 0 else 16

    def one(i, carry):
        at = pl.ds(pl.multiple_of(i * tile, tile), tile)
        total = sources[0][at, :].astype(F32)
        for source in sources[1:]:
            total = total + source[at, :].astype(F32)
        target[at, :] = total.astype(target.dtype)
        return carry

    lax.fori_loop(0, rows // tile, one, 0)


class LineScatter:
    def __init__(self, wire, place, parts, ups, downs, total, own, rows, sem):
        self.wire, self.place, self.parts, self.rows = wire, place, parts, rows
        self.ups, self.downs, self.total, self.own, self.sem = ups, downs, total, own, sem
        self.up_slots = [wire.slot() for _ in range(place.n)]
        self.down_slots = [wire.slot() for _ in range(place.n)]

    def part(self, j):
        return self.parts.at[pl.ds(pl.multiple_of(j * self.rows, self.rows), self.rows)]

    def fetch(self, j, target):
        copy = pltpu.make_async_copy(self.part(j), target, self.sem)
        copy.start()
        copy.wait()

    def step(self, k):
        p = self.place
        j = p.n - 1 - k
        self.hop(j, self.ups, self.up_slots[j], p.above, p.below, p.z < j, p.z == 0)
        j = k
        self.hop(j, self.downs, self.down_slots[j], p.below, p.above, p.z > j, p.z == p.n - 1)

    def hop(self, j, held, slot, onto, source, active, first):
        def go():
            pl.when(first)(lambda: self.fetch(j, held.at[j]))

            @pl.when(jnp.logical_not(first))
            def _():
                self.fetch(j, self.own)
                self.wire.receive(slot, held.at[j], source)
                add_rows(held.at[j], held.at[j], self.own)

        pl.when(active)(go)
        self.wire.send(slot, held.at[j], held.at[j], onto, active)

    def last(self):
        p = self.place
        self.fetch(p.z, self.own)
        up, down = self.ups.at[p.z], self.downs.at[p.z]

        @pl.when(p.z == 0)
        def _():
            self.arrive(self.downs, self.down_slots, p.above)
            add_rows(self.total, self.own, down)

        @pl.when(p.z == p.n - 1)
        def _():
            self.arrive(self.ups, self.up_slots, p.below)
            add_rows(self.total, self.own, up)

        @pl.when((p.z > 0) & (p.z < p.n - 1))
        def _():
            self.arrive(self.ups, self.up_slots, p.below)
            self.arrive(self.downs, self.down_slots, p.above)
            add_rows(self.total, self.own, up, down)

    def arrive(self, held, slots, source):
        self.wire.receive(slots[0] + self.place.z, held.at[self.place.z], source)


class Home:
    def __init__(self, wire, place, total, home, rows):
        self.wire, self.place, self.total, self.home, self.rows = wire, place, total, home, rows
        self.slots = [wire.slot() for _ in range(1, N_DP * N_SEQ)]

    def start(self, local_sem):
        p = self.place
        piece = lambda s: self.total.at[pl.ds(pl.multiple_of(s * self.rows, self.rows), self.rows)]
        for step, dp, s, device in p.others():
            self.wire.send(self.slots[step - 1], piece(s), self.home.at[p.dp, p.s], device)
        self.copied = pltpu.make_async_copy(piece(p.s), self.home.at[p.dp, p.s], local_sem)
        self.copied.start()

    def wait(self):
        p = self.place
        parts = N_DP * N_SEQ
        for step in range(1, parts):
            at = lax.rem(p.part - step + parts, parts)
            dp, s = lax.div(at, N_SEQ), lax.rem(at, N_SEQ)
            self.wire.receive(self.slots[step - 1], self.home.at[dp, s], {"dp": dp, "seq": s})
        self.copied.wait()


class DenseExchange:
    def __init__(self, wire, place, source, target):
        self.wire, self.place, self.source, self.target = wire, place, source, target
        self.slots = [wire.slot() for _ in range(1, N_DP * N_SEQ)]

    def start(self, local_sem):
        p = self.place
        for step, dp, s, device in p.others():
            self.wire.send(self.slots[step - 1], self.source(dp * N_SEQ + s), self.target(p.part), device)
        self.copied = pltpu.make_async_copy(self.source(p.part), self.target(p.part), local_sem)
        self.copied.start()

    def wait(self):
        p = self.place
        parts = N_DP * N_SEQ
        for step in range(1, parts):
            at = lax.rem(p.part - step + parts, parts)
            device = {"dp": lax.div(at, N_SEQ), "seq": lax.rem(at, N_SEQ)}
            self.wire.receive(self.slots[step - 1], self.target(at), device)
        self.copied.wait()


class PlaneScatter:
    def __init__(self, wire, place, parts, mate, from_far, from_across, turned, total, own, sem):
        self.wire, self.place, self.parts, self.mate, self.sums = wire, place, parts, mate, mate
        self.from_far, self.from_across, self.turned = from_far, from_across, turned
        self.total, self.own, self.sem = total, own, sem
        self.half = total.shape[0] // 2
        self.core_slots = [[wire.slot() for _ in range(2)] for _ in range(2)]
        names = ("turn_across", "turn_far", "far0", "far1", "across0", "across1")
        self.slots = {name: wire.slot() for name in names}

    def start(self):
        p = self.place
        core = lax.rem(p.s_core, 2)
        for dp in range(2):
            for y in range(2):
                self.wire.send(
                    self.core_slots[dp][y], self.parts.at[dp, 2 * y + core], self.mate.at[dp, y], p.core
                )

    def combine(self, dp, y):
        p = self.place
        core = lax.rem(p.s, 2)
        for d in range(2):
            for v in range(2):

                @pl.when((dp == d) & (y == v))
                def _(d=d, v=v):
                    copy = pltpu.make_async_copy(self.parts.at[d, 2 * v + core], self.own, self.sem)
                    copy.start()
                    self.wire.receive(self.core_slots[d][v], self.mate.at[d, v], p.core)
                    copy.wait()
                    add_rows(self.sums.at[d, v], self.own, self.mate.at[d, v])

    def turn(self):
        p, w, h, slots = self.place, self.wire, self.half, self.slots
        y = lax.div(p.s, 2)
        y_far = 1 - y
        low, high = pl.ds(0, h), pl.ds(h, h)
        self.combine(p.dp_far, y_far)
        both = self.sums.at[p.dp_far, y_far]
        w.send(slots["turn_across"], both.at[low], self.turned.at[low], p.across)
        w.send(slots["turn_far"], both.at[high], self.turned.at[high], p.far)
        self.combine(p.dp, y_far)
        far = self.sums.at[p.dp, y_far]
        w.send(slots["far1"], far.at[high], self.from_far.at[high], p.far)
        self.combine(p.dp_far, y)
        across = self.sums.at[p.dp_far, y]
        w.send(slots["across0"], across.at[low], self.from_across.at[low], p.across)
        self.combine(p.dp, y)

    def turn_again(self):
        p, w, h, slots = self.place, self.wire, self.half, self.slots
        y = lax.div(p.s, 2)
        low, high = pl.ds(0, h), pl.ds(h, h)
        far, across = self.sums.at[p.dp, 1 - y], self.sums.at[p.dp_far, y]
        w.receive(slots["turn_across"], self.turned.at[low], p.across)
        add_rows(far.at[low], far.at[low], self.turned.at[low])
        w.send(slots["far0"], far.at[low], self.from_far.at[low], p.far)
        w.receive(slots["turn_far"], self.turned.at[high], p.far)
        add_rows(across.at[high], across.at[high], self.turned.at[high])
        w.send(slots["across1"], across.at[high], self.from_across.at[high], p.across)

    def last(self):
        p, w, h, slots = self.place, self.wire, self.half, self.slots
        low, high = pl.ds(0, h), pl.ds(h, h)
        w.receive(slots["far1"], self.from_far.at[high], p.far)
        w.receive(slots["far0"], self.from_far.at[low], p.far)
        w.receive(slots["across0"], self.from_across.at[low], p.across)
        w.receive(slots["across1"], self.from_across.at[high], p.across)
        add_rows(self.total, self.sums.at[p.dp, lax.div(p.s, 2)], self.from_far, self.from_across)


def attention_body(scale, projected, cos_ref, sin_ref, d_att_ref, att_ref, d_proj_ref, keys_acc, values_acc):
    length = projected.shape[1]
    tile = min(256, length)
    half = ROT // 2
    cosine = cos_ref[...]
    sine = sin_ref[...]

    def turn(block):
        first = block[:, :128]
        rolled = jnp.concatenate([first[:, half:ROT], first[:, :half], first[:, ROT:]], axis=1)
        return jnp.concatenate([first * cosine + rolled * sine, block[:, 128:]], axis=1)

    def turn_back(block):
        first = block[:, :128]
        scaled = first * sine
        rolled = jnp.concatenate([scaled[:, half:ROT], scaled[:, :half], scaled[:, ROT:]], axis=1)
        return jnp.concatenate([first * cosine + rolled, block[:, 128:]], axis=1)

    queries = turn(projected[0, :, 0:HEAD_DIM]).astype(BF)
    keys = turn(projected[0, :, HEAD_DIM : 2 * HEAD_DIM]).astype(BF)
    values = projected[0, :, 2 * HEAD_DIM :].astype(BF)
    d_att_all = d_att_ref[0]
    keys_acc[...] = jnp.zeros_like(keys_acc)
    values_acc[...] = jnp.zeros_like(values_acc)
    d_queries = []
    for at in range(length // tile):
        rows = slice(at * tile, (at + 1) * tile)
        seen = (at + 1) * tile
        q = queries[rows]
        d_att = d_att_all[rows]
        k, v = keys[:seen], values[:seen]
        scores = lax.dot_general(q, k, NT, preferred_element_type=F32) * scale
        row = lax.broadcasted_iota(jnp.int32, scores.shape, 0) + at * tile
        column = lax.broadcasted_iota(jnp.int32, scores.shape, 1)
        scores = jnp.where(row >= column, scores, MASKED)
        top = jnp.max(scores, axis=1, keepdims=True)
        grown = jnp.exp(scores - top)
        prob = grown * (1.0 / jnp.sum(grown, axis=1, keepdims=True))
        prob_low = prob.astype(BF)
        att_ref[0, rows, :] = jnp.dot(prob_low, v, preferred_element_type=F32).astype(BF)
        d_prob = lax.dot_general(d_att, v, NT, preferred_element_type=F32)
        inner = jnp.sum(d_prob * prob, axis=1, keepdims=True)
        d_scores = (prob * (d_prob - inner)).astype(BF)
        d_queries.append(jnp.dot(d_scores, k, preferred_element_type=F32) * scale)
        keys_acc[:seen, :] += lax.dot_general(d_scores, q, TN, preferred_element_type=F32)
        values_acc[:seen, :] += lax.dot_general(prob_low, d_att, TN, preferred_element_type=F32)
    d_proj_ref[0, :, 0:HEAD_DIM] = turn_back(jnp.concatenate(d_queries, axis=0)).astype(BF)
    d_proj_ref[0, :, HEAD_DIM : 2 * HEAD_DIM] = turn_back(keys_acc[...] * scale).astype(BF)
    d_proj_ref[0, :, 2 * HEAD_DIM :] = values_acc[...].astype(BF)


def attention(projected, d_att):
    seqs, length, _ = projected.shape
    cosine, sine = rotary_tables(jnp.arange(length).astype(F32))
    half = ROT // 2
    sine_turn = jnp.concatenate([-sine[:, :half], sine[:, half:]], axis=1)
    cosine = jnp.concatenate([cosine, jnp.ones((length, 128 - ROT), F32)], axis=1)
    sine_turn = jnp.concatenate([sine_turn, jnp.zeros((length, 128 - ROT), F32)], axis=1)
    whole = pl.BlockSpec((length, 128), lambda s: (0, 0))
    one = lambda width: pl.BlockSpec((1, length, width), lambda s: (s, 0, 0))
    return pl.pallas_call(
        functools.partial(attention_body, 1.0 / math.sqrt(HEAD_DIM)),
        grid=(seqs,),
        in_specs=[one(3 * HEAD_DIM), whole, whole, one(HEAD_DIM)],
        out_specs=[one(HEAD_DIM), one(3 * HEAD_DIM)],
        out_shape=[
            jax.ShapeDtypeStruct((seqs, length, HEAD_DIM), BF),
            jax.ShapeDtypeStruct((seqs, length, 3 * HEAD_DIM), BF),
        ],
        scratch_shapes=[pltpu.VMEM((length, HEAD_DIM), F32), pltpu.VMEM((length, HEAD_DIM), F32)],
        compiler_params=pltpu.CompilerParams(vmem_limit_bytes=48 * 1024 * 1024),
        cost_estimate=pl.CostEstimate(
            flops=seqs * length * length * HEAD_DIM * 9,
            bytes_accessed=seqs * length * HEAD_DIM * 22,
            transcendentals=seqs * length * length,
        ),
        name="attention",
    )(projected, cosine, sine_turn, d_att)


def gelu_parts(values):
    phi_wide = 0.5 * (1.0 + lax.erf(values * (1.0 / math.sqrt(2.0))))
    density = jnp.exp(-0.5 * values * values) * (1.0 / math.sqrt(2.0 * math.pi))
    return values * phi_wide, phi_wide + values * density


def any_spec(count):
    return [pl.BlockSpec(memory_space=pl.ANY)] * count


def slots_needed(n_zero):
    return 8 * n_zero + 96


def gather_body(
    n_zero,
    rows,
    x_ref,
    g_ref,
    dn_ref,
    qk_ref,
    up_ref,
    wt_ref,
    x_all,
    g_all,
    dn_all,
    dense_own,
    qk_all,
    up_all,
    wt_all,
    send_sems,
    recv_sems,
    local_sems,
):
    place = Place(n_zero)
    wire = Wire(send_sems, recv_sems)
    block = rows * N_SEQ
    pairs = ((dn_ref, dn_all), (qk_ref, qk_all), (up_ref, up_all), (wt_ref, wt_all))
    exchanges = [SeqExchange(wire, place, send, whole, rows) for send, whole in pairs]
    dn, qk, up, wt = [LineGather(wire, place, whole, block) for _, whole in pairs]
    x = PlaneGather(wire, place, x_ref, x_all)
    g = PlaneGather(wire, place, g_ref, g_all)
    dense = DenseExchange(
        wire,
        place,
        lambda c: dn_all.at[pl.ds(pl.multiple_of(c * HEAD_W, HEAD_W), HEAD_W)],
        lambda c: dense_own.at[:, pl.ds(pl.multiple_of(c * HEAD_W, HEAD_W), HEAD_W)],
    )
    place.barrier()
    for k, exchange in enumerate(exchanges):
        exchange.start(local_sems.at[k])
        if k == 1:
            x.start(local_sems.at[4])
            g.start(local_sems.at[5])
    exchanges[0].wait()
    dn.pass_on(1)
    exchanges[1].wait()
    qk.pass_on(1)
    exchanges[2].wait()
    up.pass_on(1)
    exchanges[3].wait()
    x.turn()
    g.turn()
    for line in (dn, qk, up, wt):
        for k in range(2, n_zero):
            line.take(k - 1)
            line.pass_on(k)
        line.take(n_zero - 1)
        if line is dn:
            dense.start(local_sems.at[6])
            x.turn_again()
            g.turn_again()
        if line is qk:
            wt.pass_on(1)
            x.wait()
            g.wait()
            dense.wait()
    wire.finish()


def gather(n_zero, rows, x, g, dn, qk, up, wt):
    shape = lambda *dims: jax.ShapeDtypeStruct(dims, BF)
    slots = slots_needed(n_zero)
    return pl.pallas_call(
        functools.partial(gather_body, n_zero, rows),
        in_specs=any_spec(6),
        out_specs=any_spec(7),
        out_shape=[
            shape(N_DP, N_SEQ, *x.shape),
            shape(N_DP, N_SEQ, *g.shape),
            shape(D, HEAD_W),
            shape(HEAD_W, D),
            shape(D, 3 * HEAD_W),
            shape(D, HID_W),
            shape(D, HID_W),
        ],
        scratch_shapes=[
            pltpu.SemaphoreType.DMA((slots,)),
            pltpu.SemaphoreType.DMA((slots,)),
            pltpu.SemaphoreType.DMA((8,)),
        ],
        compiler_params=pltpu.CompilerParams(collective_id=0, has_side_effects=True),
        name="gather",
    )(x, g, dn, qk, up, wt)


def scatter_body(n_zero, rows, *refs):
    out_parts, tok_parts, dn_part, qk_part, up_part, wt_part = refs[:6]
    out_sum, tok_sum, dn_home, qk_home, up_home, wt_home, dn_cols = refs[6:13]
    send_sems, recv_sems, local_sems = refs[13:16]
    scratch = list(refs[16:])
    take = lambda count: [scratch.pop(0) for _ in range(count)]
    place = Place(n_zero)
    wire = Wire(send_sems, recv_sems)
    block = rows * N_SEQ
    plane = []
    for k, (parts, result) in enumerate(((out_parts, out_sum), (tok_parts, tok_sum))):
        mate, far, across, turned, total, own = take(6)
        sem = local_sems.at[k]
        plane.append((PlaneScatter(wire, place, parts, mate, far, across, turned, total, own, sem), result))
    lines = []
    pairs = ((dn_cols, dn_home), (qk_part, qk_home), (up_part, up_home), (wt_part, wt_home))
    for k, (parts, home) in enumerate(pairs):
        ups, downs, total, own = take(4)
        line = LineScatter(wire, place, parts, ups, downs, total, own, block, local_sems.at[2 + k])
        lines.append((line, Home(wire, place, total, home, rows), k))
    dense = DenseExchange(
        wire,
        place,
        lambda c: dn_part.at[:, pl.ds(pl.multiple_of(c * HEAD_W, HEAD_W), HEAD_W)],
        lambda c: dn_cols.at[pl.ds(pl.multiple_of(c * HEAD_W, HEAD_W), HEAD_W)],
    )
    place.barrier()
    dense.start(local_sems.at[6])
    for scatter, _ in plane:
        scatter.start()
    dn, qk, up, wt = lines
    todo = [(line, k) for line in (wt, up, qk, dn) for k in range(n_zero - 1)]
    for index, (line, k) in enumerate(todo):
        if index == 2:
            for scatter, _ in plane:
                scatter.turn()
        if index == 4:
            for scatter, _ in plane:
                scatter.turn_again()
        if line is dn and k == 0:
            dense.wait()
        line[0].step(k)
        if k == n_zero - 2:
            line[0].last()
            line[1].start(local_sems.at[7 + line[2]])
    for scatter, result in plane:
        scatter.last()
        copy = pltpu.make_async_copy(scatter.total, result, scatter.sem)
        copy.start()
        copy.wait()
    for _, home, _ in lines:
        home.wait()
    wire.finish()


def scatter(n_zero, rows, out_parts, tok_parts, dn_part, qk_part, up_part, wt_part):
    tokens = out_parts.shape[2]
    block = rows * N_SEQ
    slots = slots_needed(n_zero)
    vmem = lambda *dims: pltpu.VMEM(dims, BF)
    widths = (HEAD_W, 3 * HEAD_W, HID_W, HID_W)
    scratch = []
    for _ in range(2):
        scratch += [vmem(2, 2, tokens, D), vmem(tokens, D), vmem(tokens, D), vmem(tokens, D)]
        scratch += [pltpu.VMEM((tokens, D), F32), vmem(tokens, D)]
    for width in widths:
        scratch += [vmem(n_zero, block, width), vmem(n_zero, block, width)]
        scratch += [vmem(block, width), vmem(block, width)]
    return pl.pallas_call(
        functools.partial(scatter_body, n_zero, rows),
        in_specs=any_spec(6),
        out_specs=any_spec(7),
        out_shape=[jax.ShapeDtypeStruct((tokens, D), F32)] * 2
        + [jax.ShapeDtypeStruct((N_DP, N_SEQ, rows, width), BF) for width in widths]
        + [jax.ShapeDtypeStruct((D, HEAD_W), BF)],
        scratch_shapes=[
            pltpu.SemaphoreType.DMA((slots,)),
            pltpu.SemaphoreType.DMA((slots,)),
            pltpu.SemaphoreType.DMA((12,)),
        ]
        + scratch,
        compiler_params=pltpu.CompilerParams(
            collective_id=1, has_side_effects=True, vmem_limit_bytes=60 * 1024 * 1024
        ),
        name="scatter",
    )(out_parts, tok_parts, dn_part, qk_part, up_part, wt_part)


def adam_body(decay, flipped, home, param, first, second, new, first_new, second_new, grad_out):
    gradient = home[0, 0].astype(F32)
    if flipped:
        gradient = gradient.T
    updated = adam_step(param[...], gradient, first[...], second[...], decay)
    new[...], first_new[...], second_new[...] = updated
    grad_out[...] = gradient


def adam(home, pieces, param, first, second, flipped=False):
    rows, width = home.shape[2], home.shape[3] // pieces
    if flipped:
        block = pl.BlockSpec((width, rows), lambda c, t: (t * PARTS + c, 0))
    else:
        block = pl.BlockSpec((rows, width), lambda c, t: (0, t * PARTS + c))
    return pl.pallas_call(
        functools.partial(adam_body, WEIGHT_DECAY, flipped),
        grid=(PARTS, pieces),
        in_specs=[
            pl.BlockSpec((1, 1, rows, width), lambda c, t: (c // N_SEQ, c % N_SEQ, 0, t)),
            block,
            block,
            block,
        ],
        out_specs=[block] * 4,
        out_shape=[jax.ShapeDtypeStruct(param.shape, F32)] * 4,
        compiler_params=pltpu.CompilerParams(vmem_limit_bytes=48 * 1024 * 1024),
        name="adam",
    )(home, param, first, second)


def make_body(sizes):
    n_zero = sizes["zero"]
    everywhere = ("dp", "zero", "seq")

    def body(
        inputs,
        out_grad,
        vectors,
        qkv_weight,
        dense_weight,
        up_weight,
        down_weight,
        vectors_first,
        qkv_first,
        dense_first,
        up_first,
        down_first,
        vectors_second,
        qkv_second,
        dense_second,
        up_second,
        down_second,
    ):
        dp_i, zero_i, seq_i = (lax.axis_index(axis) for axis in everywhere)
        part_i = dp_i * N_SEQ + seq_i
        seqs_here, local_len = inputs.shape[0], inputs.shape[1]
        token_rows = seqs_here * local_len
        rows = qkv_weight.shape[0]
        pick = lambda value, index, axis: lax.dynamic_index_in_dim(value, index, axis, keepdims=False)

        vec_all = lax.all_gather(vectors.astype(BF), ("zero", "seq"), axis=0, tiled=True).astype(F32)
        ln1_gain, ln1_bias = vec_all[:D], vec_all[D : 2 * D]
        qkv_bias = vec_all[2 * D : 5 * D].reshape(3, PARTS, HEAD_W)
        dense_bias = vec_all[5 * D : 6 * D]
        ln2_gain, ln2_bias = vec_all[6 * D : 7 * D], vec_all[7 * D : 8 * D]
        up_bias = vec_all[8 * D : 8 * D + FF].reshape(PARTS, HID_W)
        down_bias = vec_all[8 * D + FF :]

        def columns(value, width):
            wide = value.shape[1] // N_DP
            half = lax.dynamic_slice_in_dim(value, dp_i * wide, wide, 1).astype(BF)
            return half.reshape(rows, N_SEQ, width).transpose(1, 0, 2)

        qk_low = jnp.concatenate(
            [columns(qkv_weight[:, t * D : (t + 1) * D], HEAD_W) for t in range(3)], axis=2
        )
        dn_low = columns(dense_weight, HEAD_W)
        up_low = columns(up_weight, HID_W)
        wt_low = lax.dynamic_slice_in_dim(down_weight, dp_i * (FF // N_DP), FF // N_DP, 0).astype(BF)
        wt_low = wt_low.reshape(N_SEQ, HID_W, rows).transpose(0, 2, 1)

        tokens_low = inputs.reshape(token_rows, D)
        grad_low = out_grad.reshape(token_rows, D)
        tokens_all, grad_all, _, dense_own, qkv_own, up_own, wt_own = gather(
            n_zero, rows, tokens_low, grad_low, dn_low, qk_low, up_low, wt_low
        )
        seqs = N_DP * seqs_here
        length = N_SEQ * local_len
        order = lambda value: value.reshape(N_DP, N_SEQ, seqs_here, local_len, -1).transpose(
            0, 2, 1, 3, 4
        ).reshape(seqs * length, -1)
        unorder = lambda value: value.reshape(N_DP, seqs_here, N_SEQ, local_len, D).transpose(
            0, 2, 1, 3, 4
        ).reshape(N_DP, N_SEQ, token_rows, D)
        tokens = order(tokens_all)
        grads = order(grad_all)

        def statistics(values):
            average = jnp.mean(values, axis=-1, keepdims=True)
            centred = values - average
            spread = jnp.mean(centred * centred, axis=-1, keepdims=True)
            return centred, lax.rsqrt(spread + NORM_EPSILON)

        centred, rate = statistics(tokens.astype(F32))
        xhat = centred * rate
        normed_one = (xhat * ln1_gain + ln1_bias).astype(BF)
        normed_two = (xhat * ln2_gain + ln2_bias).astype(BF)

        projected = jnp.dot(normed_one, qkv_own, preferred_element_type=F32)
        projected = projected + pick(qkv_bias, part_i, 1).reshape(3 * HEAD_W)
        d_att = lax.dot_general(grads, dense_own, NT, preferred_element_type=F32).astype(BF)
        attended, d_proj = attention(
            projected.reshape(seqs, length, 3 * HEAD_W), d_att.reshape(seqs, length, HEAD_W)
        )
        attended = attended.reshape(seqs * length, HEAD_W)
        d_proj = d_proj.reshape(seqs * length, 3 * HEAD_W)
        d_qkv_bias = jnp.sum(d_proj.astype(F32), axis=0)
        d_normed_one = lax.dot_general(d_proj, qkv_own, NT, preferred_element_type=F32)
        qk_part = lax.dot_general(normed_one, d_proj, TN, preferred_element_type=F32).astype(BF)
        dn_part = lax.dot_general(attended, grads, TN, preferred_element_type=F32).astype(BF)

        pre_act = jnp.dot(normed_two, up_own, preferred_element_type=F32) + pick(up_bias, part_i, 0)
        hidden_wide, slope = gelu_parts(pre_act)
        hidden = hidden_wide.astype(BF)
        wt_part = lax.dot_general(grads, hidden, TN, preferred_element_type=F32).astype(BF)
        d_hidden = jnp.dot(grads, wt_own, preferred_element_type=F32)
        d_pre = (d_hidden * slope).astype(BF)
        d_up_bias = jnp.sum(d_pre.astype(F32), axis=0)
        up_part = lax.dot_general(normed_two, d_pre, TN, preferred_element_type=F32).astype(BF)
        d_normed_two = lax.dot_general(d_pre, up_own, NT, preferred_element_type=F32)

        out_part = jnp.dot(attended, dense_own, preferred_element_type=F32) + lax.dot_general(
            hidden, wt_own, NT, preferred_element_type=F32
        )
        d_gain_one = jnp.sum(d_normed_one * xhat, axis=0)
        d_bias_one = jnp.sum(d_normed_one, axis=0)
        d_gain_two = jnp.sum(d_normed_two * xhat, axis=0)
        d_bias_two = jnp.sum(d_normed_two, axis=0)
        tok_part = d_normed_one * ln1_gain + d_normed_two * ln2_gain

        out_sum, d_xhat, dn_home, qk_home, up_home, wt_home, _ = scatter(
            n_zero,
            rows,
            unorder(out_part.astype(BF)),
            unorder(tok_part.astype(BF)),
            dn_part,
            qk_part,
            up_part,
            wt_part,
        )

        tokens_wide = tokens_low.astype(F32)
        grad_wide = grad_low.astype(F32)
        outputs = (tokens_wide + out_sum + dense_bias + down_bias).astype(BF).reshape(inputs.shape)
        centred_own, rate_own = statistics(tokens_wide)
        xhat_own = centred_own * rate_own
        d_tokens = rate_own * (
            d_xhat
            - jnp.mean(d_xhat, axis=-1, keepdims=True)
            - xhat_own * jnp.mean(d_xhat * xhat_own, axis=-1, keepdims=True)
        )
        input_grad = (grad_wide + d_tokens).astype(BF).reshape(inputs.shape)

        d_out_bias = jnp.sum(grad_wide, axis=0)
        place_in = lambda value, count: lax.dynamic_update_index_in_dim(
            jnp.zeros((value.shape[0], count, value.shape[1]), F32), value, part_i, 1
        ).reshape(-1)
        vector_local = jnp.concatenate(
            [
                d_gain_one,
                d_bias_one,
                place_in(d_qkv_bias.reshape(3, HEAD_W), PARTS),
                d_out_bias,
                d_gain_two,
                d_bias_two,
                place_in(d_up_bias.reshape(1, HID_W), PARTS),
                d_out_bias,
            ]
        )
        vector_sum = lax.psum(vector_local, everywhere)
        vectors_grad = lax.dynamic_slice_in_dim(
            vector_sum, (zero_i * N_SEQ + seq_i) * vectors.shape[0], vectors.shape[0], 0
        )

        vec_upd = adam_step(vectors, vectors_grad, vectors_first, vectors_second, 0.0) + (vectors_grad,)
        qkv_upd = adam(qk_home, 3, qkv_weight, qkv_first, qkv_second)
        dense_upd = adam(dn_home, 1, dense_weight, dense_first, dense_second)
        up_upd = adam(up_home, 1, up_weight, up_first, up_second)
        down_upd = adam(wt_home, 1, down_weight, down_first, down_second, flipped=True)
        updates = (vec_upd, qkv_upd, dense_upd, up_upd, down_upd)
        picked = lambda k: tuple(update[k] for update in updates)
        return (outputs, input_grad) + picked(3) + picked(0) + picked(1) + picked(2)

    return body


def solution(mesh):
    wide = P(("dp", "zero"), "seq", None)
    vector = P(("zero", "seq"))
    rows = P(("zero", "seq"), None)
    columns = P(None, ("zero", "seq"))
    state = (vector, rows, rows, rows, columns)
    return jax.shard_map(
        make_body(dict(mesh.shape)),
        mesh=mesh,
        in_specs=(wide, wide) + state * 3,
        out_specs=(wide, wide) + state * 4,
        check_vma=False,
    )
```

time: 981 us -> 918 us (0.936)
  Pallas kernels: 12.2 us -> 598 us
  waiting for transfers between devices: 295 us -> 66.4 us
  local copies, waits for them, and re-layouts: 195 us -> 27.5 us
  starting transfers between devices: 127 us -> 0.04 us
  other arithmetic: 162 us -> 41.5 us
    pallas_call x0 -> x6, Pallas kernels: none -> 586 us  [the longest x1 273 us: scatter(): pl.pallas_call(functools.partial(scatter_body, n_zero, rows), in_specs=an...]
    ppermute x69 -> x0, waiting for transfers between devices: 295 us -> none  [the longest x27 126 us: swap(): return lax.ppermute(value, axis, [(i, i ^ bit) for i in range(size)])]
    ppermute x69 -> x0, starting transfers between devices: 127 us -> none  [the longest x12 43.1 us: line_gather(): lax.ppermute(above, 'zero', [(i, i + 1) for i in range(step - 1, size - 1)])]
    unnamed x206 -> x102, local copies, waits for them, and re-layouts: 93.2 us -> 11.3 us
    psum x1, waiting for transfers between devices: 0.01 us -> 66.4 us  [body(): vector_sum = lax.psum(vector_local, everywhere)]
    another operation x46 -> x0, other arithmetic: 39.9 us -> none  [pair(): return jnp.stack([low, high], axis=axis)]
    convert_element_type x19 -> x2, other arithmetic: 47.1 us -> 12.8 us  [body(): normed_one = (xhat * ln1_gain + ln1_bias).astype(BF)]
    sub x5 -> x1, other arithmetic: 30.5 us -> 1.41 us  [adam_step(): parameter - LEARN_RATE * (first_hat / (jnp.sqrt(second_hat) + EPSILON) +...]
  transfers between devices with their start and end apart: 72 -> 1, of which waited for: 31 -> 1; matrix products, arithmetic and copies ran while one was open for 38% -> 0% of each run, Pallas kernels for 1% -> 5%
where the time goes in v2:
time: 918 us; the launch traced here: 911 us
  Pallas kernels  598 us (65%)
  matrix products  139 us (15%)
  waiting for transfers between devices  66.4 us (7%)
  other arithmetic  41.5 us (5%)
  local copies, waits for them, and re-layouts  27.5 us (3%)
  blocking collectives  23.4 us (3%)
  between operations  15.2 us (2%)
    pallas_call x1, Pallas kernels, scatter(): pl.pallas_call(functools.partial(scatter_body, n_zero, rows), in_specs=an...  273 us
    pallas_call x1, Pallas kernels, gather(): pl.pallas_call(functools.partial(gather_body, n_zero, rows), in_specs=any...  266 us
    psum x1, waiting for transfers between devices, body(): vector_sum = lax.psum(vector_local, everywhere)  66.4 us
    pallas_call x4, Pallas kernels, adam(): pl.pallas_call(functools.partial(adam_body, WEIGHT_DECAY, flipped), grid=...  47.5 us
    all_gather x1, blocking collectives, body(): lax.all_gather(vectors.astype(BF), ('zero', 'seq'), axis=0, tiled=True)  23.4 us
    dot_general x1, matrix products, body(): lax.dot_general(d_pre, up_own, NT, preferred_element_type=F32)  22.9 us
  transfers between devices with their start and end apart: 1, of which 1 were waited for; matrix products, arithmetic and copies ran while one was open for 0% of the time, Pallas kernels for 5%

profile of v2, /device:TPU:0, one launch (start us, length us, event | category | flops | bytes accessed | tf_op | source)
XLA Modules:
  0.0 911.0 jit_solution(9292355504303951520)
XLA Ops:
  8.0 23.4 %all-gather = bf16[16,1,1664]{2,1,0:T(2,128)(2,1)S(1)} all-gather(bf16[1,1,1664]{2,1,0:T(2,128)(2,1)S(1)} %reshape.222), channel_id=1, replica_groups=mesh['dp'=2,'zero'=4,'seq'=4] {'zero','seq'}, dimensions={0}, use_global_device_ids=true | all-gather | bytes 56576 | tf_op jit(solution)/shard_map/all_gather | solution.py:750
  58.7 266.0 %gather.1 = (bf16[2,4,256,2048]{3,2,1,0:T(8,128)(2,1)}, bf16[2,4,256,2048]{3,2,1,0:T(8,128)(2,1)}, bf16[2048,256]{1,0:T(8,128)(2,1)}, bf16[256,2048]{1,0:T(8,128...) custom-call(bf16[256,2048]{1,0:T(8,128)(2,1)} %bitcast.87, ...), custom_call_target="tpu_custom_call" | custom-call | tf_op jit(solution)/shard_map/gather/pallas_call | solution.py:578
  324.7 4.7 convert_reduce_fusion
  337.3 5.5 add_convert_fusion
  342.8 7.4 add_convert_fusion.4
  350.2 8.6 broadcast_add_fusion
  358.8 12.3 %attention.1 = (bf16[2,1024,256]{2,1,0:T(8,128)(2,1)S(1)}, bf16[2,1024,768]{2,1,0:T(8,128)(2,1)}) custom-call(f32[2,1024,768]{2,1,0:T(8,128)} %bitcast.128, f32[1024,128]{1,0:T(8,128)S(1)} %concatenate.17.cos_ref, f32[1024,128]{1,0:T(8,128)S(1)} %maximum_maximum_fusion.sin_ref, bf16[2,1024,256]{2,1,0:T(8,128)(2,1)S(1)} %bitcast.85), custom_call_target="tpu_custom_call" | custom-call | flops 4831838208 | bytes 11534336 | tf_op jit(solution)/shard_map/attention/pallas_call | solution.py:475
  373.6 12.7 %fusion.33 = f32[2048,2048]{1,0:T(8,128)} fusion(bf16[2048,768]{1,0:T(8,128)(2,1)} %bitcast.105, bf16[2048,768]{1,0:T(8,128)(2,1)S(1)} %copy-done.36), kind=kOutput, calls=%fused_computation.90 | convolution fusion | flops 6442450944 | bytes 23068672 | tf_op jit(solution)/shard_map/dot_general | solution.py:807
  386.4 8.5 convolution_convert_fusion.2.refs_3_
  395.0 6.8 convolution_convert_fusion.3.refs_2_
  401.9 14.0 %multiply_convert_fusion = (bf16[2048,1024]{1,0:T(8,128)(2,1)S(1)}, f32[2048,1024]{1,0:T(8,128)}) fusion(f32[1024]{0:T(1024)S(1)} %bitcast.125, bf16[2048,2048]{1,0:T(8,128)(2,1)} %get-tuple-element.96, bf16[2048,1024]{1,0:T(8,128)(2,1)S(1)} %copy-done.34), kind=kOutput, calls=%fused_computation.19 | convolution fusion | flops 8602517504 | bytes 25169920 | tf_op jit(solution)/shard_map/dot_general | solution.py:811
  415.9 10.5 %convolution_convert_fusion.refs_5_ = bf16[2048,1024]{1,0:T(8,128)(2,1)} fusion(bf16[2048,2048]{1,0:T(8,128)(2,1)S(1)} %bitcast.92, bf16[2048,1024]{1,0:T(8,128)(2,1)S(1)} %get-tuple-element.117), kind=kOutput, calls=%fused_computation.22 | convolution fusion | flops 8592031744 | bytes 16777216 | tf_op jit(solution)/shard_map/dot_general | solution.py:814
  426.4 11.7 %fusion.32 = f32[2048,2048]{1,0:T(8,128)} fusion(bf16[2048,1024]{1,0:T(8,128)(2,1)S(1)} %get-tuple-element.117, bf16[2048,1024]{1,0:T(8,128)(2,1)S(1)} %copy-done.35), kind=kOutput, calls=%fused_computation.89 | convolution fusion | flops 8589934592 | bytes 25165824 | tf_op jit(solution)/shard_map/dot_general | solution.py:821
  438.1 15.4 %convert_reduce_fusion.1 = (f32[1024]{0:T(1024)S(1)}, bf16[2048,1024]{1,0:T(8,128)(2,1)}) fusion(f32[2048,1024]{1,0:T(8,128)} %get-tuple-element.118, f32[1024]{0:T(1024)S(1)} %bitcast.126, bf16[2048,2048]{1,0:T(8,128)(2,1)S(1)} %bitcast.93, bf16[2048,1024]{1,0:T(8,128)(2,1)S(1)} %copy-done.35), kind=kOutput, calls=%fused_computation.18 | convolution fusion | flops 8617196544 | bytes 25174016 | tf_op jit(solution)/shard_map/dot_general | solution.py:815
  453.5 12.2 %convolution_convert_fusion.1.refs_4_ = bf16[2048,1024]{1,0:T(8,128)(2,1)} fusion(bf16[2048,2048]{1,0:T(8,128)(2,1)S(1)} %bitcast.96, bf16[2048,1024]{1,0:T(8,128)(2,1)} %get-tuple-element.120), kind=kOutput, calls=%fused_computation.23 | convolution fusion | flops 8592031744 | bytes 16777216 | tf_op jit(solution)/shard_map/dot_general | solution.py:818
  465.7 11.4 %add_convert_fusion.2 = bf16[2048,2048]{1,0:T(8,128)(2,1)} fusion(f32[2048,2048]{1,0:T(8,128)} %fusion.32, bf16[2048,256]{1,0:T(8,128)(2,1)S(1)} %bitcast.84, bf16[256,2048]{1,0:T(8,128)(2,1)S(1)} %copy-done.16), kind=kOutput, calls=%fused_computation.6 | convolution fusion | flops 2155872256 | bytes 27262976 | tf_op jit(solution)/shard_map/dot_general | solution.py:821
  477.1 22.9 %fusion.26 = (f32[2048]{0:T(1024)S(1)}, f32[2048]{0:T(1024)S(1)}, bf16[2048,2048]{1,0:T(8,128)(2,1)}, f32[2048]{0:T(1024)S(1)}, f32[2048]{0:T(1024)S(1)}) fusion(f32[2048]{0:T(1024)S(1)} %bitcast.124, f32[2048]{0:T(1024)S(1)} %bitcast.122, bf16[2,4,256,2048]{3,2,1,0:T(8,128)(2,1)} %get-tuple-element.52, f32[2048]{0:T(1024)S(1)} %copy-done.23, ...), kind=kOutput, calls=%fused_computation.84 | convolution fusion | flops 8644452352 | bytes 42008576 | tf_op jit(solution)/shard_map/dot_general | solution.py:819
  500.1 272.7 %scatter.1 = (f32[256,2048]{1,0:T(8,128)}, f32[256,2048]{1,0:T(8,128)}, bf16[2,4,128,256]{3,2,1,0:T(8,128)(2,1)}, bf16[2,4,128,768]{3,2,1,0:T(8,128)(2,1)}, bf16...) custom-call(bf16[2,4,256,2048]{3,2,1,0:T(8,128)(2,1)} %bitcast.86, ...), custom_call_target="tpu_custom_call" | custom-call | tf_op jit(solution)/shard_map/scatter/pallas_call | solution.py:669
  775.4 5.8 convert_reduce_fusion.4
  786.7 3.9 adam.5
  792.1 16.6 %adam.4 = (f32[128,6144]{1,0:T(8,128)}, f32[128,6144]{1,0:T(8,128)}, f32[128,6144]{1,0:T(8,128)}, f32[128,6144]{1,0:T(8,128)}) custom-call(bf16[2,4,128,768]{3,2,1,0:T(8,128)(2,1)S(1)} %copy-done.5, f32[128,6144]{1,0:T(8,128)S(1)} %copy-done.1, f32[128,6144]{1,0:T(8,128)} %first.4, f32[128,6144]{1,0:T(8,128)} %second.4), custom_call_target="tpu_custom_call" | custom-call | tf_op jit(solution)/shard_map/adam/pallas_call | solution.py:704
  808.8 13.7 %adam.6 = (f32[128,8192]{1,0:T(8,128)}, f32[128,8192]{1,0:T(8,128)}, f32[128,8192]{1,0:T(8,128)}, f32[128,8192]{1,0:T(8,128)}) custom-call(bf16[2,4,128,1024]{3,2,1,0:T(8,128)(2,1)S(1)} %copy-done.3, f32[128,8192]{1,0:T(8,128)} %param.40, f32[128,8192]{1,0:T(8,128)} %first.6, f32[128,8192]{1,0:T(8,128)} %second.6), custom_call_target="tpu_custom_call" | custom-call | tf_op jit(solution)/shard_map/adam/pallas_call | solution.py:704
  822.5 13.3 %adam.7 = (f32[8192,128]{1,0:T(8,128)}, f32[8192,128]{1,0:T(8,128)}, f32[8192,128]{1,0:T(8,128)}, f32[8192,128]{1,0:T(8,128)}) custom-call(bf16[2,4,128,1024]{3,2,1,0:T(8,128)(2,1)S(1)} %copy-done.2, f32[8192,128]{1,0:T(8,128)} %param.41, f32[8192,128]{1,0:T(8,128)} %first.7, f32[8192,128]{1,0:T(8,128)} %second.7), custom_call_target="tpu_custom_call" | custom-call | tf_op jit(solution)/shard_map/adam/pallas_call | solution.py:704
  835.8 66.4 %all-reduce.3.cloned.1.call-done = f32[26624]{0:T(1024)} async-done(((f32[26624]{0:T(1024)}), f32[26624]{0:T(1024)}) %all-reduce.3.cloned.1.call-update) | async-done | bytes 106512 | tf_op jit(solution)/shard_map/psum | solution.py:869
  (157 shorter events, 49.4 us)
Async XLA Ops:
  7.2 895.0 %all-reduce.3.cloned.1.call-start = ((), (), s32[]{:S(2)}) async-start(), calls=%async_computation | async-start | bytes 212992 | tf_op jit(solution)/shard_map/psum | solution.py:869
  32.1 310.7 %copy-start.18 = (f32[2048]{0:T(1024)}, f32[2048]{0:T(1024)S(1)}, u32[]{:S(2)}) copy-start(f32[2048]{0:T(1024)S(1)} %get-tuple-element.112) | copy-start | bytes 24580
  32.1 310.7 %copy-start.22 = (f32[2048]{0:T(1024)}, f32[2048]{0:T(1024)S(1)}, u32[]{:S(2)}) copy-start(f32[2048]{0:T(1024)S(1)} %get-tuple-element.110) | copy-start | bytes 24580
  38.8 13.5 %copy-start = (f32[128,6144]{1,0:T(8,128)S(1)}, f32[128,6144]{1,0:T(8,128)}, u32[]{:S(2)}) copy-start(f32[128,6144]{1,0:T(8,128)} %param.38) | copy-start | bytes 9437188
  329.5 13.3 %copy-start.24 = (f32[2,2,4,128]{3,1,2,0:T(2,128)}, f32[2,2,4,128]{3,1,2,0:T(2,128)S(1)}, u32[]{:S(2)}) copy-start(f32[2,2,4,128]{3,1,2,0:T(2,128)S(1)} %copy.69) | copy-start | bytes 24580
  371.1 15.3 %slice-start.4 = ((s8[8388608]{0:T(1024)(128)(4,1)}), s8[4194304]{0:T(1024)(128)(4,1)S(1)}, s32[]{:S(2)}) async-start(s8[8388608]{0:T(1024)(128)(4,1)} %bitcast.97), calls=%async_computation.5 | async-start | bytes 8388608
  373.6 12.8 %slice-start.5 = ((s8[8388608]{0:T(1024)(128)(4,1)}), s8[4194304]{0:T(1024)(128)(4,1)S(1)}, s32[]{:S(2)}) async-start(s8[8388608]{0:T(1024)(128)(4,1)} %bitcast.97), calls=%async_computation.6 | async-start | bytes 8388608
  373.6 12.8 %copy-start.12 = (bf16[2,1024,768]{2,1,0:T(8,128)(2,1)S(1)}, bf16[2,1024,768]{2,1,0:T(8,128)(2,1)}, u32[]{:S(2)}) copy-start(bf16[2,1024,768]{2,1,0:T(8,128)(2,1)} %get-tuple-element.59) | copy-start | bytes 9437188
  395.0 20.9 %slice-start = ((s8[8388608]{0:T(1024)(128)(4,1)}), s8[4194304]{0:T(1024)(128)(4,1)S(1)}, s32[]{:S(2)}) async-start(s8[8388608]{0:T(1024)(128)(4,1)} %bitcast.90), calls=%async_computation.1 | async-start | bytes 8388608
  401.9 14.0 %slice-start.1 = ((s8[8388608]{0:T(1024)(128)(4,1)}), s8[4194304]{0:T(1024)(128)(4,1)S(1)}, s32[]{:S(2)}) async-start(s8[8388608]{0:T(1024)(128)(4,1)} %bitcast.90), calls=%async_computation.2 | async-start | bytes 8388608
  426.4 27.1 %slice-start.2 = ((s8[8388608]{0:T(1024)(128)(4,1)}), s8[4194304]{0:T(1024)(128)(4,1)S(1)}, s32[]{:S(2)}) async-start(s8[8388608]{0:T(1024)(128)(4,1)} %bitcast.95), calls=%async_computation.3 | async-start | bytes 8388608
  438.1 15.4 %slice-start.3 = ((s8[8388608]{0:T(1024)(128)(4,1)}), s8[4194304]{0:T(1024)(128)(4,1)S(1)}, s32[]{:S(2)}) async-start(s8[8388608]{0:T(1024)(128)(4,1)} %bitcast.95), calls=%async_computation.4 | async-start | bytes 8388608
  453.5 12.2 %copy-start.16 = (bf16[256,2048]{1,0:T(8,128)(2,1)S(1)}, bf16[256,2048]{1,0:T(8,128)(2,1)}, u32[]{:S(2)}) copy-start(bf16[256,2048]{1,0:T(8,128)(2,1)} %get-tuple-element.55) | copy-start | bytes 3145732
  500.0 272.7 %copy-start.10 = (bf16[1,256,2048]{2,1,0:T(8,128)(2,1)S(1)}, bf16[1,256,2048]{2,1,0:T(8,128)(2,1)}, u32[]{:S(2)}) copy-start(bf16[1,256,2048]{2,1,0:T(8,128)(2,1)} %param.21) | copy-start | bytes 3145732
  500.0 272.7 %copy-start.30 = (f32[256]{0:T(256)S(1)}, f32[256]{0:T(256)}, u32[]{:S(2)}) copy-start(f32[256]{0:T(256)} %copy-done.29) | copy-start | bytes 3076
  500.0 272.8 %copy-start.31 = (f32[256]{0:T(256)S(1)}, f32[256]{0:T(256)}, u32[]{:S(2)}) copy-start(f32[256]{0:T(256)} %add_rsqrt_fusion.1) | copy-start | bytes 3076
  500.0 275.4 %copy-start.20 = (f32[2048]{0:T(1024)S(1)}, f32[2048]{0:T(1024)}, u32[]{:S(2)}) copy-start(f32[2048]{0:T(1024)} %get-tuple-element.107) | copy-start | bytes 24580
  500.1 275.4 %copy-start.21 = (f32[2048]{0:T(1024)S(1)}, f32[2048]{0:T(1024)}, u32[]{:S(2)}) copy-start(f32[2048]{0:T(1024)} %get-tuple-element.108) | copy-start | bytes 24580
  774.9 15.7 %copy-start.1 = (f32[128,6144]{1,0:T(8,128)S(1)}, f32[128,6144]{1,0:T(8,128)}, u32[]{:S(2)}) copy-start(f32[128,6144]{1,0:T(8,128)} %param.38) | copy-start | bytes 9437188
  790.6 18.2 %copy-start.3 = (bf16[2,4,128,1024]{3,2,1,0:T(8,128)(2,1)S(1)}, bf16[2,4,128,1024]{3,2,1,0:T(8,128)(2,1)}, u32[]{:S(2)}) copy-start(bf16[2,4,128,1024]{3,2,1,0:T(8,128)(2,1)} %get-tuple-element.66.home) | copy-start | bytes 6291460
  808.8 13.7 %copy-start.2 = (bf16[2,4,128,1024]{3,2,1,0:T(8,128)(2,1)S(1)}, bf16[2,4,128,1024]{3,2,1,0:T(8,128)(2,1)}, u32[]{:S(2)}) copy-start(bf16[2,4,128,1024]{3,2,1,0:T(8,128)(2,1)} %get-tuple-element.68.home) | copy-start | bytes 6291460
  822.5 79.7 %copy-start.28 = (f32[1664]{0:T(1024)S(1)}, f32[1664]{0:T(1024)}, u32[]{:S(2)}) copy-start(f32[1664]{0:T(1024)} %param.23) | copy-start | bytes 19972
  822.5 79.7 %copy-start.32 = (f32[1664]{0:T(1024)S(1)}, f32[1664]{0:T(1024)}, u32[]{:S(2)}) copy-start(f32[1664]{0:T(1024)} %param.28) | copy-start | bytes 19972
  822.5 79.7 %copy-start.33 = (f32[1664]{0:T(1024)S(1)}, f32[1664]{0:T(1024)}, u32[]{:S(2)}) copy-start(f32[1664]{0:T(1024)} %param.33) | copy-start | bytes 19972
  (20 other events, 114.4 us)
Sparse Core Ops, SparseCore 0:
  782.1 120.0 all-reduce.2

commit v3 on v2

--- a/solution.py
+++ b/solution.py
@@ -183,11 +183,16 @@
     def __init__(self, wire, place, block, whole):
         self.wire, self.place, self.own, self.whole = wire, place, block, whole
         self.slots = {name: wire.slot() for name in ("far", "across", "both0", "both1", "c0", "c1", "c2", "c3")}
-        self.half = block.shape[0] // 2
+        self.rows = block.shape[0]
+        self.half = self.rows // 2
+
+    def at(self, dp, s):
+        row = (dp * N_SEQ + s) * self.rows
+        return self.whole.at[pl.ds(pl.multiple_of(row, self.rows), self.rows)]
 
     def start(self, local_sem):
         p, w, slots = self.place, self.wire, self.slots
-        mine = self.whole.at[p.dp, p.s]
+        mine = self.at(p.dp, p.s)
         w.send(slots["far"], self.own, mine, p.far)
         w.send(slots["across"], self.own, mine, p.across)
         w.send(slots["c0"], self.own, mine, p.core)
@@ -196,7 +201,7 @@
 
     def turn(self):
         p, w, slots, h = self.place, self.wire, self.slots, self.half
-        far, across = self.whole.at[p.dp, p.s_far], self.whole.at[p.dp_far, p.s]
+        far, across = self.at(p.dp, p.s_far), self.at(p.dp_far, p.s)
         w.receive(slots["far"], far, p.far)
         w.send(slots["both0"], far.at[pl.ds(0, h)], far.at[pl.ds(0, h)], p.across)
         w.send(slots["c1"], far, far, p.core)
@@ -206,17 +211,17 @@
 
     def turn_again(self):
         p, w, slots, h = self.place, self.wire, self.slots, self.half
-        both = self.whole.at[p.dp_far, p.s_far]
+        both = self.at(p.dp_far, p.s_far)
         w.receive(slots["both0"], both.at[pl.ds(0, h)], p.across)
         w.receive(slots["both1"], both.at[pl.ds(h, h)], p.far)
         w.send(slots["c3"], both, both, p.core)
 
     def wait(self):
         p, w, slots = self.place, self.wire, self.slots
-        w.receive(slots["c0"], self.whole.at[p.dp, p.s_core], p.core)
-        w.receive(slots["c1"], self.whole.at[p.dp, p.s_both], p.core)
-        w.receive(slots["c2"], self.whole.at[p.dp_far, p.s_core], p.core)
-        w.receive(slots["c3"], self.whole.at[p.dp_far, p.s_both], p.core)
+        w.receive(slots["c0"], self.at(p.dp, p.s_core), p.core)
+        w.receive(slots["c1"], self.at(p.dp, p.s_both), p.core)
+        w.receive(slots["c2"], self.at(p.dp_far, p.s_core), p.core)
+        w.receive(slots["c3"], self.at(p.dp_far, p.s_both), p.core)
         self.copied.wait()
 
 
@@ -236,9 +241,9 @@
 
 
 class LineScatter:
-    def __init__(self, wire, place, parts, ups, downs, total, own, rows, sem):
+    def __init__(self, wire, place, parts, held, total, own, rows, sem):
         self.wire, self.place, self.parts, self.rows = wire, place, parts, rows
-        self.ups, self.downs, self.total, self.own, self.sem = ups, downs, total, own, sem
+        self.held, self.total, self.own, self.sem, self.slot = held, total, own, sem, 0
         self.up_slots = [wire.slot() for _ in range(place.n)]
         self.down_slots = [wire.slot() for _ in range(place.n)]
 
@@ -246,53 +251,65 @@
         return self.parts.at[pl.ds(pl.multiple_of(j * self.rows, self.rows), self.rows)]
 
     def fetch(self, j, target):
-        copy = pltpu.make_async_copy(self.part(j), target, self.sem)
+        return pltpu.make_async_copy(self.part(j), target, self.sem)
+
+    def advance(self):
+        p, slot = self.place, self.slot
+        self.slot = slot + 1
+        top = p.n - 1
+        up = jnp.minimum(top - slot + p.z, top)
+        self.hop(up, up + 1, self.up_slots[0] + up, p.above, p.below, p.z <= slot, p.z == 0)
+        down = jnp.maximum(slot - top + p.z, 0)
+        self.hop(down, down, self.down_slots[0] + down, p.below, p.above, top - p.z <= slot, p.z == top)
+
+    def hop(self, j, index, slot, onto, source, active, first):
+        held = self.held.at[index]
+
+        def go():
+            @pl.when(first)
+            def _():
+                copy = self.fetch(j, held)
+                copy.start()
+                copy.wait()
+
+            @pl.when(jnp.logical_not(first))
+            def _():
+                copy = self.fetch(j, self.own)
+                copy.start()
+                self.wire.receive(slot, held, source)
+                copy.wait()
+                add_rows(held, held, self.own)
+
+        pl.when(active)(go)
+        self.wire.send(slot, held, held, onto, active)
+
+    def last(self):
+        p = self.place
+        while self.slot < p.n - 1:
+            self.advance()
+        copy = self.fetch(p.z, self.own)
         copy.start()
         copy.wait()
-
-    def step(self, k):
-        p = self.place
-        j = p.n - 1 - k
-        self.hop(j, self.ups, self.up_slots[j], p.above, p.below, p.z < j, p.z == 0)
-        j = k
-        self.hop(j, self.downs, self.down_slots[j], p.below, p.above, p.z > j, p.z == p.n - 1)
-
-    def hop(self, j, held, slot, onto, source, active, first):
-        def go():
-            pl.when(first)(lambda: self.fetch(j, held.at[j]))
-
-            @pl.when(jnp.logical_not(first))
-            def _():
-                self.fetch(j, self.own)
-                self.wire.receive(slot, held.at[j], source)
-                add_rows(held.at[j], held.at[j], self.own)
-
-        pl.when(active)(go)
-        self.wire.send(slot, held.at[j], held.at[j], onto, active)
-
-    def last(self):
-        p = self.place
-        self.fetch(p.z, self.own)
-        up, down = self.ups.at[p.z], self.downs.at[p.z]
+        up, down = self.held.at[p.z + 1], self.held.at[p.z]
 
         @pl.when(p.z == 0)
         def _():
-            self.arrive(self.downs, self.down_slots, p.above)
+            self.arrive(down, self.down_slots, p.above)
             add_rows(self.total, self.own, down)
 
         @pl.when(p.z == p.n - 1)
         def _():
-            self.arrive(self.ups, self.up_slots, p.below)
+            self.arrive(up, self.up_slots, p.below)
             add_rows(self.total, self.own, up)
 
         @pl.when((p.z > 0) & (p.z < p.n - 1))
         def _():
-            self.arrive(self.ups, self.up_slots, p.below)
-            self.arrive(self.downs, self.down_slots, p.above)
+            self.arrive(up, self.up_slots, p.below)
+            self.arrive(down, self.down_slots, p.above)
             add_rows(self.total, self.own, up, down)
 
     def arrive(self, held, slots, source):
-        self.wire.receive(slots[0] + self.place.z, held.at[self.place.z], source)
+        self.wire.receive(slots[0] + self.place.z, held, source)
 
 
 class Home:
@@ -345,10 +362,15 @@
         self.wire, self.place, self.parts, self.mate, self.sums = wire, place, parts, mate, mate
         self.from_far, self.from_across, self.turned = from_far, from_across, turned
         self.total, self.own, self.sem = total, own, sem
-        self.half = total.shape[0] // 2
+        self.rows = total.shape[0]
+        self.half = self.rows // 2
         self.core_slots = [[wire.slot() for _ in range(2)] for _ in range(2)]
         names = ("turn_across", "turn_far", "far0", "far1", "across0", "across1")
         self.slots = {name: wire.slot() for name in names}
+
+    def part(self, dp, s):
+        row = (dp * N_SEQ + s) * self.rows
+        return self.parts.at[pl.ds(pl.multiple_of(row, self.rows), self.rows)]
 
     def start(self):
         p = self.place
@@ -356,7 +378,7 @@
         for dp in range(2):
             for y in range(2):
                 self.wire.send(
-                    self.core_slots[dp][y], self.parts.at[dp, 2 * y + core], self.mate.at[dp, y], p.core
+                    self.core_slots[dp][y], self.part(dp, 2 * y + core), self.mate.at[dp, y], p.core
                 )
 
     def combine(self, dp, y):
@@ -367,7 +389,7 @@
 
                 @pl.when((dp == d) & (y == v))
                 def _(d=d, v=v):
-                    copy = pltpu.make_async_copy(self.parts.at[d, 2 * v + core], self.own, self.sem)
+                    copy = pltpu.make_async_copy(self.part(d, 2 * v + core), self.own, self.sem)
                     copy.start()
                     self.wire.receive(self.core_slots[d][v], self.mate.at[d, v], p.core)
                     copy.wait()
@@ -412,278 +434,454 @@
         add_rows(self.total, self.sums.at[p.dp, lax.div(p.s, 2)], self.from_far, self.from_across)
 
 
-def attention_body(scale, projected, cos_ref, sin_ref, d_att_ref, att_ref, d_proj_ref, keys_acc, values_acc):
-    length = projected.shape[1]
-    tile = min(256, length)
-    half = ROT // 2
-    cosine = cos_ref[...]
-    sine = sin_ref[...]
-
-    def turn(block):
-        first = block[:, :128]
-        rolled = jnp.concatenate([first[:, half:ROT], first[:, :half], first[:, ROT:]], axis=1)
-        return jnp.concatenate([first * cosine + rolled * sine, block[:, 128:]], axis=1)
-
-    def turn_back(block):
-        first = block[:, :128]
-        scaled = first * sine
-        rolled = jnp.concatenate([scaled[:, half:ROT], scaled[:, :half], scaled[:, ROT:]], axis=1)
-        return jnp.concatenate([first * cosine + rolled, block[:, 128:]], axis=1)
-
-    queries = turn(projected[0, :, 0:HEAD_DIM]).astype(BF)
-    keys = turn(projected[0, :, HEAD_DIM : 2 * HEAD_DIM]).astype(BF)
-    values = projected[0, :, 2 * HEAD_DIM :].astype(BF)
-    d_att_all = d_att_ref[0]
-    keys_acc[...] = jnp.zeros_like(keys_acc)
-    values_acc[...] = jnp.zeros_like(values_acc)
-    d_queries = []
-    for at in range(length // tile):
-        rows = slice(at * tile, (at + 1) * tile)
-        seen = (at + 1) * tile
-        q = queries[rows]
-        d_att = d_att_all[rows]
-        k, v = keys[:seen], values[:seen]
-        scores = lax.dot_general(q, k, NT, preferred_element_type=F32) * scale
-        row = lax.broadcasted_iota(jnp.int32, scores.shape, 0) + at * tile
-        column = lax.broadcasted_iota(jnp.int32, scores.shape, 1)
-        scores = jnp.where(row >= column, scores, MASKED)
-        top = jnp.max(scores, axis=1, keepdims=True)
-        grown = jnp.exp(scores - top)
-        prob = grown * (1.0 / jnp.sum(grown, axis=1, keepdims=True))
-        prob_low = prob.astype(BF)
-        att_ref[0, rows, :] = jnp.dot(prob_low, v, preferred_element_type=F32).astype(BF)
-        d_prob = lax.dot_general(d_att, v, NT, preferred_element_type=F32)
-        inner = jnp.sum(d_prob * prob, axis=1, keepdims=True)
-        d_scores = (prob * (d_prob - inner)).astype(BF)
-        d_queries.append(jnp.dot(d_scores, k, preferred_element_type=F32) * scale)
-        keys_acc[:seen, :] += lax.dot_general(d_scores, q, TN, preferred_element_type=F32)
-        values_acc[:seen, :] += lax.dot_general(prob_low, d_att, TN, preferred_element_type=F32)
-    d_proj_ref[0, :, 0:HEAD_DIM] = turn_back(jnp.concatenate(d_queries, axis=0)).astype(BF)
-    d_proj_ref[0, :, HEAD_DIM : 2 * HEAD_DIM] = turn_back(keys_acc[...] * scale).astype(BF)
-    d_proj_ref[0, :, 2 * HEAD_DIM :] = values_acc[...].astype(BF)
-
-
-def attention(projected, d_att):
-    seqs, length, _ = projected.shape
-    cosine, sine = rotary_tables(jnp.arange(length).astype(F32))
-    half = ROT // 2
-    sine_turn = jnp.concatenate([-sine[:, :half], sine[:, half:]], axis=1)
-    cosine = jnp.concatenate([cosine, jnp.ones((length, 128 - ROT), F32)], axis=1)
-    sine_turn = jnp.concatenate([sine_turn, jnp.zeros((length, 128 - ROT), F32)], axis=1)
-    whole = pl.BlockSpec((length, 128), lambda s: (0, 0))
-    one = lambda width: pl.BlockSpec((1, length, width), lambda s: (s, 0, 0))
-    return pl.pallas_call(
-        functools.partial(attention_body, 1.0 / math.sqrt(HEAD_DIM)),
-        grid=(seqs,),
-        in_specs=[one(3 * HEAD_DIM), whole, whole, one(HEAD_DIM)],
-        out_specs=[one(HEAD_DIM), one(3 * HEAD_DIM)],
-        out_shape=[
-            jax.ShapeDtypeStruct((seqs, length, HEAD_DIM), BF),
-            jax.ShapeDtypeStruct((seqs, length, 3 * HEAD_DIM), BF),
-        ],
-        scratch_shapes=[pltpu.VMEM((length, HEAD_DIM), F32), pltpu.VMEM((length, HEAD_DIM), F32)],
-        compiler_params=pltpu.CompilerParams(vmem_limit_bytes=48 * 1024 * 1024),
-        cost_estimate=pl.CostEstimate(
-            flops=seqs * length * length * HEAD_DIM * 9,
-            bytes_accessed=seqs * length * HEAD_DIM * 22,
-            transcendentals=seqs * length * length,
-        ),
-        name="attention",
-    )(projected, cosine, sine_turn, d_att)
-
-
 def gelu_parts(values):
     phi_wide = 0.5 * (1.0 + lax.erf(values * (1.0 / math.sqrt(2.0))))
     density = jnp.exp(-0.5 * values * values) * (1.0 / math.sqrt(2.0 * math.pi))
     return values * phi_wide, phi_wide + values * density
 
 
+TILE = 256
+
+
+def pipe(body, grid, ins, outs, refs):
+    pltpu.emit_pipeline(
+        body, grid=(grid,), in_specs=[spec for spec in ins], out_specs=[spec for spec in outs]
+    )(*refs)
+
+
+def tall(width, tile=TILE):
+    return pl.BlockSpec((tile, width), lambda i: (i, 0))
+
+
+def slim(height, tile=TILE):
+    return pl.BlockSpec((height, tile), lambda i: (0, i))
+
+
+def fixed(height, width):
+    return pl.BlockSpec((height, width), lambda i: (0, 0), pipeline_mode=pl.Buffered(1))
+
+
+def column_sums(total, values):
+    rows, width = values.shape
+    total[...] += jnp.sum(values.reshape(rows // 8, 8, width), axis=0)
+
+
+def rotate(block, cosine, sine):
+    half = ROT // 2
+    first = block[:, :128]
+    rolled = jnp.concatenate([first[:, half:ROT], first[:, :half], first[:, ROT:]], axis=1)
+    return jnp.concatenate([first * cosine + rolled * sine, block[:, 128:]], axis=1)
+
+
+def rotate_back(block, cosine, sine):
+    half = ROT // 2
+    first = block[:, :128]
+    scaled = first * sine
+    rolled = jnp.concatenate([scaled[:, half:ROT], scaled[:, :half], scaled[:, ROT:]], axis=1)
+    return jnp.concatenate([first * cosine + rolled, block[:, 128:]], axis=1)
+
+
+class Layer:
+    def __init__(self, refs):
+        self.__dict__.update(refs)
+        self.tokens = self.x.shape[0]
+        self.length = self.tokens // N_DP
+        self.tiles = self.tokens // TILE
+
+    def clear(self):
+        for total in (self.gain1, self.bias1, self.gain2, self.bias2, self.qkv_total, self.up_total):
+            total[...] = jnp.zeros_like(total)
+
+    def normalise(self, part, of):
+        count = self.tokens // of
+        rows = pl.ds(part * count, count)
+
+        def body(x, n1, n2, xh):
+            def some(i, carry):
+                at = pl.ds(pl.multiple_of(i * 32, 32), 32)
+                values = x[at, :].astype(F32)
+                centred = values - jnp.mean(values, axis=1, keepdims=True)
+                spread = jnp.mean(centred * centred, axis=1, keepdims=True)
+                xhat = centred * lax.rsqrt(spread + NORM_EPSILON)
+                xh[at, :] = xhat.astype(BF)
+                n1[at, :] = (xhat * self.vec[0:1, :] + self.vec[1:2, :]).astype(BF)
+                n2[at, :] = (xhat * self.vec[2:3, :] + self.vec[3:4, :]).astype(BF)
+                return carry
+
+            lax.fori_loop(0, TILE // 32, some, 0)
+
+        pipe(
+            body,
+            count // TILE,
+            [tall(D)],
+            [tall(D)] * 3,
+            [ref.at[rows] for ref in (self.x, self.n1, self.n2, self.xhat)],
+        )
+
+    def attend(self, seq):
+        scale = 1.0 / math.sqrt(HEAD_DIM)
+        length = self.length
+
+        def project(q_refs, n1, qkv, g, dense):
+            at = pl.ds(pl.multiple_of(pl.program_id(0) * TILE, TILE), TILE)
+            cosine, sine = self.cos[at, :], self.sin[at, :]
+            wide = jnp.dot(n1[...], qkv[...], preferred_element_type=F32) + self.qkv_bias[...]
+            q_refs[0][at, :] = rotate(wide[:, :HEAD_W], cosine, sine).astype(BF)
+            q_refs[1][at, :] = rotate(wide[:, HEAD_W : 2 * HEAD_W], cosine, sine).astype(BF)
+            q_refs[2][at, :] = wide[:, 2 * HEAD_W :].astype(BF)
+            q_refs[3][at, :] = lax.dot_general(g[...], dense[...], NT, preferred_element_type=F32).astype(BF)
+
+        def one(q_ref, k_ref, v_ref, d_att_ref, k_total, v_total):
+            base = seq * length
+            rows = pl.ds(base, length)
+            pipe(
+                functools.partial(project, (q_ref, k_ref, v_ref, d_att_ref)),
+                length // TILE,
+                [tall(D), fixed(D, 3 * HEAD_W), tall(D), fixed(HEAD_W, D)],
+                [],
+                (self.n1.at[rows], self.qkv, self.g.at[rows], self.dense),
+            )
+            k_total[...] = jnp.zeros_like(k_total)
+            v_total[...] = jnp.zeros_like(v_total)
+            for i in range(length // TILE):
+                seen = (i + 1) * TILE
+                here = pl.ds(i * TILE, TILE)
+                there = pl.ds(base + i * TILE, TILE)
+                q, d_att = q_ref[here, :], d_att_ref[here, :]
+                k, v = k_ref[:seen, :], v_ref[:seen, :]
+                scores = lax.dot_general(q, k, NT, preferred_element_type=F32) * scale
+                row = lax.broadcasted_iota(jnp.int32, scores.shape, 0) + i * TILE
+                column = lax.broadcasted_iota(jnp.int32, scores.shape, 1)
+                scores = jnp.where(row >= column, scores, MASKED)
+                grown = jnp.exp(scores - jnp.max(scores, axis=1, keepdims=True))
+                prob = grown * (1.0 / jnp.sum(grown, axis=1, keepdims=True))
+                prob_low = prob.astype(BF)
+                self.att[there, :] = jnp.dot(prob_low, v, preferred_element_type=F32).astype(BF)
+                d_prob = lax.dot_general(d_att, v, NT, preferred_element_type=F32)
+                inner = jnp.sum(d_prob * prob, axis=1, keepdims=True)
+                d_scores = (prob * (d_prob - inner)).astype(BF)
+                d_q = jnp.dot(d_scores, k, preferred_element_type=F32) * scale
+                d_q = rotate_back(d_q, self.cos[here, :], self.sin[here, :]).astype(BF)
+                self.d_proj[there, :HEAD_W] = d_q
+                k_total[:seen, :] += lax.dot_general(d_scores, q, TN, preferred_element_type=F32)
+                v_total[:seen, :] += lax.dot_general(prob_low, d_att, TN, preferred_element_type=F32)
+            for i in range(length // TILE):
+                here = pl.ds(i * TILE, TILE)
+                there = pl.ds(base + i * TILE, TILE)
+                d_k = rotate_back(k_total[here, :] * scale, self.cos[here, :], self.sin[here, :])
+                self.d_proj[there, HEAD_W : 2 * HEAD_W] = d_k.astype(BF)
+                self.d_proj[there, 2 * HEAD_W :] = v_total[here, :].astype(BF)
+                column_sums(self.qkv_total, self.d_proj[there, :].astype(F32))
+
+        low, wide = pltpu.VMEM((length, HEAD_W), BF), pltpu.VMEM((length, HEAD_W), F32)
+        pl.run_scoped(one, low, low, low, low, wide, wide)
+
+    def dense_gradient(self):
+        def body(g, part):
+            part[...] = lax.dot_general(self.att[...], g[...], TN, preferred_element_type=F32).astype(BF)
+
+        pipe(body, D // 512, [slim(self.tokens, 512)], [slim(HEAD_W, 512)], (self.g, self.dn_part))
+
+    def qkv_gradient(self):
+        def body(n1, part):
+            part[...] = lax.dot_general(n1[...], self.d_proj[...], TN, preferred_element_type=F32).astype(BF)
+
+        pipe(body, D // TILE, [slim(self.tokens)], [tall(3 * HEAD_W)], (self.n1, self.qk_part))
+
+    def back_one(self):
+        def body(qkv, xh, part):
+            at = pl.ds(pl.multiple_of(pl.program_id(0) * TILE, TILE), TILE)
+            d_n = lax.dot_general(self.d_proj[at, :], qkv[...], NT, preferred_element_type=F32)
+            part[...] = (d_n * self.vec[0:1, :]).astype(BF)
+            column_sums(self.bias1, d_n)
+            column_sums(self.gain1, d_n * xh[...].astype(F32))
+
+        pipe(body, self.tiles, [fixed(D, 3 * HEAD_W), tall(D)], [tall(D)], (self.qkv, self.xhat, self.s1))
+
+    def expand(self):
+        def body(n2, up, hidden, slope):
+            pre = jnp.dot(n2[...], up[...], preferred_element_type=F32) + self.up_bias[...]
+            value, rise = gelu_parts(pre)
+            hidden[...] = value.astype(BF)
+            slope[...] = rise.astype(BF)
+
+        pipe(
+            body,
+            self.tiles,
+            [tall(D), fixed(D, HID_W)],
+            [tall(HID_W)] * 2,
+            (self.n2, self.up, self.hidden, self.slope),
+        )
+
+    def down_gradient(self):
+        def body(g, hidden, part):
+            part[...] = lax.dot_general(g[...], hidden[...], TN, preferred_element_type=F32).astype(BF)
+
+        pipe(
+            body,
+            D // TILE,
+            [slim(self.tokens), fixed(self.tokens, HID_W)],
+            [tall(HID_W)],
+            (self.g, self.hidden, self.wt_part),
+        )
+
+    def contract_back(self):
+        def body(g, wt, slope, d_pre):
+            d_hidden = jnp.dot(g[...], wt[...], preferred_element_type=F32)
+            low = (d_hidden * slope[...].astype(F32)).astype(BF)
+            d_pre[...] = low
+            column_sums(self.up_total, low.astype(F32))
+
+        pipe(
+            body,
+            self.tiles,
+            [tall(D), fixed(D, HID_W), tall(HID_W)],
+            [tall(HID_W)],
+            (self.g, self.wt, self.slope, self.d_pre),
+        )
+
+    def up_gradient(self):
+        def body(n2, d_pre, part):
+            part[...] = lax.dot_general(n2[...], d_pre[...], TN, preferred_element_type=F32).astype(BF)
+
+        pipe(
+            body,
+            D // TILE,
+            [slim(self.tokens), fixed(self.tokens, HID_W)],
+            [tall(HID_W)],
+            (self.n2, self.d_pre, self.up_part),
+        )
+
+    def back_two(self):
+        def body(d_pre, up, xh, s1, part):
+            d_n = lax.dot_general(d_pre[...], up[...], NT, preferred_element_type=F32)
+            part[...] = (s1[...].astype(F32) + d_n * self.vec[2:3, :]).astype(BF)
+            column_sums(self.bias2, d_n)
+            column_sums(self.gain2, d_n * xh[...].astype(F32))
+
+        pipe(
+            body,
+            self.tiles,
+            [tall(HID_W), fixed(D, HID_W), tall(D), tall(D)],
+            [tall(D)],
+            (self.d_pre, self.up, self.xhat, self.s1, self.tok_parts),
+        )
+
+    def output(self):
+        def body(hidden, dense, wt, part):
+            at = pl.ds(pl.multiple_of(pl.program_id(0) * TILE, TILE), TILE)
+            total = jnp.dot(self.att[at, :], dense[...], preferred_element_type=F32)
+            total = total + lax.dot_general(hidden[...], wt[...], NT, preferred_element_type=F32)
+            part[...] = total.astype(BF)
+
+        pipe(
+            body,
+            self.tiles,
+            [tall(HID_W), fixed(HEAD_W, D), fixed(D, HID_W)],
+            [tall(D)],
+            (self.hidden, self.dense, self.wt, self.out_parts),
+        )
+
+
 def any_spec(count):
     return [pl.BlockSpec(memory_space=pl.ANY)] * count
 
 
 def slots_needed(n_zero):
-    return 8 * n_zero + 96
-
-
-def gather_body(
-    n_zero,
-    rows,
-    x_ref,
-    g_ref,
-    dn_ref,
-    qk_ref,
-    up_ref,
-    wt_ref,
-    x_all,
-    g_all,
-    dn_all,
-    dense_own,
-    qk_all,
-    up_all,
-    wt_all,
-    send_sems,
-    recv_sems,
-    local_sems,
-):
+    return 16 * n_zero + 100
+
+
+INPUTS = ("x_own", "g_own", "dn_low", "qk_low", "up_low", "wt_low", "vec", "qkv_bias", "up_bias", "cos", "sin")
+RESULTS = ("out_sum", "tok_sum", "dn_home", "qk_home", "up_home", "wt_home")
+TOTALS = (("gain1", D), ("bias1", D), ("gain2", D), ("bias2", D), ("qkv_total", 3 * HEAD_W), ("up_total", HID_W))
+WIDTHS = (HEAD_W, 3 * HEAD_W, HID_W, HID_W)
+
+
+def buffers(tokens):
+    square = ("x", "g", "n1", "n2", "xhat", "s1", "tok_parts", "out_parts")
+    shapes = {name: (tokens, D) for name in square}
+    shapes.update({name: (tokens, HID_W) for name in ("hidden", "slope", "d_pre")})
+    shapes.update(dense=(HEAD_W, D), dn_part=(HEAD_W, D), dn_all=(D, HEAD_W), dn_cols=(D, HEAD_W))
+    shapes.update(qkv=(D, 3 * HEAD_W), qk_part=(D, 3 * HEAD_W))
+    shapes.update({name: (D, HID_W) for name in ("up", "wt", "up_part", "wt_part")})
+    return shapes
+
+
+def layer_body(n_zero, rows, tokens, *refs):
+    names = INPUTS + RESULTS + tuple(name for name, _ in TOTALS) + tuple(buffers(tokens))
+    names += ("att", "d_proj", "send_sems", "recv_sems", "local_sems", "own", "total")
+    held = dict(zip(names, refs))
+    scratch = list(refs[len(names) :])
+    take = lambda count: [scratch.pop(0) for _ in range(count)]
+    layer = Layer(held)
     place = Place(n_zero)
-    wire = Wire(send_sems, recv_sems)
+    wire = Wire(layer.send_sems, layer.recv_sems)
+    local = lambda index: layer.local_sems.at[index]
     block = rows * N_SEQ
-    pairs = ((dn_ref, dn_all), (qk_ref, qk_all), (up_ref, up_all), (wt_ref, wt_all))
-    exchanges = [SeqExchange(wire, place, send, whole, rows) for send, whole in pairs]
-    dn, qk, up, wt = [LineGather(wire, place, whole, block) for _, whole in pairs]
-    x = PlaneGather(wire, place, x_ref, x_all)
-    g = PlaneGather(wire, place, g_ref, g_all)
-    dense = DenseExchange(
-        wire,
-        place,
-        lambda c: dn_all.at[pl.ds(pl.multiple_of(c * HEAD_W, HEAD_W), HEAD_W)],
-        lambda c: dense_own.at[:, pl.ds(pl.multiple_of(c * HEAD_W, HEAD_W), HEAD_W)],
+    chunk = lambda c: pl.ds(pl.multiple_of(c * HEAD_W, HEAD_W), HEAD_W)
+
+    sources = (layer.dn_low, layer.qk_low, layer.up_low, layer.wt_low)
+    wholes = (layer.dn_all, layer.qkv, layer.up, layer.wt)
+    exchanges = [SeqExchange(wire, place, low, whole, rows) for low, whole in zip(sources, wholes)]
+    dn, qk, up, wt = [LineGather(wire, place, whole, block) for whole in wholes]
+    x = PlaneGather(wire, place, layer.x_own, layer.x)
+    g = PlaneGather(wire, place, layer.g_own, layer.g)
+    dense_in = DenseExchange(
+        wire, place, lambda c: layer.dn_all.at[chunk(c)], lambda c: layer.dense.at[:, chunk(c)]
     )
+    dense_out = DenseExchange(
+        wire, place, lambda c: layer.dn_part.at[:, chunk(c)], lambda c: layer.dn_cols.at[chunk(c)]
+    )
+    planes = []
+    for k, parts in enumerate((layer.out_parts, layer.tok_parts)):
+        mate, far, across, turned = take(4)
+        planes.append(
+            PlaneScatter(wire, place, parts, mate, far, across, turned, layer.total, layer.own, local(k))
+        )
+    out, tok = planes
+    sums, homes = [], []
+    parts = (layer.dn_cols, layer.qk_part, layer.up_part, layer.wt_part)
+    results = (layer.dn_home, layer.qk_home, layer.up_home, layer.wt_home)
+    for k, width in enumerate(WIDTHS):
+        ring, total = take(2)
+        own = take(1)[0]
+        sums.append(LineScatter(wire, place, parts[k], ring, total, own, block, local(2 + k)))
+        homes.append(Home(wire, place, total, results[k], rows))
+    dn_sum, qk_sum, up_sum, wt_sum = sums
+
+    def ahead(line, step):
+        line.take(step)
+        if step + 1 < n_zero:
+            line.pass_on(step + 1)
+
+    def rest(line, start):
+        for step in range(start, n_zero):
+            ahead(line, step)
+
+    def finish(k):
+        sums[k].last()
+        homes[k].start(local(6 + k))
+
+    def store(scatter, result):
+        scatter.last()
+        copy = pltpu.make_async_copy(scatter.total, result, scatter.sem)
+        copy.start()
+        copy.wait()
+
     place.barrier()
-    for k, exchange in enumerate(exchanges):
-        exchange.start(local_sems.at[k])
-        if k == 1:
-            x.start(local_sems.at[4])
-            g.start(local_sems.at[5])
+    layer.clear()
+    exchanges[0].start(local(6))
+    exchanges[1].start(local(7))
+    x.start(local(10))
+    g.start(local(11))
+    exchanges[2].start(local(8))
+    exchanges[3].start(local(9))
     exchanges[0].wait()
     dn.pass_on(1)
     exchanges[1].wait()
     qk.pass_on(1)
+    rest(dn, 1)
+    dense_in.start(local(6))
+    x.turn()
+    g.turn()
+    ahead(qk, 1)
     exchanges[2].wait()
     up.pass_on(1)
+    x.turn_again()
+    g.turn_again()
+    x.wait()
+    layer.normalise(0, 2)
+    ahead(qk, 2) if n_zero > 3 else None
+    layer.normalise(1, 2)
+    rest(qk, min(3, n_zero - 1))
     exchanges[3].wait()
-    x.turn()
-    g.turn()
-    for line in (dn, qk, up, wt):
-        for k in range(2, n_zero):
-            line.take(k - 1)
-            line.pass_on(k)
-        line.take(n_zero - 1)
-        if line is dn:
-            dense.start(local_sems.at[6])
-            x.turn_again()
-            g.turn_again()
-        if line is qk:
-            wt.pass_on(1)
-            x.wait()
-            g.wait()
-            dense.wait()
-    wire.finish()
-
-
-def gather(n_zero, rows, x, g, dn, qk, up, wt):
-    shape = lambda *dims: jax.ShapeDtypeStruct(dims, BF)
-    slots = slots_needed(n_zero)
-    return pl.pallas_call(
-        functools.partial(gather_body, n_zero, rows),
-        in_specs=any_spec(6),
-        out_specs=any_spec(7),
-        out_shape=[
-            shape(N_DP, N_SEQ, *x.shape),
-            shape(N_DP, N_SEQ, *g.shape),
-            shape(D, HEAD_W),
-            shape(HEAD_W, D),
-            shape(D, 3 * HEAD_W),
-            shape(D, HID_W),
-            shape(D, HID_W),
-        ],
-        scratch_shapes=[
-            pltpu.SemaphoreType.DMA((slots,)),
-            pltpu.SemaphoreType.DMA((slots,)),
-            pltpu.SemaphoreType.DMA((8,)),
-        ],
-        compiler_params=pltpu.CompilerParams(collective_id=0, has_side_effects=True),
-        name="gather",
-    )(x, g, dn, qk, up, wt)
-
-
-def scatter_body(n_zero, rows, *refs):
-    out_parts, tok_parts, dn_part, qk_part, up_part, wt_part = refs[:6]
-    out_sum, tok_sum, dn_home, qk_home, up_home, wt_home, dn_cols = refs[6:13]
-    send_sems, recv_sems, local_sems = refs[13:16]
-    scratch = list(refs[16:])
-    take = lambda count: [scratch.pop(0) for _ in range(count)]
-    place = Place(n_zero)
-    wire = Wire(send_sems, recv_sems)
-    block = rows * N_SEQ
-    plane = []
-    for k, (parts, result) in enumerate(((out_parts, out_sum), (tok_parts, tok_sum))):
-        mate, far, across, turned, total, own = take(6)
-        sem = local_sems.at[k]
-        plane.append((PlaneScatter(wire, place, parts, mate, far, across, turned, total, own, sem), result))
-    lines = []
-    pairs = ((dn_cols, dn_home), (qk_part, qk_home), (up_part, up_home), (wt_part, wt_home))
-    for k, (parts, home) in enumerate(pairs):
-        ups, downs, total, own = take(4)
-        line = LineScatter(wire, place, parts, ups, downs, total, own, block, local_sems.at[2 + k])
-        lines.append((line, Home(wire, place, total, home, rows), k))
-    dense = DenseExchange(
-        wire,
-        place,
-        lambda c: dn_part.at[:, pl.ds(pl.multiple_of(c * HEAD_W, HEAD_W), HEAD_W)],
-        lambda c: dn_cols.at[pl.ds(pl.multiple_of(c * HEAD_W, HEAD_W), HEAD_W)],
-    )
-    place.barrier()
-    dense.start(local_sems.at[6])
-    for scatter, _ in plane:
-        scatter.start()
-    dn, qk, up, wt = lines
-    todo = [(line, k) for line in (wt, up, qk, dn) for k in range(n_zero - 1)]
-    for index, (line, k) in enumerate(todo):
-        if index == 2:
-            for scatter, _ in plane:
-                scatter.turn()
-        if index == 4:
-            for scatter, _ in plane:
-                scatter.turn_again()
-        if line is dn and k == 0:
-            dense.wait()
-        line[0].step(k)
-        if k == n_zero - 2:
-            line[0].last()
-            line[1].start(local_sems.at[7 + line[2]])
-    for scatter, result in plane:
-        scatter.last()
-        copy = pltpu.make_async_copy(scatter.total, result, scatter.sem)
-        copy.start()
-        copy.wait()
-    for _, home, _ in lines:
+    g.wait()
+    dense_in.wait()
+    layer.attend(0)
+    ahead(up, 1)
+    wt.pass_on(1)
+    layer.attend(1)
+    layer.dense_gradient()
+    dense_out.start(local(7))
+    ahead(up, 2) if n_zero > 3 else None
+    layer.qkv_gradient()
+    qk_sum.advance()
+    layer.back_one()
+    rest(up, min(3, n_zero - 1))
+    ahead(wt, 1)
+    dense_out.wait()
+    dn_sum.advance()
+    layer.expand()
+    ahead(wt, 2) if n_zero > 3 else None
+    qk_sum.advance()
+    dn_sum.advance()
+    layer.down_gradient()
+    wt_sum.advance()
+    rest(wt, min(3, n_zero - 1))
+    qk_sum.advance()
+    dn_sum.advance()
+    layer.contract_back()
+    wt_sum.advance()
+    finish(0)
+    finish(1)
+    layer.up_gradient()
+    up_sum.advance()
+    wt_sum.advance()
+    layer.output()
+    out.start()
+    up_sum.advance()
+    finish(3)
+    layer.back_two()
+    tok.start()
+    out.turn()
+    up_sum.advance()
+    tok.turn()
+    out.turn_again()
+    finish(2)
+    tok.turn_again()
+    store(out, layer.out_sum)
+    store(tok, layer.tok_sum)
+    for home in homes:
         home.wait()
     wire.finish()
 
 
-def scatter(n_zero, rows, out_parts, tok_parts, dn_part, qk_part, up_part, wt_part):
-    tokens = out_parts.shape[2]
+def layer_call(n_zero, rows, tokens, *operands):
+    local = tokens // PARTS
     block = rows * N_SEQ
     slots = slots_needed(n_zero)
     vmem = lambda *dims: pltpu.VMEM(dims, BF)
-    widths = (HEAD_W, 3 * HEAD_W, HID_W, HID_W)
-    scratch = []
+    scratch = [
+        vmem(tokens, HEAD_W),
+        vmem(tokens, 3 * HEAD_W),
+        pltpu.SemaphoreType.DMA((slots,)),
+        pltpu.SemaphoreType.DMA((slots,)),
+        pltpu.SemaphoreType.DMA((12,)),
+        vmem(local, D),
+        pltpu.VMEM((local, D), F32),
+    ]
     for _ in range(2):
-        scratch += [vmem(2, 2, tokens, D), vmem(tokens, D), vmem(tokens, D), vmem(tokens, D)]
-        scratch += [pltpu.VMEM((tokens, D), F32), vmem(tokens, D)]
-    for width in widths:
-        scratch += [vmem(n_zero, block, width), vmem(n_zero, block, width)]
-        scratch += [vmem(block, width), vmem(block, width)]
+        scratch += [vmem(2, 2, local, D), vmem(local, D), vmem(local, D), vmem(local, D)]
+    for width in WIDTHS:
+        scratch += [vmem(n_zero + 1, block, width), vmem(block, width), vmem(block, width)]
+    homes = [jax.ShapeDtypeStruct((N_DP, N_SEQ, rows, width), BF) for width in WIDTHS]
+    anywhere = pl.BlockSpec(memory_space=pl.ANY)
+    vector = pl.BlockSpec(memory_space=pltpu.VMEM)
+    held = buffers(tokens)
     return pl.pallas_call(
-        functools.partial(scatter_body, n_zero, rows),
-        in_specs=any_spec(6),
-        out_specs=any_spec(7),
-        out_shape=[jax.ShapeDtypeStruct((tokens, D), F32)] * 2
-        + [jax.ShapeDtypeStruct((N_DP, N_SEQ, rows, width), BF) for width in widths]
-        + [jax.ShapeDtypeStruct((D, HEAD_W), BF)],
-        scratch_shapes=[
-            pltpu.SemaphoreType.DMA((slots,)),
-            pltpu.SemaphoreType.DMA((slots,)),
-            pltpu.SemaphoreType.DMA((12,)),
-        ]
-        + scratch,
+        functools.partial(layer_body, n_zero, rows, tokens),
+        in_specs=[anywhere] * 6 + [vector] * 5,
+        out_specs=[anywhere] * len(RESULTS) + [vector] * len(TOTALS) + [anywhere] * len(held),
+        out_shape=[jax.ShapeDtypeStruct((local, D), F32)] * 2
+        + homes
+        + [jax.ShapeDtypeStruct((8, width), F32) for _, width in TOTALS]
+        + [jax.ShapeDtypeStruct(shape, BF) for shape in held.values()],
+        scratch_shapes=scratch,
         compiler_params=pltpu.CompilerParams(
-            collective_id=1, has_side_effects=True, vmem_limit_bytes=60 * 1024 * 1024
+            collective_id=0, has_side_effects=True, vmem_limit_bytes=62 * 1024 * 1024
         ),
-        name="scatter",
-    )(out_parts, tok_parts, dn_part, qk_part, up_part, wt_part)
+        name="layer",
+    )(*operands)
 
 
 def adam_body(decay, flipped, home, param, first, second, new, first_new, second_new, grad_out):
@@ -770,73 +968,38 @@
 
         tokens_low = inputs.reshape(token_rows, D)
         grad_low = out_grad.reshape(token_rows, D)
-        tokens_all, grad_all, _, dense_own, qkv_own, up_own, wt_own = gather(
-            n_zero, rows, tokens_low, grad_low, dn_low, qk_low, up_low, wt_low
-        )
-        seqs = N_DP * seqs_here
-        length = N_SEQ * local_len
-        order = lambda value: value.reshape(N_DP, N_SEQ, seqs_here, local_len, -1).transpose(
-            0, 2, 1, 3, 4
-        ).reshape(seqs * length, -1)
-        unorder = lambda value: value.reshape(N_DP, seqs_here, N_SEQ, local_len, D).transpose(
-            0, 2, 1, 3, 4
-        ).reshape(N_DP, N_SEQ, token_rows, D)
-        tokens = order(tokens_all)
-        grads = order(grad_all)
+        tokens = N_DP * N_SEQ * token_rows
+        cosine, sine = rotary_tables(jnp.arange(tokens // N_DP).astype(F32))
+        half = ROT // 2
+        cosine = jnp.concatenate([cosine, jnp.ones((tokens // N_DP, 128 - ROT), F32)], axis=1)
+        sine = jnp.concatenate(
+            [-sine[:, :half], sine[:, half:], jnp.zeros((tokens // N_DP, 128 - ROT), F32)], axis=1
+        )
+        results = layer_call(
+            n_zero,
+            rows,
+            tokens,
+            tokens_low,
+            grad_low,
+            dn_low,
+            qk_low,
+            up_low,
+            wt_low,
+            jnp.stack([ln1_gain, ln1_bias, ln2_gain, ln2_bias]),
+            pick(qkv_bias, part_i, 1).reshape(1, 3 * HEAD_W),
+            pick(up_bias, part_i, 0).reshape(1, HID_W),
+            cosine,
+            sine,
+        )
+        out_sum, d_xhat, dn_home, qk_home, up_home, wt_home = results[: len(RESULTS)]
+        totals = [jnp.sum(total, axis=0) for total in results[len(RESULTS) : len(RESULTS) + len(TOTALS)]]
+        d_gain_one, d_bias_one, d_gain_two, d_bias_two, d_qkv_bias, d_up_bias = totals
 
         def statistics(values):
             average = jnp.mean(values, axis=-1, keepdims=True)
             centred = values - average
             spread = jnp.mean(centred * centred, axis=-1, keepdims=True)
             return centred, lax.rsqrt(spread + NORM_EPSILON)
-
-        centred, rate = statistics(tokens.astype(F32))
-        xhat = centred * rate
-        normed_one = (xhat * ln1_gain + ln1_bias).astype(BF)
-        normed_two = (xhat * ln2_gain + ln2_bias).astype(BF)
-
-        projected = jnp.dot(normed_one, qkv_own, preferred_element_type=F32)
-        projected = projected + pick(qkv_bias, part_i, 1).reshape(3 * HEAD_W)
-        d_att = lax.dot_general(grads, dense_own, NT, preferred_element_type=F32).astype(BF)
-        attended, d_proj = attention(
-            projected.reshape(seqs, length, 3 * HEAD_W), d_att.reshape(seqs, length, HEAD_W)
-        )
-        attended = attended.reshape(seqs * length, HEAD_W)
-        d_proj = d_proj.reshape(seqs * length, 3 * HEAD_W)
-        d_qkv_bias = jnp.sum(d_proj.astype(F32), axis=0)
-        d_normed_one = lax.dot_general(d_proj, qkv_own, NT, preferred_element_type=F32)
-        qk_part = lax.dot_general(normed_one, d_proj, TN, preferred_element_type=F32).astype(BF)
-        dn_part = lax.dot_general(attended, grads, TN, preferred_element_type=F32).astype(BF)
-
-        pre_act = jnp.dot(normed_two, up_own, preferred_element_type=F32) + pick(up_bias, part_i, 0)
-        hidden_wide, slope = gelu_parts(pre_act)
-        hidden = hidden_wide.astype(BF)
-        wt_part = lax.dot_general(grads, hidden, TN, preferred_element_type=F32).astype(BF)
-        d_hidden = jnp.dot(grads, wt_own, preferred_element_type=F32)
-        d_pre = (d_hidden * slope).astype(BF)
-        d_up_bias = jnp.sum(d_pre.astype(F32), axis=0)
-        up_part = lax.dot_general(normed_two, d_pre, TN, preferred_element_type=F32).astype(BF)
-        d_normed_two = lax.dot_general(d_pre, up_own, NT, preferred_element_type=F32)
-
-        out_part = jnp.dot(attended, dense_own, preferred_element_type=F32) + lax.dot_general(
-            hidden, wt_own, NT, preferred_element_type=F32
-        )
-        d_gain_one = jnp.sum(d_normed_one * xhat, axis=0)
-        d_bias_one = jnp.sum(d_normed_one, axis=0)
-        d_gain_two = jnp.sum(d_normed_two * xhat, axis=0)
-        d_bias_two = jnp.sum(d_normed_two, axis=0)
-        tok_part = d_normed_one * ln1_gain + d_normed_two * ln2_gain
-
-        out_sum, d_xhat, dn_home, qk_home, up_home, wt_home, _ = scatter(
-            n_zero,
-            rows,
-            unorder(out_part.astype(BF)),
-            unorder(tok_part.astype(BF)),
-            dn_part,
-            qk_part,
-            up_part,
-            wt_part,
-        )
 
         tokens_wide = tokens_low.astype(F32)
         grad_wide = grad_low.astype(F32)

time: 918 us -> 698 us (0.76)
  matrix products: 139 us -> 0 us
  Pallas kernels: 598 us -> 524 us
  waiting for transfers between devices: 66.4 us -> 95.2 us
  other arithmetic: 41.5 us -> 20 us
  local copies, waits for them, and re-layouts: 27.5 us -> 15.6 us
    dot_general x12 -> x0, matrix products: 139 us -> none  [the longest x1 22.9 us: body(): lax.dot_general(d_pre, up_own, NT, preferred_element_type=F32)]
    pallas_call x3 -> x1, Pallas kernels: 551 us -> 476 us  [layer_call(): pl.pallas_call(functools.partial(layer_body, n_zero, rows, tokens), in_sp...]
    psum x1, waiting for transfers between devices: 66.4 us -> 95.2 us  [body(): vector_sum = lax.psum(vector_local, everywhere)]
    convert_element_type x3 -> x1, other arithmetic: 12.8 us -> 0.01 us  [body(): cosine, sine = rotary_tables(jnp.arange(tokens // N_DP).astype(F32))]
    unnamed x102 -> x50, local copies, waits for them, and re-layouts: 11.3 us -> 2.12 us
  transfers between devices with their start and end apart: 1 -> 1, of which waited for: 1 -> 1; matrix products, arithmetic and copies ran while one was open for 0% -> 0% of each run, Pallas kernels for 5% -> 7%
where the time goes in v3:
time: 698 us; the launch traced here: 693 us
  Pallas kernels  524 us (75%)
  waiting for transfers between devices  95.2 us (14%)
  blocking collectives  23.4 us (3%)
  other arithmetic  20 us (3%)
  local copies, waits for them, and re-layouts  15.6 us (2%)
  between operations  14.6 us (2%)
    pallas_call x1, Pallas kernels, layer_call(): pl.pallas_call(functools.partial(layer_body, n_zero, rows, tokens), in_sp...  476 us
    psum x1, waiting for transfers between devices, body(): vector_sum = lax.psum(vector_local, everywhere)  95.2 us
    pallas_call x4, Pallas kernels, adam(): pl.pallas_call(functools.partial(adam_body, WEIGHT_DECAY, flipped), grid=...  48.3 us
    all_gather x1, blocking collectives, body(): lax.all_gather(vectors.astype(BF), ('zero', 'seq'), axis=0, tiled=True)  23.4 us
  transfers between devices with their start and end apart: 1, of which 1 were waited for; matrix products, arithmetic and copies ran while one was open for 0% of the time, Pallas kernels for 7%

profile of v3, /device:TPU:0, one launch (start us, length us, event | category | flops | bytes accessed | tf_op | source)
XLA Modules:
  0.0 693.0 jit_solution(13649754388027338733)
XLA Ops:
  8.0 23.4 %all-gather = bf16[16,1,1664]{2,1,0:T(2,128)(2,1)S(1)} all-gather(bf16[1,1,1664]{2,1,0:T(2,128)(2,1)S(1)} %reshape.152), channel_id=1, replica_groups=mesh['dp'=2,'zero'=4,'seq'=4] {'zero','seq'}, dimensions={0}, use_global_device_ids=true | all-gather | bytes 56576 | tf_op jit(solution)/shard_map/all_gather | solution.py:948
  31.5 2.1 fusion.19
  34.2 0.9 copy.57
  35.3 0.9 copy.53
  37.5 0.9 copy.51
  38.4 1.7 constant_dynamic-slice_fusion.2
  40.8 1.3 copy.59
  42.1 1.7 dynamic-slice_convert_fusion
  43.8 1.3 copy.60
  45.3 2.2 fusion.14
  48.9 0.9 pad_maximum_fusion.refs_3_
  49.8 1.0 maximum_maximum_fusion.refs_10_
  51.5 475.8 %layer.1 = (f32[256,2048]{1,0:T(8,128)}, f32[256,2048]{1,0:T(8,128)}, bf16[2,4,128,256]{3,2,1,0:T(8,128)(2,1)}, bf16[2,4,128,768]{3,2,1,0:T(8,128)(2,1)}, bf16[2...) custom-call(bf16[256,2048]{1,0:T(8,128)(2,1)} %bitcast.37, ...), custom_call_target="tpu_custom_call" | custom-call | tf_op jit(solution)/shard_map/layer/pallas_call | solution.py:871
  527.3 0.9 reduce_sum.103
  528.2 0.9 reduce_sum.104
  530.2 1.7 fusion.7
  531.9 2.4 fusion.17
  534.4 5.7 convert_reduce_fusion.1
  541.0 13.6 %adam.6 = (f32[128,8192]{1,0:T(8,128)}, f32[128,8192]{1,0:T(8,128)}, f32[128,8192]{1,0:T(8,128)}, f32[128,8192]{1,0:T(8,128)}) custom-call(bf16[2,4,128,1024]{3,2,1,0:T(8,128)(2,1)S(1)} %copy-done.2, f32[128,8192]{1,0:T(8,128)} %param.40, f32[128,8192]{1,0:T(8,128)} %first.6, f32[128,8192]{1,0:T(8,128)} %second.6), custom_call_target="tpu_custom_call" | custom-call | tf_op jit(solution)/shard_map/adam/pallas_call | solution.py:902
  554.7 14.0 %adam.7 = (f32[8192,128]{1,0:T(8,128)}, f32[8192,128]{1,0:T(8,128)}, f32[8192,128]{1,0:T(8,128)}, f32[8192,128]{1,0:T(8,128)}) custom-call(bf16[2,4,128,1024]{3,2,1,0:T(8,128)(2,1)S(1)} %copy-done.1, f32[8192,128]{1,0:T(8,128)} %param.41, f32[8192,128]{1,0:T(8,128)} %first.7, f32[8192,128]{1,0:T(8,128)} %second.7), custom_call_target="tpu_custom_call" | custom-call | tf_op jit(solution)/shard_map/adam/pallas_call | solution.py:902
  568.7 16.8 %adam.4 = (f32[128,6144]{1,0:T(8,128)}, f32[128,6144]{1,0:T(8,128)}, f32[128,6144]{1,0:T(8,128)}, f32[128,6144]{1,0:T(8,128)}) custom-call(bf16[2,4,128,768]{3,2,1,0:T(8,128)(2,1)S(1)} %copy-done.4, f32[128,6144]{1,0:T(8,128)S(1)} %copy-done, f32[128,6144]{1,0:T(8,128)} %first.4, f32[128,6144]{1,0:T(8,128)} %second.4), custom_call_target="tpu_custom_call" | custom-call | tf_op jit(solution)/shard_map/adam/pallas_call | solution.py:902
  585.6 3.9 adam.5
  589.5 95.2 %all-reduce.3.cloned.1.call-done = f32[26624]{0:T(1024)} async-done(((f32[26624]{0:T(1024)}), f32[26624]{0:T(1024)}) %all-reduce.3.cloned.1.call-update) | async-done | bytes 106512 | tf_op jit(solution)/shard_map/psum | solution.py:1032
  684.7 1.4 multiply_subtract_fusion
  (87 shorter events, 7.9 us)
Async XLA Ops:
  7.2 677.5 %all-reduce.3.cloned.1.call-start = ((), (), s32[]{:S(2)}) async-start(), calls=%async_computation | async-start | bytes 212992 | tf_op jit(solution)/shard_map/psum | solution.py:1032
  33.6 1.4 copy-start.3
  45.1 2.7 copy-start.8
  47.5 1.4 copy-start.9
  47.5 1.4 copy-start.10
  530.2 4.1 copy-start.13
  530.2 4.2 copy-start.12
  530.2 4.2 copy-start.14
  534.4 6.6 copy-start.2
  540.3 0.7 copy-start.11
  541.0 13.7 %copy-start.1 = (bf16[2,4,128,1024]{3,2,1,0:T(8,128)(2,1)S(1)}, bf16[2,4,128,1024]{3,2,1,0:T(8,128)(2,1)}, u32[]{:S(2)}) copy-start(bf16[2,4,128,1024]{3,2,1,0:T(8,128)(2,1)} %get-tuple-element.64.home) | copy-start | bytes 6291460
  554.7 14.0 %copy-start = (f32[128,6144]{1,0:T(8,128)S(1)}, f32[128,6144]{1,0:T(8,128)}, u32[]{:S(2)}) copy-start(f32[128,6144]{1,0:T(8,128)} %param.38) | copy-start | bytes 9437188
  554.7 14.0 %copy-start.4 = (bf16[2,4,128,768]{3,2,1,0:T(8,128)(2,1)S(1)}, bf16[2,4,128,768]{3,2,1,0:T(8,128)(2,1)}, u32[]{:S(2)}) copy-start(bf16[2,4,128,768]{3,2,1,0:T(8,128)(2,1)} %get-tuple-element.58.home) | copy-start | bytes 4718596
  568.7 16.9 %copy-start.5 = (f32[128,2048]{1,0:T(8,128)S(1)}, f32[128,2048]{1,0:T(8,128)}, u32[]{:S(2)}) copy-start(f32[128,2048]{1,0:T(8,128)} %first.5) | copy-start | bytes 3145732
  568.7 16.9 %copy-start.6 = (f32[128,2048]{1,0:T(8,128)S(1)}, f32[128,2048]{1,0:T(8,128)}, u32[]{:S(2)}) copy-start(f32[128,2048]{1,0:T(8,128)} %second.5) | copy-start | bytes 3145732
  568.7 16.9 %copy-start.7 = (bf16[2,4,128,256]{3,2,1,0:T(8,128)(2,1)S(1)}, bf16[2,4,128,256]{3,2,1,0:T(8,128)(2,1)}, u32[]{:S(2)}) copy-start(bf16[2,4,128,256]{3,2,1,0:T(8,128)(2,1)} %get-tuple-element.60.home) | copy-start | bytes 1572868
  585.5 99.2 %copy-start.15 = (f32[1664]{0:T(1024)S(1)}, f32[1664]{0:T(1024)}, u32[]{:S(2)}) copy-start(f32[1664]{0:T(1024)} %param.23) | copy-start | bytes 19972
  585.5 99.2 %copy-start.16 = (f32[1664]{0:T(1024)S(1)}, f32[1664]{0:T(1024)}, u32[]{:S(2)}) copy-start(f32[1664]{0:T(1024)} %param.28) | copy-start | bytes 19972
  585.5 99.2 %copy-start.17 = (f32[1664]{0:T(1024)S(1)}, f32[1664]{0:T(1024)}, u32[]{:S(2)}) copy-start(f32[1664]{0:T(1024)} %param.33) | copy-start | bytes 19972
Sparse Core Ops, SparseCore 0:
  541.1 143.5 all-reduce.2

commit v4 on v3

--- a/solution.py
+++ b/solution.py
@@ -3,6 +3,7 @@
 
 import jax
 import jax.numpy as jnp
+import numpy as np
 from jax import lax
 from jax.experimental import pallas as pl
 from jax.experimental.pallas import tpu as pltpu
@@ -33,15 +34,6 @@
 TN = (((0,), (0,)), ((), ()))
 
 
-def rotary_tables(positions):
-    half_rot = ROT // 2
-    exponent = jnp.arange(half_rot, dtype=F32) * (2.0 / ROT)
-    inverse = jnp.power(10000.0, -exponent)
-    angles = positions[:, None] * inverse[None, :]
-    angles = jnp.concatenate([angles, angles], axis=1)
-    return (jnp.cos(angles), jnp.sin(angles))
-
-
 def adam_step(parameter, gradient, first_moment, second, decay_rate):
     first_new = BETA_ONE * first_moment + (1.0 - BETA_ONE) * gradient
     second_new = BETA_TWO * second + (1.0 - BETA_TWO) * gradient * gradient
@@ -135,22 +127,32 @@
     def block(self, index):
         return self.whole.at[pl.ds(pl.multiple_of(index * self.rows, self.rows), self.rows)]
 
-    def take(self, step):
-        p = self.place
-        self.wire.receive(self.ups[step - 1], self.block(jnp.maximum(p.z - step, 0)), p.below, p.z >= step)
-        self.wire.receive(
-            self.downs[step - 1], self.block(jnp.minimum(p.z + step, p.n - 1)), p.above, p.z + step < p.n
-        )
-
-    def pass_on(self, step):
-        p = self.place
-        up, down = jnp.maximum(p.z - step + 1, 0), jnp.minimum(p.z + step - 1, p.n - 1)
-        self.wire.send(
-            self.ups[step - 1], self.block(up), self.block(up), p.above, (p.z < p.n - 1) & (p.z >= step - 1)
-        )
-        self.wire.send(
-            self.downs[step - 1], self.block(down), self.block(down), p.below, (p.z > 0) & (p.z + step <= p.n)
-        )
+    def send_up(self, step, block, when):
+        self.wire.send(self.ups[step - 1], block, block, self.place.above, when)
+
+    def send_down(self, step, block, when):
+        self.wire.send(self.downs[step - 1], block, block, self.place.below, when)
+
+    def own_from_ends(self):
+        p = self.place
+        self.send_up(1, self.block(p.z), p.z == 0)
+        self.send_down(1, self.block(p.z), p.z == p.n - 1)
+
+    def own_from_middle(self):
+        p = self.place
+        middle = (p.z > 0) & (p.z < p.n - 1)
+        self.send_up(1, self.block(p.z), middle)
+        self.send_down(1, self.block(p.z), middle)
+
+    def ahead(self, step):
+        p = self.place
+        up, down = self.block(jnp.maximum(p.z - step, 0)), self.block(jnp.minimum(p.z + step, p.n - 1))
+        self.wire.receive(self.ups[step - 1], up, p.below, p.z >= step)
+        if step + 1 < p.n:
+            self.send_up(step + 1, up, (p.z < p.n - 1) & (p.z >= step))
+        self.wire.receive(self.downs[step - 1], down, p.above, p.z + step < p.n)
+        if step + 1 < p.n:
+            self.send_down(step + 1, down, (p.z > 0) & (p.z + step < p.n))
 
 
 class SeqExchange:
@@ -243,7 +245,8 @@
 class LineScatter:
     def __init__(self, wire, place, parts, held, total, own, rows, sem):
         self.wire, self.place, self.parts, self.rows = wire, place, parts, rows
-        self.held, self.total, self.own, self.sem, self.slot = held, total, own, sem, 0
+        self.held, self.total, self.own, self.sem = held, total, own, sem
+        self.launched, self.advanced = 0, 1
         self.up_slots = [wire.slot() for _ in range(place.n)]
         self.down_slots = [wire.slot() for _ in range(place.n)]
 
@@ -253,40 +256,46 @@
     def fetch(self, j, target):
         return pltpu.make_async_copy(self.part(j), target, self.sem)
 
-    def advance(self):
-        p, slot = self.place, self.slot
-        self.slot = slot + 1
+    def launch(self, k):
+        p = self.place
         top = p.n - 1
-        up = jnp.minimum(top - slot + p.z, top)
-        self.hop(up, up + 1, self.up_slots[0] + up, p.above, p.below, p.z <= slot, p.z == 0)
-        down = jnp.maximum(slot - top + p.z, 0)
-        self.hop(down, down, self.down_slots[0] + down, p.below, p.above, top - p.z <= slot, p.z == top)
-
-    def hop(self, j, index, slot, onto, source, active, first):
+        up, down = top - k, k
+        self.wire.send(
+            self.up_slots[up], self.part(up), self.held.at[up + 1], p.above, p.z == 0
+        )
+        self.wire.send(
+            self.down_slots[down], self.part(down), self.held.at[down], p.below, p.z == top
+        )
+        self.launched = k + 1
+
+    def advance(self, k):
+        p = self.place
+        top = p.n - 1
+        up = jnp.minimum(top - k + p.z, top)
+        self.hop(up, up + 1, self.up_slots[0] + up, p.above, p.below, (p.z > 0) & (p.z <= k))
+        down = jnp.maximum(k - top + p.z, 0)
+        self.hop(down, down, self.down_slots[0] + down, p.below, p.above, (p.z < top) & (top - p.z <= k))
+        self.advanced = k + 1
+
+    def hop(self, j, index, slot, onto, source, active):
         held = self.held.at[index]
 
         def go():
-            @pl.when(first)
-            def _():
-                copy = self.fetch(j, held)
-                copy.start()
-                copy.wait()
-
-            @pl.when(jnp.logical_not(first))
-            def _():
-                copy = self.fetch(j, self.own)
-                copy.start()
-                self.wire.receive(slot, held, source)
-                copy.wait()
-                add_rows(held, held, self.own)
+            copy = self.fetch(j, self.own)
+            copy.start()
+            self.wire.receive(slot, held, source)
+            copy.wait()
+            add_rows(held, held, self.own)
 
         pl.when(active)(go)
         self.wire.send(slot, held, held, onto, active)
 
     def last(self):
         p = self.place
-        while self.slot < p.n - 1:
-            self.advance()
+        for k in range(self.launched, p.n - 1):
+            self.launch(k)
+        for k in range(self.advanced, p.n - 1):
+            self.advance(k)
         copy = self.fetch(p.z, self.own)
         copy.start()
         copy.wait()
@@ -508,7 +517,7 @@
                 n2[at, :] = (xhat * self.vec[2:3, :] + self.vec[3:4, :]).astype(BF)
                 return carry
 
-            lax.fori_loop(0, TILE // 32, some, 0)
+            lax.fori_loop(0, TILE // 32, some, 0, unroll=4)
 
         pipe(
             body,
@@ -688,11 +697,11 @@
 
 
 def slots_needed(n_zero):
-    return 16 * n_zero + 100
-
-
-INPUTS = ("x_own", "g_own", "dn_low", "qk_low", "up_low", "wt_low", "vec", "qkv_bias", "up_bias", "cos", "sin")
-RESULTS = ("out_sum", "tok_sum", "dn_home", "qk_home", "up_home", "wt_home")
+    return 20 * n_zero + 120
+
+
+INPUTS = ("x_own", "g_own", "dn_low", "qk_low", "up_low", "wt_low", "vec_own", "out_bias", "cos", "sin")
+RESULTS = ("out_sum", "tok_sum", "dn_home", "qk_home", "up_home", "wt_home", "vec_all", "vec_sums")
 TOTALS = (("gain1", D), ("bias1", D), ("gain2", D), ("bias2", D), ("qkv_total", 3 * HEAD_W), ("up_total", HID_W))
 WIDTHS = (HEAD_W, 3 * HEAD_W, HID_W, HID_W)
 
@@ -707,9 +716,82 @@
     return shapes
 
 
+VEC_ROWS = 16
+CHUNK = 128
+
+
+class VectorGather:
+    def __init__(self, wire, place, own, whole):
+        self.wire, self.place, self.own, self.whole = wire, place, own, whole
+        self.slots = [wire.slot() for _ in range(1, N_SEQ)]
+        self.line = LineGather(wire, place, whole, N_SEQ)
+
+    def target(self, s):
+        return self.whole.at[pl.ds(self.place.z * N_SEQ + s, 1)]
+
+    def start(self, local_sem):
+        p = self.place
+        for step in range(1, N_SEQ):
+            self.wire.send(self.slots[step - 1], self.own, self.target(p.s), {"seq": lax.rem(p.s + step, N_SEQ)})
+        self.copied = pltpu.make_async_copy(self.own, self.target(p.s), local_sem)
+        self.copied.start()
+
+    def wait(self):
+        p = self.place
+        for step in range(1, N_SEQ):
+            source = lax.rem(p.s - step + N_SEQ, N_SEQ)
+            self.wire.receive(self.slots[step - 1], self.target(source), {"seq": source})
+        self.copied.wait()
+
+
+def lay_out_vectors(layer, place):
+    rows = layer.vec_all.shape[1]
+
+
+    def piece(q):
+        shard, row = (q // rows, q % rows) if isinstance(q, int) else (lax.div(q, rows), lax.rem(q, rows))
+        return layer.vec_all[shard, pl.ds(row, 1), :]
+
+    count = D // CHUNK
+    for row, first in enumerate((0, count, 6 * count, 7 * count)):
+        for i in range(count):
+            layer.vec[row : row + 1, i * CHUNK : (i + 1) * CHUNK] = piece(first + i)
+    each = HEAD_W // CHUNK
+    for t in range(3):
+        for i in range(each):
+            at = t * HEAD_W + i * CHUNK
+            layer.qkv_bias[:, at : at + CHUNK] = piece((2 + t) * count + place.part * each + i)
+    each = HID_W // CHUNK
+    for i in range(each):
+        layer.up_bias[:, i * CHUNK : (i + 1) * CHUNK] = piece(8 * count + place.part * each + i)
+
+
+def partial_vectors(layer):
+    fold = lambda total: jnp.sum(total[...], axis=0, keepdims=True)
+    rows = [fold(total) for total in (layer.gain1, layer.bias1, layer.gain2, layer.bias2)]
+    rows.append(layer.out_bias[...])
+    wide = jnp.concatenate(rows + [jnp.zeros((3, D), F32)], axis=0)
+    for c in range(PARTS):
+        layer.pieces_out[c] = wide[:, c * HEAD_W : (c + 1) * HEAD_W]
+
+
+def own_vectors(layer, own):
+    total = layer.pieces_in[0]
+    for c in range(1, PARTS):
+        total = total + layer.pieces_in[c]
+    own[pl.ds(0, 8), :] = total
+    qkv = jnp.sum(layer.qkv_total[...], axis=0, keepdims=True)
+    up = jnp.sum(layer.up_total[...], axis=0, keepdims=True)
+    cut = lambda row, count: [row[:, i * HEAD_W : (i + 1) * HEAD_W] for i in range(count)]
+    rows = cut(qkv, 3) + cut(up, 4) + [jnp.zeros((1, HEAD_W), F32)]
+    own[pl.ds(8, 8), :] = jnp.concatenate(rows, axis=0)
+
+
 def layer_body(n_zero, rows, tokens, *refs):
-    names = INPUTS + RESULTS + tuple(name for name, _ in TOTALS) + tuple(buffers(tokens))
+    names = INPUTS + RESULTS + tuple(buffers(tokens))
     names += ("att", "d_proj", "send_sems", "recv_sems", "local_sems", "own", "total")
+    names += ("vec", "qkv_bias", "up_bias", "pieces_out", "pieces_in", "vec_line", "vec_total")
+    names += tuple(name for name, _ in TOTALS)
     held = dict(zip(names, refs))
     scratch = list(refs[len(names) :])
     take = lambda count: [scratch.pop(0) for _ in range(count)]
@@ -749,15 +831,6 @@
         homes.append(Home(wire, place, total, results[k], rows))
     dn_sum, qk_sum, up_sum, wt_sum = sums
 
-    def ahead(line, step):
-        line.take(step)
-        if step + 1 < n_zero:
-            line.pass_on(step + 1)
-
-    def rest(line, start):
-        for step in range(start, n_zero):
-            ahead(line, step)
-
     def finish(k):
         sums[k].last()
         homes[k].start(local(6 + k))
@@ -768,81 +841,160 @@
         copy.start()
         copy.wait()
 
+    alone = layer.vec_all.shape[0] == 1
+    gather = None if alone else VectorGather(wire, place, layer.vec_own, layer.vec_all)
+
+    def vector_in_start():
+        if not alone:
+            gather.start(local(18))
+
+    def vector_in_pass():
+        if not alone:
+            gather.wait()
+            gather.line.own_from_ends()
+            gather.line.own_from_middle()
+
+    def vector_in_rest():
+        if alone:
+            copy = pltpu.make_async_copy(layer.vec_own, layer.vec_all, local(18))
+            copy.start()
+            copy.wait()
+        else:
+            for step in range(1, n_zero):
+                gather.line.ahead(step)
+        lay_out_vectors(layer, place)
+
+    pieces = DenseExchange(
+        wire, place, lambda c: layer.pieces_out.at[c], lambda c: layer.pieces_in.at[c]
+    )
+    vector_line = LineGather(wire, place, layer.vec_line, VEC_ROWS)
+    vector_spread = DenseExchange(
+        wire, place, lambda c: layer.vec_total, lambda c: layer.vec_sums.at[c]
+    )
+
+    def vector_out_start():
+        partial_vectors(layer)
+        pieces.start(local(18))
+
+    def vector_out_pass():
+        pieces.wait()
+        own = vector_line.block(place.z)
+        own_vectors(layer, own)
+        vector_line.own_from_ends()
+        vector_line.own_from_middle()
+
+    def vector_out_spread():
+        total = layer.vec_line[pl.ds(0, VEC_ROWS), :]
+        for j in range(1, n_zero):
+            total = total + layer.vec_line[pl.ds(j * VEC_ROWS, VEC_ROWS), :]
+        layer.vec_total[...] = total
+        vector_spread.start(local(19))
+
     place.barrier()
     layer.clear()
-    exchanges[0].start(local(6))
-    exchanges[1].start(local(7))
+    exchanges[0].start(local(12))
+    vector_in_start()
+    exchanges[2].start(local(14))
     x.start(local(10))
+    exchanges[0].wait()
+    dn.own_from_ends()
+    dn.own_from_middle()
+    vector_in_pass()
+    dn.ahead(1)
+    exchanges[2].wait()
+    up.own_from_ends()
+    exchanges[1].start(local(13))
+    up.own_from_middle()
+    dn.ahead(2)
+    x.turn()
     g.start(local(11))
-    exchanges[2].start(local(8))
-    exchanges[3].start(local(9))
-    exchanges[0].wait()
-    dn.pass_on(1)
-    exchanges[1].wait()
-    qk.pass_on(1)
-    rest(dn, 1)
-    dense_in.start(local(6))
-    x.turn()
-    g.turn()
-    ahead(qk, 1)
-    exchanges[2].wait()
-    up.pass_on(1)
+    up.ahead(1)
+    exchanges[3].start(local(15))
+    vector_in_rest()
     x.turn_again()
-    g.turn_again()
+    up.ahead(2)
     x.wait()
     layer.normalise(0, 2)
-    ahead(qk, 2) if n_zero > 3 else None
+    exchanges[1].wait()
+    qk.own_from_ends()
+    qk.own_from_middle()
+    for step in range(3, n_zero):
+        dn.ahead(step)
     layer.normalise(1, 2)
-    rest(qk, min(3, n_zero - 1))
+    g.turn()
+    for step in range(3, n_zero):
+        up.ahead(step)
+    layer.expand()
     exchanges[3].wait()
+    wt.own_from_ends()
+    qk.ahead(1)
+    g.turn_again()
     g.wait()
+    layer.down_gradient()
+    dense_in.start(local(16))
+    qk.ahead(2)
+    wt_sum.launch(0)
+    for step in range(3, n_zero):
+        qk.ahead(step)
+    wt.own_from_middle()
     dense_in.wait()
     layer.attend(0)
-    ahead(up, 1)
-    wt.pass_on(1)
+    wt_sum.launch(1)
+    wt.ahead(1)
+    wt_sum.launch(2)
     layer.attend(1)
+    wt_sum.advance(1)
+    layer.qkv_gradient()
     layer.dense_gradient()
-    dense_out.start(local(7))
-    ahead(up, 2) if n_zero > 3 else None
-    layer.qkv_gradient()
-    qk_sum.advance()
+    qk_sum.launch(0)
+    qk_sum.launch(1)
+    wt.ahead(2)
+    qk_sum.launch(2)
+    dense_out.start(local(17))
     layer.back_one()
-    rest(up, min(3, n_zero - 1))
-    ahead(wt, 1)
+    for step in range(3, n_zero):
+        wt.ahead(step)
     dense_out.wait()
-    dn_sum.advance()
-    layer.expand()
-    ahead(wt, 2) if n_zero > 3 else None
-    qk_sum.advance()
-    dn_sum.advance()
-    layer.down_gradient()
-    wt_sum.advance()
-    rest(wt, min(3, n_zero - 1))
-    qk_sum.advance()
-    dn_sum.advance()
+    wt_sum.advance(2)
     layer.contract_back()
-    wt_sum.advance()
+    layer.output()
+    dn_sum.launch(0)
+    out.start()
+    finish(3)
+    layer.up_gradient()
+    up_sum.launch(0)
+    out.turn()
+    qk_sum.advance(1)
+    dn_sum.launch(1)
+    layer.back_two()
+    up_sum.launch(1)
+    out.turn_again()
+    homes[3].wait()
+    dn_sum.advance(1)
+    tok.start()
+    qk_sum.advance(2)
+    tok.turn()
+    vector_out_start()
+    dn_sum.launch(2)
+    up_sum.advance(1)
+    dn_sum.advance(2)
+    tok.turn_again()
+    up_sum.launch(2)
+    up_sum.advance(2)
+    store(out, layer.out_sum)
+    vector_out_pass()
+    finish(1)
     finish(0)
-    finish(1)
-    layer.up_gradient()
-    up_sum.advance()
-    wt_sum.advance()
-    layer.output()
-    out.start()
-    up_sum.advance()
-    finish(3)
-    layer.back_two()
-    tok.start()
-    out.turn()
-    up_sum.advance()
-    tok.turn()
-    out.turn_again()
+    store(tok, layer.tok_sum)
     finish(2)
-    tok.turn_again()
-    store(out, layer.out_sum)
-    store(tok, layer.tok_sum)
-    for home in homes:
-        home.wait()
+    vector_line.ahead(1)
+    for step in range(2, n_zero):
+        vector_line.ahead(step)
+    vector_out_spread()
+    homes[2].wait()
+    homes[0].wait()
+    homes[1].wait()
+    vector_spread.wait()
     wire.finish()
 
 
@@ -850,16 +1002,21 @@
     local = tokens // PARTS
     block = rows * N_SEQ
     slots = slots_needed(n_zero)
+    shards = (9 * D + FF) // (operands[6].shape[1] * CHUNK)
     vmem = lambda *dims: pltpu.VMEM(dims, BF)
     scratch = [
         vmem(tokens, HEAD_W),
         vmem(tokens, 3 * HEAD_W),
         pltpu.SemaphoreType.DMA((slots,)),
         pltpu.SemaphoreType.DMA((slots,)),
-        pltpu.SemaphoreType.DMA((12,)),
+        pltpu.SemaphoreType.DMA((20,)),
         vmem(local, D),
         pltpu.VMEM((local, D), F32),
     ]
+    wide = lambda *dims: pltpu.VMEM(dims, F32)
+    scratch += [wide(4, D), wide(1, 3 * HEAD_W), wide(1, HID_W), wide(PARTS, 8, HEAD_W)]
+    scratch += [wide(PARTS, 8, HEAD_W), wide(n_zero * VEC_ROWS, HEAD_W), wide(VEC_ROWS, HEAD_W)]
+    scratch += [wide(8, width) for _, width in TOTALS]
     for _ in range(2):
         scratch += [vmem(2, 2, local, D), vmem(local, D), vmem(local, D), vmem(local, D)]
     for width in WIDTHS:
@@ -870,11 +1027,14 @@
     held = buffers(tokens)
     return pl.pallas_call(
         functools.partial(layer_body, n_zero, rows, tokens),
-        in_specs=[anywhere] * 6 + [vector] * 5,
-        out_specs=[anywhere] * len(RESULTS) + [vector] * len(TOTALS) + [anywhere] * len(held),
+        in_specs=[anywhere] * 7 + [vector] * 3,
+        out_specs=[anywhere] * (len(RESULTS) - 2) + [vector] * 2 + [anywhere] * len(held),
         out_shape=[jax.ShapeDtypeStruct((local, D), F32)] * 2
         + homes
-        + [jax.ShapeDtypeStruct((8, width), F32) for _, width in TOTALS]
+        + [
+            jax.ShapeDtypeStruct((shards,) + operands[6].shape[1:], F32),
+            jax.ShapeDtypeStruct((PARTS, VEC_ROWS, HEAD_W), F32),
+        ]
         + [jax.ShapeDtypeStruct(shape, BF) for shape in held.values()],
         scratch_shapes=scratch,
         compiler_params=pltpu.CompilerParams(
@@ -885,9 +1045,10 @@
 
 
 def adam_body(decay, flipped, home, param, first, second, new, first_new, second_new, grad_out):
-    gradient = home[0, 0].astype(F32)
     if flipped:
-        gradient = gradient.T
+        gradient = home[0, 0].astype(F32).T
+    else:
+        gradient = jnp.concatenate([home[0, k] for k in range(home.shape[1])], axis=1).astype(F32)
     updated = adam_step(param[...], gradient, first[...], second[...], decay)
     new[...], first_new[...], second_new[...] = updated
     grad_out[...] = gradient
@@ -895,15 +1056,18 @@
 
 def adam(home, pieces, param, first, second, flipped=False):
     rows, width = home.shape[2], home.shape[3] // pieces
+    together = max(1, min(N_SEQ, HID_W // width))
+    groups = PARTS // together
     if flipped:
-        block = pl.BlockSpec((width, rows), lambda c, t: (t * PARTS + c, 0))
+        block = pl.BlockSpec((width, rows), lambda c, t: (c, 0))
     else:
-        block = pl.BlockSpec((rows, width), lambda c, t: (0, t * PARTS + c))
+        block = pl.BlockSpec((rows, width * together), lambda c, t: (0, t * groups + c))
+    each = N_SEQ // together
     return pl.pallas_call(
         functools.partial(adam_body, WEIGHT_DECAY, flipped),
-        grid=(PARTS, pieces),
+        grid=(groups, pieces),
         in_specs=[
-            pl.BlockSpec((1, 1, rows, width), lambda c, t: (c // N_SEQ, c % N_SEQ, 0, t)),
+            pl.BlockSpec((1, together, rows, width), lambda c, t: (c // each, c % each, 0, t)),
             block,
             block,
             block,
@@ -913,6 +1077,17 @@
         compiler_params=pltpu.CompilerParams(vmem_limit_bytes=48 * 1024 * 1024),
         name="adam",
     )(home, param, first, second)
+
+
+def rotary_rows(length):
+    exponent = np.arange(ROT // 2, dtype=np.float32) * np.float32(2.0 / ROT)
+    inverse = np.power(np.float32(10000.0), -exponent)
+    angles = np.arange(length, dtype=np.float32)[:, None] * inverse[None, :]
+    cosine, sine = np.cos(angles), np.sin(angles)
+    ones = np.ones((length, 128 - ROT), np.float32)
+    cosine = np.concatenate([cosine, cosine, ones], axis=1)
+    sine = np.concatenate([-sine, sine, 0.0 * ones], axis=1)
+    return jnp.asarray(cosine), jnp.asarray(sine)
 
 
 def make_body(sizes):
@@ -939,19 +1114,9 @@
         down_second,
     ):
         dp_i, zero_i, seq_i = (lax.axis_index(axis) for axis in everywhere)
-        part_i = dp_i * N_SEQ + seq_i
         seqs_here, local_len = inputs.shape[0], inputs.shape[1]
         token_rows = seqs_here * local_len
         rows = qkv_weight.shape[0]
-        pick = lambda value, index, axis: lax.dynamic_index_in_dim(value, index, axis, keepdims=False)
-
-        vec_all = lax.all_gather(vectors.astype(BF), ("zero", "seq"), axis=0, tiled=True).astype(F32)
-        ln1_gain, ln1_bias = vec_all[:D], vec_all[D : 2 * D]
-        qkv_bias = vec_all[2 * D : 5 * D].reshape(3, PARTS, HEAD_W)
-        dense_bias = vec_all[5 * D : 6 * D]
-        ln2_gain, ln2_bias = vec_all[6 * D : 7 * D], vec_all[7 * D : 8 * D]
-        up_bias = vec_all[8 * D : 8 * D + FF].reshape(PARTS, HID_W)
-        down_bias = vec_all[8 * D + FF :]
 
         def columns(value, width):
             wide = value.shape[1] // N_DP
@@ -969,12 +1134,13 @@
         tokens_low = inputs.reshape(token_rows, D)
         grad_low = out_grad.reshape(token_rows, D)
         tokens = N_DP * N_SEQ * token_rows
-        cosine, sine = rotary_tables(jnp.arange(tokens // N_DP).astype(F32))
-        half = ROT // 2
-        cosine = jnp.concatenate([cosine, jnp.ones((tokens // N_DP, 128 - ROT), F32)], axis=1)
-        sine = jnp.concatenate(
-            [-sine[:, :half], sine[:, half:], jnp.zeros((tokens // N_DP, 128 - ROT), F32)], axis=1
-        )
+        grad_wide = grad_low.astype(F32)
+        d_out_bias = jnp.sum(grad_wide, axis=0, keepdims=True)
+        vec_low = lax.reduce_precision(vectors, exponent_bits=8, mantissa_bits=7)
+        if vectors.shape[0] % CHUNK == 0:
+            vec_low = vec_low.reshape(1, -1, CHUNK)
+        else:
+            vec_low = lax.all_gather(vec_low, ("zero", "seq"), axis=0, tiled=True).reshape(1, -1, CHUNK)
         results = layer_call(
             n_zero,
             rows,
@@ -985,15 +1151,13 @@
             qk_low,
             up_low,
             wt_low,
-            jnp.stack([ln1_gain, ln1_bias, ln2_gain, ln2_bias]),
-            pick(qkv_bias, part_i, 1).reshape(1, 3 * HEAD_W),
-            pick(up_bias, part_i, 0).reshape(1, HID_W),
-            cosine,
-            sine,
-        )
-        out_sum, d_xhat, dn_home, qk_home, up_home, wt_home = results[: len(RESULTS)]
-        totals = [jnp.sum(total, axis=0) for total in results[len(RESULTS) : len(RESULTS) + len(TOTALS)]]
-        d_gain_one, d_bias_one, d_gain_two, d_bias_two, d_qkv_bias, d_up_bias = totals
+            vec_low,
+            d_out_bias,
+            *rotary_rows(tokens // N_DP),
+        )
+        out_sum, d_xhat, dn_home, qk_home, up_home, wt_home, vec_all, vec_sums = results[: len(RESULTS)]
+        vec_flat = vec_all.reshape(-1)
+        dense_bias, down_bias = vec_flat[5 * D : 6 * D], vec_flat[8 * D + FF : 9 * D + FF]
 
         def statistics(values):
             average = jnp.mean(values, axis=-1, keepdims=True)
@@ -1002,7 +1166,6 @@
             return centred, lax.rsqrt(spread + NORM_EPSILON)
 
         tokens_wide = tokens_low.astype(F32)
-        grad_wide = grad_low.astype(F32)
         outputs = (tokens_wide + out_sum + dense_bias + down_bias).astype(BF).reshape(inputs.shape)
         centred_own, rate_own = statistics(tokens_wide)
         xhat_own = centred_own * rate_own
@@ -1013,23 +1176,19 @@
         )
         input_grad = (grad_wide + d_tokens).astype(BF).reshape(inputs.shape)
 
-        d_out_bias = jnp.sum(grad_wide, axis=0)
-        place_in = lambda value, count: lax.dynamic_update_index_in_dim(
-            jnp.zeros((value.shape[0], count, value.shape[1]), F32), value, part_i, 1
-        ).reshape(-1)
-        vector_local = jnp.concatenate(
+        row = lambda k: vec_sums[:, k].reshape(-1)
+        vector_sum = jnp.concatenate(
             [
-                d_gain_one,
-                d_bias_one,
-                place_in(d_qkv_bias.reshape(3, HEAD_W), PARTS),
-                d_out_bias,
-                d_gain_two,
-                d_bias_two,
-                place_in(d_up_bias.reshape(1, HID_W), PARTS),
-                d_out_bias,
+                row(0),
+                row(1),
+                vec_sums[:, 8:11].transpose(1, 0, 2).reshape(-1),
+                row(4),
+                row(2),
+                row(3),
+                vec_sums[:, 11:15].reshape(-1),
+                row(4),
             ]
         )
-        vector_sum = lax.psum(vector_local, everywhere)
         vectors_grad = lax.dynamic_slice_in_dim(
             vector_sum, (zero_i * N_SEQ + seq_i) * vectors.shape[0], vectors.shape[0], 0
         )

time: 698 us -> 472 us (0.68)
  waiting for transfers between devices: 95.2 us -> 0 us
  Pallas kernels: 524 us -> 440 us
  blocking collectives: 23.4 us -> 0 us
  between operations: 14.6 us -> 1.05 us
  other arithmetic: 20 us -> 11.9 us
    psum x1 -> x0, waiting for transfers between devices: 95.2 us -> none  [body(): vector_sum = lax.psum(vector_local, everywhere)]
    pallas_call x1, Pallas kernels: 476 us -> 400 us  [layer_call(): pl.pallas_call(functools.partial(layer_body, n_zero, rows, tokens), in_sp...]
    all_gather x1 -> x0, blocking collectives: 23.4 us -> none  [body(): lax.all_gather(vectors.astype(BF), ('zero', 'seq'), axis=0, tiled=True)]
    pallas_call x4, Pallas kernels: 48.3 us -> 39.7 us  [adam(): pl.pallas_call(functools.partial(adam_body, WEIGHT_DECAY, flipped), grid=...]
    reduce_sum x7 -> x1, other arithmetic: 8.27 us -> 0.77 us  [body(): d_out_bias = jnp.sum(grad_wide, axis=0, keepdims=True)]
  transfers between devices with their start and end apart: 1 -> 0, of which waited for: 1 -> 0; matrix products, arithmetic and copies ran while one was open for 0% -> 0% of each run, Pallas kernels for 7% -> 0%
where the time goes in v4:
time: 472 us; the launch traced here: 467 us
  Pallas kernels  440 us (93%)
  local copies, waits for them, and re-layouts  14.5 us (3%)
  other arithmetic  11.9 us (3%)
    pallas_call x1, Pallas kernels, layer_call(): pl.pallas_call(functools.partial(layer_body, n_zero, rows, tokens), in_sp...  400 us
    pallas_call x4, Pallas kernels, adam(): pl.pallas_call(functools.partial(adam_body, WEIGHT_DECAY, flipped), grid=...  39.7 us

profile of v4, /device:TPU:0, one launch (start us, length us, event | category | flops | bytes accessed | tf_op | source)
XLA Modules:
  0.0 467.4 jit_solution(9475446486653469930)
XLA Ops:
  0.7 2.1 fusion.17
  3.4 0.5 copy-done.3
  4.4 0.9 pad_maximum_fusion.refs_3_
  5.5 0.9 copy.42
  6.3 1.7 constant_dynamic-slice_fusion
  8.0 0.7 copy.60
  8.7 1.3 copy.50
  10.0 1.8 dynamic-slice_convert_fusion
  11.8 1.3 copy.51
  13.1 0.8 convert_reduce_fusion.1
  13.9 0.6 reduce-precision_bitcast_fusion.refs_6_
  14.5 400.3 %layer.1 = (f32[256,2048]{1,0:T(8,128)}, f32[256,2048]{1,0:T(8,128)}, bf16[2,4,128,256]{3,2,1,0:T(8,128)(2,1)}, bf16[2,4,128,768]{3,2,1,0:T(8,128)(2,1)}, bf16[2...) custom-call(bf16[256,2048]{1,0:T(8,128)(2,1)} %bitcast.42, ...), custom_call_target="tpu_custom_call" | custom-call | tf_op jit(solution)/shard_map/layer/pallas_call | solution.py:1028
  414.8 1.2 fusion.18
  416.1 0.8 slice_bitcast_fusion.1
  417.0 0.8 slice_bitcast_fusion
  417.9 0.7 multiply_subtract_fusion
  418.6 1.4 convert_reduce_fusion
  420.1 0.4 fusion.7
  420.6 2.1 fusion.15
  422.7 4.9 %fusion.13 = (bf16[1,256,2048]{2,1,0:T(8,128)(2,1)}, bf16[1,256,2048]{2,1,0:T(8,128)(2,1)}) fusion(f32[256,2048]{1,0:T(8,128)} %get-tuple-element.48, f32[256]{0:T(256)S(1)} %broadcast_multiply_fusion, f32[256]{0:T(256)S(1)} %broadcast_multiply_fusion.1, f32[256]{0:T(256)S(1)} %add_rsqrt_fusion, f32[256]{0:T(256)S(1)} %broadcast_multiply_fusion.2, ...), kind=kLoop, calls=%fused_computation.19 | loop fusion | flops 7340032 | bytes 8409088 | tf_op jit(solution)/shard_map/reshape | solution.py:1177
  427.6 13.6 %adam.6 = (f32[128,8192]{1,0:T(8,128)}, f32[128,8192]{1,0:T(8,128)}, f32[128,8192]{1,0:T(8,128)}, f32[128,8192]{1,0:T(8,128)}) custom-call(bf16[2,4,128,1024]{3,2,1,0:T(8,128)(2,1)S(1)} %copy-done.2, f32[128,8192]{1,0:T(8,128)} %param.42, f32[128,8192]{1,0:T(8,128)} %first.6, f32[128,8192]{1,0:T(8,128)} %second.6), custom_call_target="tpu_custom_call" | custom-call | tf_op jit(solution)/shard_map/adam/pallas_call | solution.py:1066
  441.3 14.0 %adam.7 = (f32[8192,128]{1,0:T(8,128)}, f32[8192,128]{1,0:T(8,128)}, f32[8192,128]{1,0:T(8,128)}, f32[8192,128]{1,0:T(8,128)}) custom-call(bf16[2,4,128,1024]{3,2,1,0:T(8,128)(2,1)S(1)} %copy-done.1, f32[8192,128]{1,0:T(8,128)} %param.43, f32[8192,128]{1,0:T(8,128)} %first.7, f32[8192,128]{1,0:T(8,128)} %second.7), custom_call_target="tpu_custom_call" | custom-call | tf_op jit(solution)/shard_map/adam/pallas_call | solution.py:1066
  455.3 9.5 %adam.4 = (f32[128,6144]{1,0:T(8,128)}, f32[128,6144]{1,0:T(8,128)}, f32[128,6144]{1,0:T(8,128)}, f32[128,6144]{1,0:T(8,128)}) custom-call(bf16[2,4,128,768]{3,2,1,0:T(8,128)(2,1)S(1)} %copy-done.4, f32[128,6144]{1,0:T(8,128)S(1)} %copy-done, f32[128,6144]{1,0:T(8,128)} %first.4, f32[128,6144]{1,0:T(8,128)} %second.4), custom_call_target="tpu_custom_call" | custom-call | tf_op jit(solution)/shard_map/adam/pallas_call | solution.py:1066
  464.8 2.6 adam.5
  (55 shorter events, 1.4 us)
Async XLA Ops:
  2.7 1.2 copy-start.3
  10.0 3.1 copy-start.9
  11.8 2.1 copy-start.12
  14.5 403.4 %copy-start.13 = (f32[1664]{0:T(1024)S(1)}, f32[1664]{0:T(1024)}, u32[]{:S(2)}) copy-start(f32[1664]{0:T(1024)} %param.30) | copy-start | bytes 19972
  14.5 403.4 %copy-start.14 = (f32[1664]{0:T(1024)S(1)}, f32[1664]{0:T(1024)}, u32[]{:S(2)}) copy-start(f32[1664]{0:T(1024)} %param.35) | copy-start | bytes 19972
  414.8 5.3 %copy-start.8 = (bf16[1,256,2048]{2,1,0:T(8,128)(2,1)S(1)}, bf16[1,256,2048]{2,1,0:T(8,128)(2,1)}, u32[]{:S(2)}) copy-start(bf16[1,256,2048]{2,1,0:T(8,128)(2,1)} %param.23) | copy-start | bytes 3145732
  420.1 2.6 copy-start.11
  420.1 2.6 copy-start.10
  422.7 4.9 %copy-start.2 = (bf16[2,4,128,1024]{3,2,1,0:T(8,128)(2,1)S(1)}, bf16[2,4,128,1024]{3,2,1,0:T(8,128)(2,1)}, u32[]{:S(2)}) copy-start(bf16[2,4,128,1024]{3,2,1,0:T(8,128)(2,1)} %get-tuple-element.54.home) | copy-start | bytes 6291460
  427.6 13.6 %copy-start.1 = (bf16[2,4,128,1024]{3,2,1,0:T(8,128)(2,1)S(1)}, bf16[2,4,128,1024]{3,2,1,0:T(8,128)(2,1)}, u32[]{:S(2)}) copy-start(bf16[2,4,128,1024]{3,2,1,0:T(8,128)(2,1)} %get-tuple-element.56.home) | copy-start | bytes 6291460
  441.3 14.0 %copy-start = (f32[128,6144]{1,0:T(8,128)S(1)}, f32[128,6144]{1,0:T(8,128)}, u32[]{:S(2)}) copy-start(f32[128,6144]{1,0:T(8,128)} %param.40) | copy-start | bytes 9437188
  441.3 14.0 %copy-start.4 = (bf16[2,4,128,768]{3,2,1,0:T(8,128)(2,1)S(1)}, bf16[2,4,128,768]{3,2,1,0:T(8,128)(2,1)}, u32[]{:S(2)}) copy-start(bf16[2,4,128,768]{3,2,1,0:T(8,128)(2,1)} %get-tuple-element.50.home) | copy-start | bytes 4718596
  455.3 9.5 %copy-start.5 = (f32[128,2048]{1,0:T(8,128)S(1)}, f32[128,2048]{1,0:T(8,128)}, u32[]{:S(2)}) copy-start(f32[128,2048]{1,0:T(8,128)} %first.5) | copy-start | bytes 3145732
  455.3 9.5 %copy-start.6 = (f32[128,2048]{1,0:T(8,128)S(1)}, f32[128,2048]{1,0:T(8,128)}, u32[]{:S(2)}) copy-start(f32[128,2048]{1,0:T(8,128)} %second.5) | copy-start | bytes 3145732
  455.3 9.5 %copy-start.7 = (bf16[2,4,128,256]{3,2,1,0:T(8,128)(2,1)S(1)}, bf16[2,4,128,256]{3,2,1,0:T(8,128)(2,1)}, u32[]{:S(2)}) copy-start(bf16[2,4,128,256]{3,2,1,0:T(8,128)(2,1)} %get-tuple-element.52.home) | copy-start | bytes 1572868

commit v5 on v4

--- a/solution.py
+++ b/solution.py
@@ -326,12 +326,17 @@
         self.wire, self.place, self.total, self.home, self.rows = wire, place, total, home, rows
         self.slots = [wire.slot() for _ in range(1, N_DP * N_SEQ)]
 
+    def target(self, dp, s):
+        return self.home.at[dp, s]
+
+    def piece(self, s):
+        return self.total.at[pl.ds(pl.multiple_of(s * self.rows, self.rows), self.rows)]
+
     def start(self, local_sem):
         p = self.place
-        piece = lambda s: self.total.at[pl.ds(pl.multiple_of(s * self.rows, self.rows), self.rows)]
         for step, dp, s, device in p.others():
-            self.wire.send(self.slots[step - 1], piece(s), self.home.at[p.dp, p.s], device)
-        self.copied = pltpu.make_async_copy(piece(p.s), self.home.at[p.dp, p.s], local_sem)
+            self.wire.send(self.slots[step - 1], self.piece(s), self.target(p.dp, p.s), device)
+        self.copied = pltpu.make_async_copy(self.piece(p.s), self.target(p.dp, p.s), local_sem)
         self.copied.start()
 
     def wait(self):
@@ -340,7 +345,7 @@
         for step in range(1, parts):
             at = lax.rem(p.part - step + parts, parts)
             dp, s = lax.div(at, N_SEQ), lax.rem(at, N_SEQ)
-            self.wire.receive(self.slots[step - 1], self.home.at[dp, s], {"dp": dp, "seq": s})
+            self.wire.receive(self.slots[step - 1], self.target(dp, s), {"dp": dp, "seq": s})
         self.copied.wait()
 
 
@@ -1054,17 +1059,14 @@
     grad_out[...] = gradient
 
 
-def adam(home, pieces, param, first, second, flipped=False):
+def adam(home, pieces, param, first, second):
     rows, width = home.shape[2], home.shape[3] // pieces
     together = max(1, min(N_SEQ, HID_W // width))
     groups = PARTS // together
-    if flipped:
-        block = pl.BlockSpec((width, rows), lambda c, t: (c, 0))
-    else:
-        block = pl.BlockSpec((rows, width * together), lambda c, t: (0, t * groups + c))
+    block = pl.BlockSpec((rows, width * together), lambda c, t: (0, t * groups + c))
     each = N_SEQ // together
     return pl.pallas_call(
-        functools.partial(adam_body, WEIGHT_DECAY, flipped),
+        functools.partial(adam_body, WEIGHT_DECAY, False),
         grid=(groups, pieces),
         in_specs=[
             pl.BlockSpec((1, together, rows, width), lambda c, t: (c // each, c % each, 0, t)),
@@ -1077,6 +1079,56 @@
         compiler_params=pltpu.CompilerParams(vmem_limit_bytes=48 * 1024 * 1024),
         name="adam",
     )(home, param, first, second)
+
+
+def adam_pair_body(decay, *refs):
+    adam_body(decay, False, *refs[0:4], *refs[8:12])
+    adam_body(decay, True, *refs[4:8], *refs[12:16])
+
+
+def adam_pair(up_home, up, wt_home, down):
+    rows, width = up_home.shape[2:]
+    home = pl.BlockSpec((1, 1, rows, width), lambda c: (c // N_SEQ, c % N_SEQ, 0, 0))
+    columns = pl.BlockSpec((rows, width), lambda c: (0, c))
+    tall_rows = pl.BlockSpec((width, rows), lambda c: (c, 0))
+    results = pl.pallas_call(
+        functools.partial(adam_pair_body, WEIGHT_DECAY),
+        grid=(PARTS,),
+        in_specs=[home] + [columns] * 3 + [home] + [tall_rows] * 3,
+        out_specs=[columns] * 4 + [tall_rows] * 4,
+        out_shape=[jax.ShapeDtypeStruct(up[0].shape, F32)] * 4 + [jax.ShapeDtypeStruct(down[0].shape, F32)] * 4,
+        compiler_params=pltpu.CompilerParams(vmem_limit_bytes=56 * 1024 * 1024),
+        name="adam_pair",
+    )(up_home, *up, wt_home, *down)
+    return results[:4], results[4:]
+
+
+def pack_body(half, *refs):
+    dense, query, key, value, up, down, dn_low, qk_low, up_low, wt_low = refs
+    dn_low[0] = dense[...].astype(BF)
+    qk_low[0] = jnp.concatenate([query[...], key[...], value[...]], axis=1).astype(BF)
+    up_low[0] = up[...].astype(BF)
+    wt_low[0] = down[...].T.astype(BF)
+
+
+def pack(half, qkv_weight, dense_weight, up_weight, down_weight):
+    rows = qkv_weight.shape[0]
+    columns = lambda width, t: pl.BlockSpec((rows, width), lambda s, h: (0, t * PARTS + h[0] * N_SEQ + s))
+    widths = (HEAD_W, 3 * HEAD_W, HID_W, HID_W)
+    return pl.pallas_call(
+        pack_body,
+        grid_spec=pltpu.PrefetchScalarGridSpec(
+            num_scalar_prefetch=1,
+            grid=(N_SEQ,),
+            in_specs=[columns(HEAD_W, 0)]
+            + [columns(HEAD_W, t) for t in range(3)]
+            + [columns(HID_W, 0), pl.BlockSpec((HID_W, rows), lambda s, h: (h[0] * N_SEQ + s, 0))],
+            out_specs=[pl.BlockSpec((1, rows, width), lambda s, h: (s, 0, 0)) for width in widths],
+        ),
+        out_shape=[jax.ShapeDtypeStruct((N_SEQ, rows, width), BF) for width in widths],
+        compiler_params=pltpu.CompilerParams(vmem_limit_bytes=48 * 1024 * 1024),
+        name="pack",
+    )(half, dense_weight, qkv_weight, qkv_weight, qkv_weight, up_weight, down_weight)
 
 
 def rotary_rows(length):
@@ -1118,19 +1170,9 @@
         token_rows = seqs_here * local_len
         rows = qkv_weight.shape[0]
 
-        def columns(value, width):
-            wide = value.shape[1] // N_DP
-            half = lax.dynamic_slice_in_dim(value, dp_i * wide, wide, 1).astype(BF)
-            return half.reshape(rows, N_SEQ, width).transpose(1, 0, 2)
-
-        qk_low = jnp.concatenate(
-            [columns(qkv_weight[:, t * D : (t + 1) * D], HEAD_W) for t in range(3)], axis=2
-        )
-        dn_low = columns(dense_weight, HEAD_W)
-        up_low = columns(up_weight, HID_W)
-        wt_low = lax.dynamic_slice_in_dim(down_weight, dp_i * (FF // N_DP), FF // N_DP, 0).astype(BF)
-        wt_low = wt_low.reshape(N_SEQ, HID_W, rows).transpose(0, 2, 1)
-
+        dn_low, qk_low, up_low, wt_low = pack(
+            dp_i.astype(jnp.int32).reshape(1), qkv_weight, dense_weight, up_weight, down_weight
+        )
         tokens_low = inputs.reshape(token_rows, D)
         grad_low = out_grad.reshape(token_rows, D)
         tokens = N_DP * N_SEQ * token_rows
@@ -1196,8 +1238,12 @@
         vec_upd = adam_step(vectors, vectors_grad, vectors_first, vectors_second, 0.0) + (vectors_grad,)
         qkv_upd = adam(qk_home, 3, qkv_weight, qkv_first, qkv_second)
         dense_upd = adam(dn_home, 1, dense_weight, dense_first, dense_second)
-        up_upd = adam(up_home, 1, up_weight, up_first, up_second)
-        down_upd = adam(wt_home, 1, down_weight, down_first, down_second, flipped=True)
+        up_upd, down_upd = adam_pair(
+            up_home,
+            (up_weight, up_first, up_second),
+            wt_home,
+            (down_weight, down_first, down_second),
+        )
         updates = (vec_upd, qkv_upd, dense_upd, up_upd, down_upd)
         picked = lambda k: tuple(update[k] for update in updates)
         return (outputs, input_grad) + picked(3) + picked(0) + picked(1) + picked(2)

time: 472 us -> 463 us (0.981)
  local copies, waits for them, and re-layouts: 14.5 us -> 7.8 us
where the time goes in v5:
time: 463 us; the launch traced here: 459 us
  Pallas kernels  441 us (95%)
  other arithmetic  9.59 us (2%)
  local copies, waits for them, and re-layouts  7.8 us (2%)
    pallas_call x1, Pallas kernels, layer_call(): pl.pallas_call(functools.partial(layer_body, n_zero, rows, tokens), in_sp...  400 us
    pallas_call x1, Pallas kernels, adam_pair(): pl.pallas_call(functools.partial(adam_pair_body, WEIGHT_DECAY), grid=(PAR...  24.6 us
    pallas_call x2, Pallas kernels, adam(): pl.pallas_call(functools.partial(adam_body, WEIGHT_DECAY, False), grid=(g...  12.1 us

profile of v5, /device:TPU:0, one launch (start us, length us, event | category | flops | bytes accessed | tf_op | source)
XLA Modules:
  0.0 459.0 jit_solution(17810033966573624421)
XLA Ops:
  0.7 0.0 copy-start.1
  0.7 1.2 copy-done.1
  1.9 3.7 pack.1
  5.6 0.0 copy-start.6
  5.6 1.0 copy-done.6
  6.6 1.0 copy-done.7
  7.5 0.9 copy-done.8
  8.4 0.7 copy-done.10
  9.1 0.8 convert_reduce_fusion.1
  9.9 0.6 reduce-precision_bitcast_fusion.refs_6_
  10.5 400.3 %layer.1 = (f32[256,2048]{1,0:T(8,128)}, f32[256,2048]{1,0:T(8,128)}, bf16[2,4,128,256]{3,2,1,0:T(8,128)(2,1)}, bf16[2,4,128,768]{3,2,1,0:T(8,128)(2,1)}, bf16[2...) custom-call(bf16[256,2048]{1,0:T(8,128)(2,1)} %bitcast.31, ...), custom_call_target="tpu_custom_call" | custom-call | tf_op jit(solution)/shard_map/layer/pallas_call | solution.py:1033
  410.8 0.0 copy-start.13
  410.8 1.2 fusion.17
  412.1 0.8 slice_bitcast_fusion.1
  413.0 0.8 slice_bitcast_fusion
  413.9 0.7 multiply_subtract_fusion
  414.6 0.2 convert_reduce_fusion
  414.8 0.4 fusion.7
  415.3 2.1 fusion.15
  417.4 4.7 %fusion.13 = (bf16[1,256,2048]{2,1,0:T(8,128)(2,1)}, bf16[1,256,2048]{2,1,0:T(8,128)(2,1)}) fusion(f32[256,2048]{1,0:T(8,128)} %get-tuple-element.56, f32[256]{0:T(256)S(1)} %get-tuple-element.93, f32[256]{0:T(256)S(1)} %get-tuple-element.94, f32[256]{0:T(256)S(1)} %add_rsqrt_fusion, f32[256]{0:T(256)S(1)} %broadcast_multiply_fusion.2, ...), kind=kLoop, calls=%fused_computation.18 | loop fusion | flops 7340032 | bytes 8409088 | tf_op jit(solution)/shard_map/reshape | solution.py:1219
  422.2 24.6 %adam_pair.1 = (f32[128,8192]{1,0:T(8,128)}, f32[128,8192]{1,0:T(8,128)}, f32[128,8192]{1,0:T(8,128)}, f32[128,8192]{1,0:T(8,128)}, f32[8192,128]{1,0:T(8,128)},...) custom-call(bf16[2,4,128,1024]{3,2,1,0:T(8,128)(2,1)} %get-tuple-element.62.refs_0_, ...), custom_call_target="tpu_custom_call" | custom-call | tf_op jit(solution)/shard_map/adam_pair/pallas_call | solution.py:1094
  446.8 0.0 copy-start.2
  446.8 9.5 %adam.2 = (f32[128,6144]{1,0:T(8,128)}, f32[128,6144]{1,0:T(8,128)}, f32[128,6144]{1,0:T(8,128)}, f32[128,6144]{1,0:T(8,128)}) custom-call(bf16[2,4,128,768]{3,2,1,0:T(8,128)(2,1)S(1)} %copy-done.3, f32[128,6144]{1,0:T(8,128)S(1)} %copy-done, f32[128,6144]{1,0:T(8,128)} %first.2, f32[128,6144]{1,0:T(8,128)} %second.2), custom_call_target="tpu_custom_call" | custom-call | tf_op jit(solution)/shard_map/adam/pallas_call | solution.py:1068
  456.3 2.6 adam.3
  (43 shorter events, 0.2 us)
Async XLA Ops:
  0.7 1.2 copy-start.1
  1.9 7.2 %copy-start.12 = (bf16[1,256,2048]{2,1,0:T(8,128)(2,1)S(1)}, bf16[1,256,2048]{2,1,0:T(8,128)(2,1)}, u32[]{:S(2)}) copy-start(bf16[1,256,2048]{2,1,0:T(8,128)(2,1)} %param.22) | copy-start | bytes 3145732
  1.9 8.0 %copy-start.15 = (f32[1664]{0:T(1024)S(1)}, f32[1664]{0:T(1024)}, u32[]{:S(2)}) copy-start(f32[1664]{0:T(1024)} %param.23) | copy-start | bytes 19972
  5.6 1.0 copy-start.6
  6.6 1.0 copy-start.7
  7.5 0.9 copy-start.8
  8.4 0.7 copy-start.10
  10.5 403.4 %copy-start.16 = (f32[1664]{0:T(1024)S(1)}, f32[1664]{0:T(1024)}, u32[]{:S(2)}) copy-start(f32[1664]{0:T(1024)} %param.28) | copy-start | bytes 19972
  10.5 403.4 %copy-start.17 = (f32[1664]{0:T(1024)S(1)}, f32[1664]{0:T(1024)}, u32[]{:S(2)}) copy-start(f32[1664]{0:T(1024)} %param.33) | copy-start | bytes 19972
  10.5 404.1 %copy-start.11 = (bf16[1,256,2048]{2,1,0:T(8,128)(2,1)S(1)}, bf16[1,256,2048]{2,1,0:T(8,128)(2,1)}, u32[]{:S(2)}) copy-start(bf16[1,256,2048]{2,1,0:T(8,128)(2,1)} %param.21) | copy-start | bytes 3145732
  410.8 6.6 %copy-start.14 = (f32[16,13,128]{2,1,0:T(8,128)S(1)}, f32[16,13,128]{2,1,0:T(8,128)}, u32[]{:S(2)}) copy-start(f32[16,13,128]{2,1,0:T(8,128)} %get-tuple-element.55) | copy-start | bytes 319492
  410.8 6.6 %copy-start.13 = (bf16[1,256,2048]{2,1,0:T(8,128)(2,1)S(1)}, bf16[1,256,2048]{2,1,0:T(8,128)(2,1)}, u32[]{:S(2)}) copy-start(bf16[1,256,2048]{2,1,0:T(8,128)(2,1)} %param.22) | copy-start | bytes 3145732
  422.2 24.6 %copy-start = (f32[128,6144]{1,0:T(8,128)S(1)}, f32[128,6144]{1,0:T(8,128)}, u32[]{:S(2)}) copy-start(f32[128,6144]{1,0:T(8,128)} %param.38) | copy-start | bytes 9437188
  422.2 24.6 %copy-start.3 = (bf16[2,4,128,768]{3,2,1,0:T(8,128)(2,1)S(1)}, bf16[2,4,128,768]{3,2,1,0:T(8,128)(2,1)}, u32[]{:S(2)}) copy-start(bf16[2,4,128,768]{3,2,1,0:T(8,128)(2,1)} %get-tuple-element.58.home) | copy-start | bytes 4718596
  446.8 9.5 %copy-start.2 = (f32[128,2048]{1,0:T(8,128)S(1)}, f32[128,2048]{1,0:T(8,128)}, u32[]{:S(2)}) copy-start(f32[128,2048]{1,0:T(8,128)} %param.39) | copy-start | bytes 3145732
  446.8 9.5 %copy-start.4 = (f32[128,2048]{1,0:T(8,128)S(1)}, f32[128,2048]{1,0:T(8,128)}, u32[]{:S(2)}) copy-start(f32[128,2048]{1,0:T(8,128)} %first.3) | copy-start | bytes 3145732
  446.8 9.5 %copy-start.5 = (f32[128,2048]{1,0:T(8,128)S(1)}, f32[128,2048]{1,0:T(8,128)}, u32[]{:S(2)}) copy-start(f32[128,2048]{1,0:T(8,128)} %second.3) | copy-start | bytes 3145732
  446.8 9.5 %copy-start.9 = (bf16[2,4,128,256]{3,2,1,0:T(8,128)(2,1)S(1)}, bf16[2,4,128,256]{3,2,1,0:T(8,128)(2,1)}, u32[]{:S(2)}) copy-start(bf16[2,4,128,256]{3,2,1,0:T(8,128)(2,1)} %get-tuple-element.60.home) | copy-start | bytes 1572868

commit v6 on v5

--- a/solution.py
+++ b/solution.py
@@ -322,12 +322,13 @@
 
 
 class Home:
-    def __init__(self, wire, place, total, home, rows):
+    def __init__(self, wire, place, total, home, first, width, rows):
         self.wire, self.place, self.total, self.home, self.rows = wire, place, total, home, rows
+        self.columns = pl.ds(first, width)
         self.slots = [wire.slot() for _ in range(1, N_DP * N_SEQ)]
 
     def target(self, dp, s):
-        return self.home.at[dp, s]
+        return self.home.at[dp, s, :, self.columns]
 
     def piece(self, s):
         return self.total.at[pl.ds(pl.multiple_of(s * self.rows, self.rows), self.rows)]
@@ -702,13 +703,14 @@
 
 
 def slots_needed(n_zero):
-    return 20 * n_zero + 120
+    return 28 * n_zero + 160
 
 
 INPUTS = ("x_own", "g_own", "dn_low", "qk_low", "up_low", "wt_low", "vec_own", "out_bias", "cos", "sin")
 RESULTS = ("out_sum", "tok_sum", "dn_home", "qk_home", "up_home", "wt_home", "vec_all", "vec_sums")
 TOTALS = (("gain1", D), ("bias1", D), ("gain2", D), ("bias2", D), ("qkv_total", 3 * HEAD_W), ("up_total", HID_W))
-WIDTHS = (HEAD_W, 3 * HEAD_W, HID_W, HID_W)
+HALF_W = HID_W // 2
+WIDTHS = (HEAD_W, 3 * HEAD_W, HALF_W, HALF_W, HALF_W, HALF_W)
 
 
 def buffers(tokens):
@@ -773,8 +775,7 @@
 
 def partial_vectors(layer):
     fold = lambda total: jnp.sum(total[...], axis=0, keepdims=True)
-    rows = [fold(total) for total in (layer.gain1, layer.bias1, layer.gain2, layer.bias2)]
-    rows.append(layer.out_bias[...])
+    rows = [fold(total) for total in (layer.gain1, layer.bias1, layer.gain2, layer.bias2, layer.out_bias)]
     wide = jnp.concatenate(rows + [jnp.zeros((3, D), F32)], axis=0)
     for c in range(PARTS):
         layer.pieces_out[c] = wide[:, c * HEAD_W : (c + 1) * HEAD_W]
@@ -827,18 +828,19 @@
         )
     out, tok = planes
     sums, homes = [], []
-    parts = (layer.dn_cols, layer.qk_part, layer.up_part, layer.wt_part)
-    results = (layer.dn_home, layer.qk_home, layer.up_home, layer.wt_home)
+    part_half = lambda ref, k: ref.at[:, pl.ds(k * HALF_W, HALF_W)]
+    parts = [layer.dn_cols, layer.qk_part]
+    parts += [part_half(ref, k) for ref in (layer.up_part, layer.wt_part) for k in (0, 1)]
+    results = [(layer.dn_home, 0), (layer.qk_home, 0)]
+    results += [(home, k * HALF_W) for home in (layer.up_home, layer.wt_home) for k in (0, 1)]
     for k, width in enumerate(WIDTHS):
-        ring, total = take(2)
-        own = take(1)[0]
-        sums.append(LineScatter(wire, place, parts[k], ring, total, own, block, local(2 + k)))
-        homes.append(Home(wire, place, total, results[k], rows))
-    dn_sum, qk_sum, up_sum, wt_sum = sums
+        ring, total, own = take(3)
+        sums.append(LineScatter(wire, place, parts[k], ring, total, own, block, local(20 + k)))
+        homes.append(Home(wire, place, total, *results[k], width, rows))
 
     def finish(k):
         sums[k].last()
-        homes[k].start(local(6 + k))
+        homes[k].start(local(26 + k))
 
     def store(scatter, result):
         scatter.last()
@@ -900,105 +902,119 @@
     exchanges[0].start(local(12))
     vector_in_start()
     exchanges[2].start(local(14))
-    x.start(local(10))
     exchanges[0].wait()
     dn.own_from_ends()
     dn.own_from_middle()
+    exchanges[1].start(local(13))
     vector_in_pass()
     dn.ahead(1)
     exchanges[2].wait()
     up.own_from_ends()
-    exchanges[1].start(local(13))
+    x.start(local(10))
+    g.start(local(11))
     up.own_from_middle()
     dn.ahead(2)
-    x.turn()
-    g.start(local(11))
-    up.ahead(1)
-    exchanges[3].start(local(15))
     vector_in_rest()
-    x.turn_again()
-    up.ahead(2)
-    x.wait()
-    layer.normalise(0, 2)
     exchanges[1].wait()
     qk.own_from_ends()
+    up.ahead(1)
+    x.turn()
     qk.own_from_middle()
     for step in range(3, n_zero):
         dn.ahead(step)
+    g.turn()
+    x.turn_again()
+    x.wait()
+    exchanges[3].start(local(15))
+    up.ahead(2)
+    layer.normalise(0, 2)
+    g.turn_again()
     layer.normalise(1, 2)
-    g.turn()
+    qk.ahead(1)
     for step in range(3, n_zero):
         up.ahead(step)
-    layer.expand()
+    dense_in.start(local(16))
     exchanges[3].wait()
     wt.own_from_ends()
-    qk.ahead(1)
-    g.turn_again()
+    layer.expand()
+    qk.ahead(2)
+    wt.own_from_middle()
     g.wait()
     layer.down_gradient()
-    dense_in.start(local(16))
-    qk.ahead(2)
-    wt_sum.launch(0)
+    sums[4].launch(0)
+    sums[5].launch(0)
     for step in range(3, n_zero):
         qk.ahead(step)
-    wt.own_from_middle()
     dense_in.wait()
     layer.attend(0)
-    wt_sum.launch(1)
+    sums[4].launch(1)
+    sums[5].launch(1)
     wt.ahead(1)
-    wt_sum.launch(2)
     layer.attend(1)
-    wt_sum.advance(1)
+    sums[4].launch(2)
     layer.qkv_gradient()
+    sums[5].launch(2)
+    sums[5].advance(1)
+    sums[1].launch(0)
+    sums[4].advance(1)
+    wt.ahead(2)
     layer.dense_gradient()
-    qk_sum.launch(0)
-    qk_sum.launch(1)
-    wt.ahead(2)
-    qk_sum.launch(2)
     dense_out.start(local(17))
     layer.back_one()
     for step in range(3, n_zero):
         wt.ahead(step)
+    sums[5].advance(2)
+    sums[1].launch(1)
+    layer.contract_back()
+    sums[4].advance(2)
+    finish(5)
+    layer.output()
+    sums[1].launch(2)
+    out.start()
+    finish(4)
+    layer.up_gradient()
     dense_out.wait()
-    wt_sum.advance(2)
-    layer.contract_back()
-    layer.output()
-    dn_sum.launch(0)
-    out.start()
+    sums[2].launch(0)
+    out.turn()
+    sums[0].launch(0)
+    sums[2].launch(1)
+    homes[5].wait()
+    sums[0].launch(1)
+    sums[1].advance(1)
+    layer.back_two()
+    tok.start()
+    out.turn_again()
+    sums[1].advance(2)
+    sums[3].launch(0)
+    vector_out_start()
+    sums[2].launch(2)
+    sums[2].advance(1)
+    tok.turn()
+    sums[0].advance(1)
+    tok.turn_again()
+    sums[3].launch(1)
+    sums[0].launch(2)
+    finish(1)
+    sums[2].advance(2)
+    sums[3].advance(1)
+    sums[0].advance(2)
+    sums[3].launch(2)
+    finish(2)
+    store(out, layer.out_sum)
+    homes[4].wait()
+    sums[3].advance(2)
+    vector_out_pass()
+    finish(0)
+    homes[1].wait()
     finish(3)
-    layer.up_gradient()
-    up_sum.launch(0)
-    out.turn()
-    qk_sum.advance(1)
-    dn_sum.launch(1)
-    layer.back_two()
-    up_sum.launch(1)
-    out.turn_again()
-    homes[3].wait()
-    dn_sum.advance(1)
-    tok.start()
-    qk_sum.advance(2)
-    tok.turn()
-    vector_out_start()
-    dn_sum.launch(2)
-    up_sum.advance(1)
-    dn_sum.advance(2)
-    tok.turn_again()
-    up_sum.launch(2)
-    up_sum.advance(2)
-    store(out, layer.out_sum)
-    vector_out_pass()
-    finish(1)
-    finish(0)
+    homes[2].wait()
+    vector_line.ahead(1)
     store(tok, layer.tok_sum)
-    finish(2)
-    vector_line.ahead(1)
     for step in range(2, n_zero):
         vector_line.ahead(step)
     vector_out_spread()
-    homes[2].wait()
+    homes[3].wait()
     homes[0].wait()
-    homes[1].wait()
     vector_spread.wait()
     wire.finish()
 
@@ -1014,7 +1030,7 @@
         vmem(tokens, 3 * HEAD_W),
         pltpu.SemaphoreType.DMA((slots,)),
         pltpu.SemaphoreType.DMA((slots,)),
-        pltpu.SemaphoreType.DMA((20,)),
+        pltpu.SemaphoreType.DMA((32,)),
         vmem(local, D),
         pltpu.VMEM((local, D), F32),
     ]
@@ -1026,7 +1042,10 @@
         scratch += [vmem(2, 2, local, D), vmem(local, D), vmem(local, D), vmem(local, D)]
     for width in WIDTHS:
         scratch += [vmem(n_zero + 1, block, width), vmem(block, width), vmem(block, width)]
-    homes = [jax.ShapeDtypeStruct((N_DP, N_SEQ, rows, width), BF) for width in WIDTHS]
+    homes = [
+        jax.ShapeDtypeStruct((N_DP, N_SEQ, rows, width), BF)
+        for width in (HEAD_W, 3 * HEAD_W, HID_W, HID_W)
+    ]
     anywhere = pl.BlockSpec(memory_space=pl.ANY)
     vector = pl.BlockSpec(memory_space=pltpu.VMEM)
     held = buffers(tokens)
@@ -1049,69 +1068,102 @@
     )(*operands)
 
 
-def adam_body(decay, flipped, home, param, first, second, new, first_new, second_new, grad_out):
-    if flipped:
-        gradient = home[0, 0].astype(F32).T
-    else:
-        gradient = jnp.concatenate([home[0, k] for k in range(home.shape[1])], axis=1).astype(F32)
-    updated = adam_step(param[...], gradient, first[...], second[...], decay)
-    new[...], first_new[...], second_new[...] = updated
-    grad_out[...] = gradient
-
-
-def adam(home, pieces, param, first, second):
-    rows, width = home.shape[2], home.shape[3] // pieces
-    together = max(1, min(N_SEQ, HID_W // width))
-    groups = PARTS // together
-    block = pl.BlockSpec((rows, width * together), lambda c, t: (0, t * groups + c))
-    each = N_SEQ // together
+def update(gradient, held, results):
+    param, first, second = (ref[...] for ref in held)
+    for ref, value in zip(results, adam_step(param, gradient, first, second, WEIGHT_DECAY)):
+        ref[...] = value
+    results[3][...] = gradient
+
+
+def finish_body(*refs):
+    refs = list(refs)
+    take = lambda count: [refs.pop(0) for _ in range(count)]
+    up_home, wt_home, dn_home, *qk_homes = take(6)
+    up, down, dense, qkv = (take(3) for _ in range(4))
+    x, g, out_sum, tok_sum, bias = take(5)
+    results = [take(4) for _ in range(4)]
+    outputs, input_grad = take(2)
+    update(up_home[0, 0].astype(F32), up, results[0])
+    update(wt_home[0, 0].astype(F32).T, down, results[1])
+    update(dn_home[0, 0].astype(F32), dense, results[2])
+    columns = jnp.concatenate([home[0, 0] for home in qk_homes], axis=1)
+    update(columns.astype(F32), qkv, results[3])
+    tokens = x[...].astype(F32)
+    outputs[...] = (tokens + out_sum[...] + bias[...]).astype(BF)
+    centred = tokens - jnp.mean(tokens, axis=1, keepdims=True)
+    spread = jnp.mean(centred * centred, axis=1, keepdims=True)
+    rate = lax.rsqrt(spread + NORM_EPSILON)
+    xhat = centred * rate
+    d_xhat = tok_sum[...]
+    d_tokens = rate * (
+        d_xhat
+        - jnp.mean(d_xhat, axis=1, keepdims=True)
+        - xhat * jnp.mean(d_xhat * xhat, axis=1, keepdims=True)
+    )
+    input_grad[...] = (g[...].astype(F32) + d_tokens).astype(BF)
+
+
+def finish_call(homes, states, x, g, out_sum, tok_sum, bias):
+    up_home, wt_home, dn_home, qk_home = homes
+    rows = up_home.shape[2]
+    home = lambda width: pl.BlockSpec((1, 1, rows, width), lambda c: (c // N_SEQ, c % N_SEQ, 0, 0))
+
+    def third(k):
+        def at(c):
+            unit = 3 * c + k
+            part = unit % PARTS
+            return (part // N_SEQ, part % N_SEQ, 0, unit // PARTS)
+
+        return pl.BlockSpec((1, 1, rows, HEAD_W), at)
+
+    columns = lambda width: pl.BlockSpec((rows, width), lambda c: (0, c))
+    blocks = (columns(HID_W), pl.BlockSpec((HID_W, rows), lambda c: (c, 0)), columns(HEAD_W), columns(3 * HEAD_W))
+    some = pl.BlockSpec((x.shape[0] // PARTS, D), lambda c: (c, 0))
+    whole = pl.BlockSpec((1, D), lambda c: (0, 0))
     return pl.pallas_call(
-        functools.partial(adam_body, WEIGHT_DECAY, False),
-        grid=(groups, pieces),
-        in_specs=[
-            pl.BlockSpec((1, together, rows, width), lambda c, t: (c // each, c % each, 0, t)),
-            block,
-            block,
-            block,
-        ],
-        out_specs=[block] * 4,
-        out_shape=[jax.ShapeDtypeStruct(param.shape, F32)] * 4,
-        compiler_params=pltpu.CompilerParams(vmem_limit_bytes=48 * 1024 * 1024),
-        name="adam",
-    )(home, param, first, second)
-
-
-def adam_pair_body(decay, *refs):
-    adam_body(decay, False, *refs[0:4], *refs[8:12])
-    adam_body(decay, True, *refs[4:8], *refs[12:16])
-
-
-def adam_pair(up_home, up, wt_home, down):
-    rows, width = up_home.shape[2:]
-    home = pl.BlockSpec((1, 1, rows, width), lambda c: (c // N_SEQ, c % N_SEQ, 0, 0))
-    columns = pl.BlockSpec((rows, width), lambda c: (0, c))
-    tall_rows = pl.BlockSpec((width, rows), lambda c: (c, 0))
-    results = pl.pallas_call(
-        functools.partial(adam_pair_body, WEIGHT_DECAY),
+        finish_body,
         grid=(PARTS,),
-        in_specs=[home] + [columns] * 3 + [home] + [tall_rows] * 3,
-        out_specs=[columns] * 4 + [tall_rows] * 4,
-        out_shape=[jax.ShapeDtypeStruct(up[0].shape, F32)] * 4 + [jax.ShapeDtypeStruct(down[0].shape, F32)] * 4,
-        compiler_params=pltpu.CompilerParams(vmem_limit_bytes=56 * 1024 * 1024),
-        name="adam_pair",
-    )(up_home, *up, wt_home, *down)
-    return results[:4], results[4:]
+        in_specs=[home(HID_W), home(HID_W), home(HEAD_W)]
+        + [third(k) for k in range(3)]
+        + [block for block in blocks for _ in range(3)]
+        + [some] * 4
+        + [whole],
+        out_specs=[block for block in blocks for _ in range(4)] + [some] * 2,
+        out_shape=[jax.ShapeDtypeStruct(state[0].shape, F32) for state in states for _ in range(4)]
+        + [jax.ShapeDtypeStruct(x.shape, BF)] * 2,
+        compiler_params=pltpu.CompilerParams(vmem_limit_bytes=60 * 1024 * 1024),
+        name="finish",
+    )(
+        up_home,
+        wt_home,
+        dn_home,
+        qk_home,
+        qk_home,
+        qk_home,
+        *(array for state in states for array in state),
+        x,
+        g,
+        out_sum,
+        tok_sum,
+        bias,
+    )
 
 
 def pack_body(half, *refs):
-    dense, query, key, value, up, down, dn_low, qk_low, up_low, wt_low = refs
+    dense, query, key, value, up, down, g, dn_low, qk_low, up_low, wt_low, g_total = refs
+
+    @pl.when(pl.program_id(0) == 0)
+    def _():
+        g_total[...] = jnp.zeros_like(g_total)
+
+    column_sums(g_total, g[...].astype(F32))
     dn_low[0] = dense[...].astype(BF)
     qk_low[0] = jnp.concatenate([query[...], key[...], value[...]], axis=1).astype(BF)
     up_low[0] = up[...].astype(BF)
     wt_low[0] = down[...].T.astype(BF)
 
 
-def pack(half, qkv_weight, dense_weight, up_weight, down_weight):
+def pack(half, qkv_weight, dense_weight, up_weight, down_weight, g):
     rows = qkv_weight.shape[0]
     columns = lambda width, t: pl.BlockSpec((rows, width), lambda s, h: (0, t * PARTS + h[0] * N_SEQ + s))
     widths = (HEAD_W, 3 * HEAD_W, HID_W, HID_W)
@@ -1122,13 +1174,16 @@
             grid=(N_SEQ,),
             in_specs=[columns(HEAD_W, 0)]
             + [columns(HEAD_W, t) for t in range(3)]
-            + [columns(HID_W, 0), pl.BlockSpec((HID_W, rows), lambda s, h: (h[0] * N_SEQ + s, 0))],
-            out_specs=[pl.BlockSpec((1, rows, width), lambda s, h: (s, 0, 0)) for width in widths],
+            + [columns(HID_W, 0), pl.BlockSpec((HID_W, rows), lambda s, h: (h[0] * N_SEQ + s, 0))]
+            + [pl.BlockSpec((g.shape[0] // N_SEQ, D), lambda s, h: (s, 0))],
+            out_specs=[pl.BlockSpec((1, rows, width), lambda s, h: (s, 0, 0)) for width in widths]
+            + [pl.BlockSpec((8, D), lambda s, h: (0, 0))],
         ),
-        out_shape=[jax.ShapeDtypeStruct((N_SEQ, rows, width), BF) for width in widths],
-        compiler_params=pltpu.CompilerParams(vmem_limit_bytes=48 * 1024 * 1024),
+        out_shape=[jax.ShapeDtypeStruct((N_SEQ, rows, width), BF) for width in widths]
+        + [jax.ShapeDtypeStruct((8, D), F32)],
+        compiler_params=pltpu.CompilerParams(vmem_limit_bytes=62 * 1024 * 1024),
         name="pack",
-    )(half, dense_weight, qkv_weight, qkv_weight, qkv_weight, up_weight, down_weight)
+    )(half, dense_weight, qkv_weight, qkv_weight, qkv_weight, up_weight, down_weight, g)
 
 
 def rotary_rows(length):
@@ -1170,14 +1225,12 @@
         token_rows = seqs_here * local_len
         rows = qkv_weight.shape[0]
 
-        dn_low, qk_low, up_low, wt_low = pack(
-            dp_i.astype(jnp.int32).reshape(1), qkv_weight, dense_weight, up_weight, down_weight
-        )
         tokens_low = inputs.reshape(token_rows, D)
         grad_low = out_grad.reshape(token_rows, D)
+        dn_low, qk_low, up_low, wt_low, d_out_bias = pack(
+            dp_i.astype(jnp.int32).reshape(1), qkv_weight, dense_weight, up_weight, down_weight, grad_low
+        )
         tokens = N_DP * N_SEQ * token_rows
-        grad_wide = grad_low.astype(F32)
-        d_out_bias = jnp.sum(grad_wide, axis=0, keepdims=True)
         vec_low = lax.reduce_precision(vectors, exponent_bits=8, mantissa_bits=7)
         if vectors.shape[0] % CHUNK == 0:
             vec_low = vec_low.reshape(1, -1, CHUNK)
@@ -1201,23 +1254,6 @@
         vec_flat = vec_all.reshape(-1)
         dense_bias, down_bias = vec_flat[5 * D : 6 * D], vec_flat[8 * D + FF : 9 * D + FF]
 
-        def statistics(values):
-            average = jnp.mean(values, axis=-1, keepdims=True)
-            centred = values - average
-            spread = jnp.mean(centred * centred, axis=-1, keepdims=True)
-            return centred, lax.rsqrt(spread + NORM_EPSILON)
-
-        tokens_wide = tokens_low.astype(F32)
-        outputs = (tokens_wide + out_sum + dense_bias + down_bias).astype(BF).reshape(inputs.shape)
-        centred_own, rate_own = statistics(tokens_wide)
-        xhat_own = centred_own * rate_own
-        d_tokens = rate_own * (
-            d_xhat
-            - jnp.mean(d_xhat, axis=-1, keepdims=True)
-            - xhat_own * jnp.mean(d_xhat * xhat_own, axis=-1, keepdims=True)
-        )
-        input_grad = (grad_wide + d_tokens).astype(BF).reshape(inputs.shape)
-
         row = lambda k: vec_sums[:, k].reshape(-1)
         vector_sum = jnp.concatenate(
             [
@@ -1236,14 +1272,22 @@
         )
 
         vec_upd = adam_step(vectors, vectors_grad, vectors_first, vectors_second, 0.0) + (vectors_grad,)
-        qkv_upd = adam(qk_home, 3, qkv_weight, qkv_first, qkv_second)
-        dense_upd = adam(dn_home, 1, dense_weight, dense_first, dense_second)
-        up_upd, down_upd = adam_pair(
-            up_home,
-            (up_weight, up_first, up_second),
-            wt_home,
-            (down_weight, down_first, down_second),
-        )
+        *changed, outputs, input_grad = finish_call(
+            (up_home, wt_home, dn_home, qk_home),
+            (
+                (up_weight, up_first, up_second),
+                (down_weight, down_first, down_second),
+                (dense_weight, dense_first, dense_second),
+                (qkv_weight, qkv_first, qkv_second),
+            ),
+            tokens_low,
+            grad_low,
+            out_sum,
+            d_xhat,
+            (dense_bias + down_bias).reshape(1, D),
+        )
+        outputs, input_grad = outputs.reshape(inputs.shape), input_grad.reshape(inputs.shape)
+        up_upd, down_upd, dense_upd, qkv_upd = (tuple(changed[4 * k : 4 * k + 4]) for k in range(4))
         updates = (vec_upd, qkv_upd, dense_upd, up_upd, down_upd)
         picked = lambda k: tuple(update[k] for update in updates)
         return (outputs, input_grad) + picked(3) + picked(0) + picked(1) + picked(2)

time: 463 us -> 452 us (0.976)
  other arithmetic: 9.59 us -> 2.6 us
    unnamed x46 -> x16, local copies, waits for them, and re-layouts: 5.7 us -> 0.93 us
    reshape x1 -> x0, other arithmetic: 4.74 us -> none  [body(): input_grad = (grad_wide + d_tokens).astype(BF).reshape(inputs.shape)]
    pallas_call x3 -> x1, Pallas kernels: 36.7 us -> 37 us  [finish_call(): pl.pallas_call(finish_body, grid=(PARTS,), in_specs=[home(HID_W), home(HI...]
where the time goes in v6:
time: 452 us; the launch traced here: 448 us
  Pallas kernels  440 us (97%)
    pallas_call x1, Pallas kernels, layer_call(): pl.pallas_call(functools.partial(layer_body, n_zero, rows, tokens), in_sp...  398 us
    pallas_call x1, Pallas kernels, finish_call(): pl.pallas_call(finish_body, grid=(PARTS,), in_specs=[home(HID_W), home(HI...  37 us

profile of v6, /device:TPU:0, one launch (start us, length us, event | category | flops | bytes accessed | tf_op | source)
XLA Modules:
  0.0 447.7 jit_solution(18115432118884679340)
XLA Ops:
  0.7 1.3 reduce-precision_bitcast_fusion.refs_6_
  2.0 5.2 %pack.1 = (bf16[4,128,256]{2,1,0:T(8,128)(2,1)}, bf16[4,128,768]{2,1,0:T(8,128)(2,1)}, bf16[4,128,1024]{2,1,0:T(8,128)(2,1)}, bf16[4,128,1024]{2,1,0:T(8,128)(2,1)}, f32[8,2048]{1,0:T(8,128)}) custom-call(s32[1]{0:T(128)} %bitcast.2.half, f32[128,2048]{1,0:T(8,128)} %refs_12_.1, f32[128,6144]{1,0:T(8,128)} %refs_15_.1, f32[128,6144]{1,0:T(8,128)} %refs_15_.1, ...), custom_call_target="tpu_custom_call" | custom-call | tf_op jit(solution)/shard_map/pack/pallas_call | solution.py:1170
  7.2 0.0 copy-start
  7.2 0.0 copy-start.1
  7.2 0.0 copy-start.2
  7.2 398.2 %layer.1 = (f32[256,2048]{1,0:T(8,128)}, f32[256,2048]{1,0:T(8,128)}, bf16[2,4,128,256]{3,2,1,0:T(8,128)(2,1)}, bf16[2,4,128,768]{3,2,1,0:T(8,128)(2,1)}, bf16[2...) custom-call(bf16[256,2048]{1,0:T(8,128)(2,1)} %bitcast.25, ...), custom_call_target="tpu_custom_call" | custom-call | tf_op jit(solution)/shard_map/layer/pallas_call | solution.py:1052
  405.4 0.8 slice_bitcast_fusion.1
  406.3 0.8 slice_bitcast_fusion
  407.1 1.1 fusion.2
  408.3 0.0 copy-done
  408.3 0.0 copy-done.1
  408.3 0.0 copy-done.2
  408.3 0.7 multiply_subtract_fusion
  409.1 0.9 reshape.78
  410.0 0.6 slice_add_fusion
  410.6 37.0 %finish.1 = (f32[128,8192]{1,0:T(8,128)}, f32[128,8192]{1,0:T(8,128)}, f32[128,8192]{1,0:T(8,128)}, f32[128,8192]{1,0:T(8,128)}, f32[8192,128]{1,0:T(8,128)}, /*...) custom-call(bf16[2,4,128,1024]{3,2,1,0:T(8,128)(2,1)} %get-tuple-ele, ...), custom_call_target="tpu_custom_call" | custom-call | tf_op jit(solution)/shard_map/finish/pallas_call | solution.py:1123
  (11 shorter events, 0.1 us)
Async XLA Ops:
  7.2 401.1 %copy-start = (f32[1664]{0:T(1024)S(1)}, f32[1664]{0:T(1024)}, u32[]{:S(2)}) copy-start(f32[1664]{0:T(1024)} %param.21) | copy-start | bytes 19972
  7.2 401.1 %copy-start.1 = (f32[1664]{0:T(1024)S(1)}, f32[1664]{0:T(1024)}, u32[]{:S(2)}) copy-start(f32[1664]{0:T(1024)} %param.26) | copy-start | bytes 19972
  7.2 401.1 %copy-start.2 = (f32[1664]{0:T(1024)S(1)}, f32[1664]{0:T(1024)}, u32[]{:S(2)}) copy-start(f32[1664]{0:T(1024)} %param.31) | copy-start | bytes 19972

commit v7 on v6

--- a/solution.py
+++ b/solution.py
@@ -456,6 +456,7 @@
 
 
 TILE = 256
+WIDE = 512
 
 
 def pipe(body, grid, ins, outs, refs):
@@ -601,7 +602,7 @@
         def body(n1, part):
             part[...] = lax.dot_general(n1[...], self.d_proj[...], TN, preferred_element_type=F32).astype(BF)
 
-        pipe(body, D // TILE, [slim(self.tokens)], [tall(3 * HEAD_W)], (self.n1, self.qk_part))
+        pipe(body, D // WIDE, [slim(self.tokens, WIDE)], [tall(3 * HEAD_W, WIDE)], (self.n1, self.qk_part))
 
     def back_one(self):
         def body(qkv, xh, part):
@@ -634,9 +635,9 @@
 
         pipe(
             body,
-            D // TILE,
-            [slim(self.tokens), fixed(self.tokens, HID_W)],
-            [tall(HID_W)],
+            D // WIDE,
+            [slim(self.tokens, WIDE), fixed(self.tokens, HID_W)],
+            [tall(HID_W, WIDE)],
             (self.g, self.hidden, self.wt_part),
         )
 
@@ -649,9 +650,9 @@
 
         pipe(
             body,
-            self.tiles,
-            [tall(D), fixed(D, HID_W), tall(HID_W)],
-            [tall(HID_W)],
+            self.tokens // WIDE,
+            [tall(D, WIDE), fixed(D, HID_W), tall(HID_W, WIDE)],
+            [tall(HID_W, WIDE)],
             (self.g, self.wt, self.slope, self.d_pre),
         )
 
@@ -661,9 +662,9 @@
 
         pipe(
             body,
-            D // TILE,
-            [slim(self.tokens), fixed(self.tokens, HID_W)],
-            [tall(HID_W)],
+            D // WIDE,
+            [slim(self.tokens, WIDE), fixed(self.tokens, HID_W)],
+            [tall(HID_W, WIDE)],
             (self.n2, self.d_pre, self.up_part),
         )
 

time: 452 us -> 448 us (level)
  no operation moved by 1% of the time
where the time goes in v7:
time: 448 us; the launch traced here: 445 us
  Pallas kernels  437 us (98%)
    pallas_call x1, Pallas kernels, layer_call(): pl.pallas_call(functools.partial(layer_body, n_zero, rows, tokens), in_sp...  395 us
    pallas_call x1, Pallas kernels, finish_call(): pl.pallas_call(finish_body, grid=(PARTS,), in_specs=[home(HID_W), home(HI...  37 us

profile of v7, /device:TPU:0, one launch (start us, length us, event | category | flops | bytes accessed | tf_op | source)
XLA Modules:
  0.0 444.6 jit_solution(17679708355544727343)
XLA Ops:
  0.7 1.3 reduce-precision_bitcast_fusion.refs_6_
  2.0 5.2 %pack.1 = (bf16[4,128,256]{2,1,0:T(8,128)(2,1)}, bf16[4,128,768]{2,1,0:T(8,128)(2,1)}, bf16[4,128,1024]{2,1,0:T(8,128)(2,1)}, bf16[4,128,1024]{2,1,0:T(8,128)(2,1)}, f32[8,2048]{1,0:T(8,128)}) custom-call(s32[1]{0:T(128)} %bitcast.2.half, f32[128,2048]{1,0:T(8,128)} %refs_12_.1, f32[128,6144]{1,0:T(8,128)} %refs_15_.1, f32[128,6144]{1,0:T(8,128)} %refs_15_.1, ...), custom_call_target="tpu_custom_call" | custom-call | tf_op jit(solution)/shard_map/pack/pallas_call | solution.py:1171
  7.2 0.0 copy-start
  7.2 0.0 copy-start.1
  7.2 0.0 copy-start.2
  7.2 395.0 %layer.1 = (f32[256,2048]{1,0:T(8,128)}, f32[256,2048]{1,0:T(8,128)}, bf16[2,4,128,256]{3,2,1,0:T(8,128)(2,1)}, bf16[2,4,128,768]{3,2,1,0:T(8,128)(2,1)}, bf16[2...) custom-call(bf16[256,2048]{1,0:T(8,128)(2,1)} %bitcast.25, ...), custom_call_target="tpu_custom_call" | custom-call | tf_op jit(solution)/shard_map/layer/pallas_call | solution.py:1053
  402.3 0.8 slice_bitcast_fusion.1
  403.1 0.8 slice_bitcast_fusion
  404.0 1.1 fusion.2
  405.2 0.0 copy-done
  405.2 0.0 copy-done.1
  405.2 0.0 copy-done.2
  405.2 0.7 multiply_subtract_fusion
  405.9 0.9 reshape.78
  406.8 0.6 slice_add_fusion
  407.4 37.0 %finish.1 = (f32[128,8192]{1,0:T(8,128)}, f32[128,8192]{1,0:T(8,128)}, f32[128,8192]{1,0:T(8,128)}, f32[128,8192]{1,0:T(8,128)}, f32[8192,128]{1,0:T(8,128)}, /*...) custom-call(bf16[2,4,128,1024]{3,2,1,0:T(8,128)(2,1)} %get-tuple-ele, ...), custom_call_target="tpu_custom_call" | custom-call | tf_op jit(solution)/shard_map/finish/pallas_call | solution.py:1124
  (11 shorter events, 0.1 us)
Async XLA Ops:
  7.2 398.0 %copy-start = (f32[1664]{0:T(1024)S(1)}, f32[1664]{0:T(1024)}, u32[]{:S(2)}) copy-start(f32[1664]{0:T(1024)} %param.21) | copy-start | bytes 19972
  7.2 398.0 %copy-start.1 = (f32[1664]{0:T(1024)S(1)}, f32[1664]{0:T(1024)}, u32[]{:S(2)}) copy-start(f32[1664]{0:T(1024)} %param.26) | copy-start | bytes 19972
  7.2 398.0 %copy-start.2 = (f32[1664]{0:T(1024)S(1)}, f32[1664]{0:T(1024)}, u32[]{:S(2)}) copy-start(f32[1664]{0:T(1024)} %param.31) | copy-start | bytes 19972

commit v8 on v7

--- a/solution.py
+++ b/solution.py
@@ -616,16 +616,18 @@
 
     def expand(self):
         def body(n2, up, hidden, slope):
-            pre = jnp.dot(n2[...], up[...], preferred_element_type=F32) + self.up_bias[...]
-            value, rise = gelu_parts(pre)
-            hidden[...] = value.astype(BF)
-            slope[...] = rise.astype(BF)
+            for k in range(WIDE // TILE):
+                at = slice(k * TILE, (k + 1) * TILE)
+                pre = jnp.dot(n2[at, :], up[...], preferred_element_type=F32) + self.up_bias[...]
+                value, rise = gelu_parts(pre)
+                hidden[at, :] = value.astype(BF)
+                slope[at, :] = rise.astype(BF)
 
         pipe(
             body,
-            self.tiles,
-            [tall(D), fixed(D, HID_W)],
-            [tall(HID_W)] * 2,
+            self.tokens // WIDE,
+            [tall(D, WIDE), fixed(D, HID_W)],
+            [tall(HID_W, WIDE)] * 2,
             (self.n2, self.up, self.hidden, self.slope),
         )
 

time: 448 us -> 448 us (level)
  no operation moved by 1% of the time
where the time goes in v8:
time: 448 us; the launch traced here: 445 us
  Pallas kernels  437 us (98%)
    pallas_call x1, Pallas kernels, layer_call(): pl.pallas_call(functools.partial(layer_body, n_zero, rows, tokens), in_sp...  395 us
    pallas_call x1, Pallas kernels, finish_call(): pl.pallas_call(finish_body, grid=(PARTS,), in_specs=[home(HID_W), home(HI...  37 us

profile of v8, /device:TPU:0, one launch (start us, length us, event | category | flops | bytes accessed | tf_op | source)
XLA Modules:
  0.0 444.6 jit_solution(9160895041506825204)
XLA Ops:
  0.7 1.3 reduce-precision_bitcast_fusion.refs_6_
  2.0 5.2 %pack.1 = (bf16[4,128,256]{2,1,0:T(8,128)(2,1)}, bf16[4,128,768]{2,1,0:T(8,128)(2,1)}, bf16[4,128,1024]{2,1,0:T(8,128)(2,1)}, bf16[4,128,1024]{2,1,0:T(8,128)(2,1)}, f32[8,2048]{1,0:T(8,128)}) custom-call(s32[1]{0:T(128)} %bitcast.2.half, f32[128,2048]{1,0:T(8,128)} %refs_12_.1, f32[128,6144]{1,0:T(8,128)} %refs_15_.1, f32[128,6144]{1,0:T(8,128)} %refs_15_.1, ...), custom_call_target="tpu_custom_call" | custom-call | tf_op jit(solution)/shard_map/pack/pallas_call | solution.py:1173
  7.2 0.0 copy-start
  7.2 0.0 copy-start.1
  7.2 0.0 copy-start.2
  7.2 395.1 %layer.1 = (f32[256,2048]{1,0:T(8,128)}, f32[256,2048]{1,0:T(8,128)}, bf16[2,4,128,256]{3,2,1,0:T(8,128)(2,1)}, bf16[2,4,128,768]{3,2,1,0:T(8,128)(2,1)}, bf16[2...) custom-call(bf16[256,2048]{1,0:T(8,128)(2,1)} %bitcast.25, ...), custom_call_target="tpu_custom_call" | custom-call | tf_op jit(solution)/shard_map/layer/pallas_call | solution.py:1055
  402.3 0.8 slice_bitcast_fusion.1
  403.2 0.8 slice_bitcast_fusion
  404.0 1.1 fusion.2
  405.2 0.0 copy-done
  405.2 0.0 copy-done.1
  405.2 0.0 copy-done.2
  405.2 0.7 multiply_subtract_fusion
  405.9 0.9 reshape.78
  406.9 0.6 slice_add_fusion
  407.5 37.0 %finish.1 = (f32[128,8192]{1,0:T(8,128)}, f32[128,8192]{1,0:T(8,128)}, f32[128,8192]{1,0:T(8,128)}, f32[128,8192]{1,0:T(8,128)}, f32[8192,128]{1,0:T(8,128)}, /*...) custom-call(bf16[2,4,128,1024]{3,2,1,0:T(8,128)(2,1)} %get-tuple-ele, ...), custom_call_target="tpu_custom_call" | custom-call | tf_op jit(solution)/shard_map/finish/pallas_call | solution.py:1126
  (11 shorter events, 0.1 us)
Async XLA Ops:
  7.2 398.0 %copy-start = (f32[1664]{0:T(1024)S(1)}, f32[1664]{0:T(1024)}, u32[]{:S(2)}) copy-start(f32[1664]{0:T(1024)} %param.21) | copy-start | bytes 19972
  7.2 398.0 %copy-start.1 = (f32[1664]{0:T(1024)S(1)}, f32[1664]{0:T(1024)}, u32[]{:S(2)}) copy-start(f32[1664]{0:T(1024)} %param.26) | copy-start | bytes 19972
  7.2 398.0 %copy-start.2 = (f32[1664]{0:T(1024)S(1)}, f32[1664]{0:T(1024)}, u32[]{:S(2)}) copy-start(f32[1664]{0:T(1024)} %param.31) | copy-start | bytes 19972
